TPU v7x, 32 devices: a whole 2x2x4 slice. The times are simulated.
32 devices in a mesh: dp: 4 (over y, x), mp: 8 (over z, core).
Axes of the slice: x: 2, y: 2, z: 4, core: 2. Of those that a mesh axis runs over, the one named last changes fastest.
Arguments:
- incoming_signal: bfloat16 [4, 4, 1024, 1024], P(None, 'dp', 'mp'), may hold values from -6 to 6
- series_number_table: int32 [4, 4, 1024], P(None, 'dp', 'mp'), may hold values from 0 to 2, as said below
- upstream_adjoint: bfloat16 [4, 4, 1024, 1024], P(None, 'dp', 'mp'), may hold values from -6 to 6
- first_scaling_factor: bfloat16 [1024], replicated, may hold values from 0.5 to 1.5
- first_scaling_offset: bfloat16 [1024], replicated, may hold values from -3 to 3
- logarithmic_fading_speeds: bfloat16 [1024], replicated, as said below
- present_step_extra: bfloat16 [1024], replicated, may hold values from -1 to 1
- lookup_shift_mixture: bfloat16 [1024], replicated, may hold values from 0.049804688 to 0.94921875
- content_shift_mixture: bfloat16 [1024], replicated, may hold values from 0.049804688 to 0.94921875
- admit_lookup_shift_mixture: bfloat16 [1024], replicated, may hold values from 0.049804688 to 0.94921875
- attention_lookup_matrix: bfloat16 [1024, 1024], replicated, may hold values from -0.1875 to 0.1875
- attention_content_matrix: bfloat16 [1024, 1024], replicated, may hold values from -0.1875 to 0.1875
- attention_admit_matrix: bfloat16 [1024, 1024], replicated, may hold values from -0.1875 to 0.1875
- attention_result_matrix: bfloat16 [1024, 1024], replicated, may hold values from -0.5 to 0.5
- second_scaling_factor: bfloat16 [1024], replicated, may hold values from 0.5 to 1.5
- second_scaling_offset: bfloat16 [1024], replicated, may hold values from -3 to 3
- inner_shift_mixture: bfloat16 [1024], replicated, may hold values from 0.049804688 to 0.94921875
- admit_shift_mixture: bfloat16 [1024], replicated, may hold values from 0.049804688 to 0.94921875
- feedforward_lookup_matrix: bfloat16 [1024, 4096], P(None, 'mp'), may hold values from -0.1875 to 0.1875
- feedforward_content_matrix: bfloat16 [4096, 1024], P('mp'), may hold values from -0.09375 to 0.09375
- feedforward_admit_matrix: bfloat16 [1024, 1024], replicated, may hold values from -0.1875 to 0.1875
Outputs:
- output: float32 [4, 4, 1024, 1024], P(None, 'dp', 'mp')
- input_grad: float32 [4, 4, 1024, 1024], P(None, 'dp', 'mp')
- grad_first_gain: float32 [1024], P(('dp', 'mp'))
- grad_first_bias: float32 [1024], P(('dp', 'mp'))
- grad_decay_log: float32 [1024], P(('dp', 'mp'))
- grad_first_bonus: float32 [1024], P(('dp', 'mp'))
- grad_key_shift: float32 [1024], P(('dp', 'mp'))
- grad_value_shift: float32 [1024], P(('dp', 'mp'))
- grad_recept_shift: float32 [1024], P(('dp', 'mp'))
- grad_key_weight: float32 [1024, 1024], P(('dp', 'mp'))
- grad_value_weight: float32 [1024, 1024], P(('dp', 'mp'))
- grad_recept_weight: float32 [1024, 1024], P(('dp', 'mp'))
- grad_output_weight: float32 [1024, 1024], P(('dp', 'mp'))
- grad_second_gain: float32 [1024], P(('dp', 'mp'))
- grad_second_bias: float32 [1024], P(('dp', 'mp'))
- grad_hidden_shift: float32 [1024], P(('dp', 'mp'))
- grad_gate_shift: float32 [1024], P(('dp', 'mp'))
- grad_hidden_weight: float32 [1024, 4096], P('dp', 'mp')
- grad_return_weight: float32 [4096, 1024], P('mp', 'dp')
- grad_gate_weight: float32 [1024, 1024], P(('dp', 'mp'))
Inputs may be any that keep to these rules, and one draw needn't show every extreme that they name: `series_number_table`: within a row the numbers never fall; each row is cut at two positions into at most three sequences numbered 0, 1, 2. For every index of the second dimension, one row chosen by the seed holds a sequence that starts within positions 1 to 64 and ends within the 64 positions that come just before the row's last position. Every rate exp(logarithmic_fading_speeds) lies below 0.101.
All inputs are finite; a program needn't handle non-finite values.
Results may differ from a plain program's by a relative error of at most 0.018.
Values may be sent and summed in bfloat16 or wider, within the bound.
A program may use at most 320 MiB of HBM per device.

v0:
```python
import jax
import jax.numpy as jnp
from jax import lax
from jax.sharding import PartitionSpec as P

EPS = 1e-05
HIGH = lax.Precision.HIGHEST


def from_behind(block, axis, distance):
    devices = range(lax.axis_size(axis))
    route = [(i - distance, i) for i in devices if i - distance in devices]
    return lax.ppermute(block, axis, route)


def carried_in(shard, axis, combine, identity, reverse):
    length, mine = (lax.axis_size(axis), lax.axis_index(axis))
    everything = jax.tree.map(lambda part: lax.all_gather(part, axis), shard)
    start = jax.tree.map(
        lambda part, zero: jnp.broadcast_to(jnp.asarray(zero, part.dtype), part.shape),
        shard,
        identity,
    )

    def step(k, before):
        at = length - 1 - k if reverse else k
        reached = at > mine if reverse else at < mine
        new = combine(before, jax.tree.map(lambda part: part[at], everything))
        return jax.tree.map(lambda a, b: jnp.where(reached, a, b), new, before)

    return lax.fori_loop(0, length, step, start)


def reduced_precision(values):
    return values.astype(jnp.bfloat16)


def product(left, right):
    return jnp.dot(left, right, preferred_element_type=jnp.float32)


def product_tn(left, right):
    return lax.dot_general(
        left, right, (((0,), (0,)), ((), ())), preferred_element_type=jnp.float32
    )


def product_nt(left, right):
    return lax.dot_general(
        left, right, (((1,), (1,)), ((), ())), preferred_element_type=jnp.float32
    )


def layer_norm(values, gain, bias):
    average = jnp.mean(values, axis=-1, keepdims=True)
    centre = values - average
    inverse = lax.rsqrt(jnp.mean(centre * centre, axis=-1, keepdims=True) + EPS)
    unit = centre * inverse
    return (unit * gain + bias, unit, inverse)


def norm_back(grad_in, unit, inverse, gain):
    scaled = grad_in * gain
    grad_values = inverse * (
        scaled
        - jnp.mean(scaled, axis=-1, keepdims=True)
        - unit * jnp.mean(scaled * unit, axis=-1, keepdims=True)
    )
    return (grad_values, jnp.sum(grad_in * unit, axis=0), jnp.sum(grad_in, axis=0))


def state_join(earlier, latter):
    return (
        latter[4] * earlier[0] + latter[0],
        latter[4] * earlier[1] + latter[1],
        latter[4] * earlier[2] + latter[5] * earlier[0] + latter[2],
        latter[4] * earlier[3] + latter[5] * earlier[1] + latter[3],
        earlier[4] * latter[4],
        earlier[5] * latter[4] + earlier[4] * latter[5],
    )


def suffix_join(earlier, latter):
    return (
        latter[0] + latter[2] * earlier[0],
        latter[1] + latter[2] * earlier[1],
        latter[2] * earlier[2],
    )


def one_micro(block_in, seg_ids, grad_out, vectors, matrices, hidden_w, return_w):
    (
        gain_one,
        bias_one,
        decay_vec,
        extra_array,
        mix_key,
        mix_value,
        mix_recept,
        gain_two,
        bias_two,
        mix_hidden,
        mix_gate,
    ) = vectors
    key_w, value_w, recept_w, output_w, gate_w = matrices
    row_count = block_in.shape[0]
    model_width = block_in.shape[1]
    seg_float = seg_ids.astype(jnp.float32)
    normed_a, unit_a, inv_a = layer_norm(block_in, gain_one, bias_one)
    prev_row, prev_seg = from_behind((normed_a[-1:], seg_float[-1:]), "mp", 1)
    same_row = jnp.concatenate(
        [
            (seg_float[:1] == prev_seg).astype(jnp.float32),
            (seg_ids[1:] == seg_ids[:-1]).astype(jnp.float32),
        ]
    )
    same_col = same_row[:, None]
    shifted_a = jnp.concatenate([prev_row, normed_a[:-1]], axis=0) * same_col
    delta_a = normed_a - shifted_a
    low_key = reduced_precision(shifted_a + delta_a * mix_key)
    low_value = reduced_precision(shifted_a + delta_a * mix_value)
    low_recept = reduced_precision(shifted_a + delta_a * mix_recept)
    lookup_start = product(low_key, key_w)
    content_start = product(low_value, value_w)
    recept = jax.nn.sigmoid(product(low_recept, recept_w))
    feature_fading = jnp.exp(decay_vec)
    positions = jnp.arange(row_count, dtype=jnp.float32)[:, None]
    rising = jnp.exp(positions * feature_fading)
    falling = jnp.exp(-(positions - 1.0) * feature_fading)
    falling_zero = jnp.exp(-positions * feature_fading)
    raised_lookup = jnp.exp(lookup_start)
    weighted_average = raised_lookup * content_start
    order_rows = jnp.arange(row_count)
    lower_tri = jnp.logical_and(
        seg_ids[:, None] == seg_ids[None, :], order_rows[None, :] < order_rows[:, None]
    ).astype(jnp.float32)
    last_mask = (seg_ids == seg_ids[-1]).astype(jnp.float32)
    first_mask = (seg_ids == seg_ids[0]).astype(jnp.float32) * same_row[0]
    forward_mat = jnp.concatenate([lower_tri, last_mask[None]], axis=0)
    stacked = jnp.concatenate(
        [
            rising * weighted_average,
            rising * raised_lookup,
            positions * rising * weighted_average,
            positions * rising * raised_lookup,
        ],
        axis=1,
    )
    summed = jnp.dot(forward_mat, stacked, precision=HIGH)
    inner_sums = summed[:row_count]
    closing = summed[row_count]
    num_loc = falling * inner_sums[:, :model_width]
    den_loc = falling * inner_sums[:, model_width : 2 * model_width]
    num_der = (
        -(positions - 1.0) * num_loc + falling * inner_sums[:, 2 * model_width : 3 * model_width]
    )
    den_der = -(positions - 1.0) * den_loc + falling * inner_sums[:, 3 * model_width :]
    end_fall = jnp.exp(-(row_count - 1.0) * feature_fading)
    state_num = end_fall * closing[:model_width]
    state_den = end_fall * closing[model_width : 2 * model_width]
    state_num_der = (
        -(row_count - 1.0) * state_num + end_fall * closing[2 * model_width : 3 * model_width]
    )
    state_den_der = -(row_count - 1.0) * state_den + end_fall * closing[3 * model_width :]
    uniform_flag = (seg_ids[-1] == seg_ids[0]).astype(jnp.float32) * same_row[0]
    carry_pass = uniform_flag * jnp.exp(-row_count * feature_fading)
    carry_der = -row_count * carry_pass
    zero_vec = jnp.zeros_like(feature_fading)
    one_vec = jnp.ones_like(feature_fading)
    in_num, in_den, in_num_der, in_den_der, pass_total, pass_der = carried_in(
        (state_num, state_den, state_num_der, state_den_der, carry_pass, carry_der),
        "mp",
        state_join,
        (zero_vec, zero_vec, zero_vec, zero_vec, one_vec, zero_vec),
        False,
    )
    carried = first_mask[:, None] * falling_zero
    dividend = num_loc + carried * in_num
    divisor_portion = den_loc + carried * in_den
    numer_der = num_der + carried * (in_num_der - positions * in_num)
    denom_der = den_der + carried * (in_den_der - positions * in_den)
    extra_summand = jnp.exp(extra_array + lookup_start)
    divisor_complete = divisor_portion + extra_summand
    mixture_result = (dividend + extra_summand * content_start) / divisor_complete
    gated = reduced_precision(recept * mixture_result)
    block_mid = block_in + product(gated, output_w)
    normed_b, unit_b, inv_b = layer_norm(block_mid, gain_two, bias_two)
    prev_mid = from_behind(normed_b[-1:], "mp", 1)
    shifted_b = jnp.concatenate([prev_mid, normed_b[:-1]], axis=0) * same_col
    delta_b = normed_b - shifted_b
    low_hidden = reduced_precision(shifted_b + delta_b * mix_hidden)
    low_gate = reduced_precision(shifted_b + delta_b * mix_gate)
    gate_two = jax.nn.sigmoid(product(low_gate, gate_w))
    hidden_rows = lax.all_gather(low_hidden, "mp", axis=0, tiled=True)
    pre_act = product(hidden_rows, hidden_w)
    rectified = jnp.maximum(pre_act, 0.0)
    squared = reduced_precision(rectified * rectified)
    returned = lax.psum_scatter(
        product(squared, return_w).astype(jnp.bfloat16), "mp", scatter_dimension=0, tiled=True
    ).astype(jnp.float32)
    output = block_mid + gate_two * returned
    grad_ret = reduced_precision(grad_out * gate_two)
    grad_gate_pre = reduced_precision(grad_out * returned * gate_two * (1.0 - gate_two))
    d_gate_w = product_tn(low_gate, grad_gate_pre)
    grad_low_gate = product_nt(grad_gate_pre, gate_w)
    grad_rows = lax.all_gather(grad_ret, "mp", axis=0, tiled=True)
    grad_squared = product_nt(grad_rows, return_w)
    d_return = product_tn(squared, grad_rows)
    grad_pre = reduced_precision(grad_squared * 2.0 * rectified)
    d_hidden = product_tn(hidden_rows, grad_pre)
    grad_low_hidden = lax.psum_scatter(
        product_nt(grad_pre, hidden_w).astype(jnp.bfloat16), "mp", scatter_dimension=0, tiled=True
    ).astype(jnp.float32)
    d_mix_hidden = jnp.sum(grad_low_hidden * delta_b, axis=0)
    d_mix_gate = jnp.sum(grad_low_gate * delta_b, axis=0)
    grad_shift_b = (
        grad_low_hidden * (1.0 - mix_hidden) + grad_low_gate * (1.0 - mix_gate)
    ) * same_col
    from_next_b = from_behind(grad_shift_b[:1], "mp", -1)
    grad_norm_b = (
        grad_low_hidden * mix_hidden
        + grad_low_gate * mix_gate
        + jnp.concatenate([grad_shift_b[1:], from_next_b], axis=0)
    )
    grad_mid_norm, d_gain_two, d_bias_two = norm_back(grad_norm_b, unit_b, inv_b, gain_two)
    grad_mid = grad_out + grad_mid_norm
    grad_att = reduced_precision(grad_mid)
    d_output_w = product_tn(gated, grad_att)
    grad_gated = product_nt(grad_att, output_w)
    grad_recept_pre = reduced_precision(grad_gated * mixture_result * recept * (1.0 - recept))
    grad_mixed = grad_gated * recept
    d_recept_w = product_tn(low_recept, grad_recept_pre)
    grad_low_recept = product_nt(grad_recept_pre, recept_w)
    dividend_adjoint = grad_mixed / divisor_complete
    divisor_adjoint = -dividend_adjoint * mixture_result
    extra_derivative_part = dividend_adjoint * content_start + divisor_adjoint
    extra_derivative = jnp.sum(extra_derivative_part * extra_summand, axis=0)
    d_rate = jnp.sum(dividend_adjoint * numer_der + divisor_adjoint * denom_der, axis=0)
    backward_mat = jnp.concatenate([lower_tri.T, first_mask[None]], axis=0)
    back_sum = jnp.dot(
        backward_mat,
        jnp.concatenate([falling * dividend_adjoint, falling * divisor_adjoint], axis=1),
        precision=HIGH,
    )
    step_back = jnp.exp(-feature_fading)
    from_num = step_back * back_sum[row_count, :model_width]
    from_den = step_back * back_sum[row_count, model_width:]
    out_num, out_den, out_pass = carried_in(
        (from_num, from_den, carry_pass), "mp", suffix_join, (zero_vec, zero_vec, one_vec), True
    )
    tail_fall = last_mask[:, None] * jnp.exp(-(row_count - 1.0 - positions) * feature_fading)
    cumulative_dividend = rising * back_sum[:row_count, :model_width] + tail_fall * out_num
    running_denominator = rising * back_sum[:row_count, model_width:] + tail_fall * out_den
    value_gradient = reduced_precision(
        dividend_adjoint * extra_summand + cumulative_dividend * raised_lookup
    )
    key_gradient = reduced_precision(
        extra_derivative_part * extra_summand
        + cumulative_dividend * weighted_average
        + running_denominator * raised_lookup
    )
    d_key_w = product_tn(low_key, key_gradient)
    d_value_w = product_tn(low_value, value_gradient)
    grad_low_key = product_nt(key_gradient, key_w)
    grad_low_value = product_nt(value_gradient, value_w)
    d_mix_key = jnp.sum(grad_low_key * delta_a, axis=0)
    d_mix_value = jnp.sum(grad_low_value * delta_a, axis=0)
    d_mix_recept = jnp.sum(grad_low_recept * delta_a, axis=0)
    grad_shift_a = (
        grad_low_key * (1.0 - mix_key)
        + grad_low_value * (1.0 - mix_value)
        + grad_low_recept * (1.0 - mix_recept)
    ) * same_col
    from_next_a = from_behind(grad_shift_a[:1], "mp", -1)
    grad_norm_a = (
        grad_low_key * mix_key
        + grad_low_value * mix_value
        + grad_low_recept * mix_recept
        + jnp.concatenate([grad_shift_a[1:], from_next_a], axis=0)
    )
    grad_in_norm, d_gain_one, d_bias_one = norm_back(grad_norm_a, unit_a, inv_a, gain_one)
    input_grad = grad_mid + grad_in_norm
    grads = (
        d_gain_one,
        d_bias_one,
        d_rate * feature_fading,
        extra_derivative,
        d_mix_key,
        d_mix_value,
        d_mix_recept,
        d_key_w,
        d_value_w,
        d_recept_w,
        d_output_w,
        d_gain_two,
        d_bias_two,
        d_mix_hidden,
        d_mix_gate,
        d_hidden,
        d_return,
        d_gate_w,
    )
    return (output, input_grad, grads)


def body(
    incoming_signal,
    series_number_table,
    upstream_adjoint,
    first_scaling_factor,
    first_scaling_offset,
    logarithmic_fading_speeds,
    present_step_extra,
    lookup_shift_mixture,
    content_shift_mixture,
    admit_lookup_shift_mixture,
    attention_lookup_matrix,
    attention_content_matrix,
    attention_admit_matrix,
    attention_result_matrix,
    second_scaling_factor,
    second_scaling_offset,
    inner_shift_mixture,
    admit_shift_mixture,
    feedforward_lookup_matrix,
    feedforward_content_matrix,
    feedforward_admit_matrix,
):
    micro_count = incoming_signal.shape[0]
    hidden_full, return_full = (feedforward_lookup_matrix, feedforward_content_matrix)
    vectors = tuple(
        (
            start_item.astype(jnp.float32)
            for start_item in (
                first_scaling_factor,
                first_scaling_offset,
                logarithmic_fading_speeds,
                present_step_extra,
                lookup_shift_mixture,
                content_shift_mixture,
                admit_lookup_shift_mixture,
                second_scaling_factor,
                second_scaling_offset,
                inner_shift_mixture,
                admit_shift_mixture,
            )
        )
    )
    matrices = (
        attention_lookup_matrix,
        attention_content_matrix,
        attention_admit_matrix,
        attention_result_matrix,
        feedforward_admit_matrix,
    )
    totals = None
    outputs_list = []
    grads_list = []
    for step_index in range(micro_count):
        ultimate_result = one_micro(
            incoming_signal[step_index, 0].astype(jnp.float32),
            series_number_table[step_index, 0],
            upstream_adjoint[step_index, 0].astype(jnp.float32),
            vectors,
            matrices,
            hidden_full,
            return_full,
        )
        outputs_list.append(ultimate_result[0])
        grads_list.append(ultimate_result[1])
        if totals is None:
            totals = ultimate_result[2]
        else:
            totals = jax.tree.map(jnp.add, totals, ultimate_result[2])
    output = jnp.stack(outputs_list)[:, None]
    input_grad = jnp.stack(grads_list)[:, None]
    owned = (
        lax.psum_scatter(totals[0], ("dp", "mp"), scatter_dimension=0, tiled=True),
        lax.psum_scatter(totals[1], ("dp", "mp"), scatter_dimension=0, tiled=True),
        lax.psum_scatter(totals[2], ("dp", "mp"), scatter_dimension=0, tiled=True),
        lax.psum_scatter(totals[3], ("dp", "mp"), scatter_dimension=0, tiled=True),
        lax.psum_scatter(totals[4], ("dp", "mp"), scatter_dimension=0, tiled=True),
        lax.psum_scatter(totals[5], ("dp", "mp"), scatter_dimension=0, tiled=True),
        lax.psum_scatter(totals[6], ("dp", "mp"), scatter_dimension=0, tiled=True),
        lax.psum_scatter(totals[7], ("dp", "mp"), scatter_dimension=0, tiled=True),
        lax.psum_scatter(totals[8], ("dp", "mp"), scatter_dimension=0, tiled=True),
        lax.psum_scatter(totals[9], ("dp", "mp"), scatter_dimension=0, tiled=True),
        lax.psum_scatter(totals[10], ("dp", "mp"), scatter_dimension=0, tiled=True),
        lax.psum_scatter(totals[11], ("dp", "mp"), scatter_dimension=0, tiled=True),
        lax.psum_scatter(totals[12], ("dp", "mp"), scatter_dimension=0, tiled=True),
        lax.psum_scatter(totals[13], ("dp", "mp"), scatter_dimension=0, tiled=True),
        lax.psum_scatter(totals[14], ("dp", "mp"), scatter_dimension=0, tiled=True),
        lax.psum_scatter(totals[17], ("dp", "mp"), scatter_dimension=0, tiled=True),
    )
    hidden_own, return_own = (
        lax.psum_scatter(
            totals[15].astype(jnp.bfloat16), "dp", scatter_dimension=0, tiled=True
        ).astype(jnp.float32),
        lax.psum_scatter(
            totals[16].astype(jnp.bfloat16), "dp", scatter_dimension=1, tiled=True
        ).astype(jnp.float32),
    )
    return (
        output,
        input_grad,
        owned[0],
        owned[1],
        owned[2],
        owned[3],
        owned[4],
        owned[5],
        owned[6],
        owned[7],
        owned[8],
        owned[9],
        owned[10],
        owned[11],
        owned[12],
        owned[13],
        owned[14],
        hidden_own,
        return_own,
        owned[15],
    )


def solution(mesh):
    placed = (
        P(None, "dp", "mp", None),
        P(None, "dp", "mp"),
        P(None, "dp", "mp", None),
        P(),
        P(),
        P(),
        P(),
        P(),
        P(),
        P(),
        P(),
        P(),
        P(),
        P(),
        P(),
        P(),
        P(),
        P(),
        P(None, "mp"),
        P("mp", None),
        P(),
    )
    return jax.shard_map(
        body,
        mesh=mesh,
        in_specs=placed,
        out_specs=(
            P(None, "dp", "mp", None),
            P(None, "dp", "mp", None),
            P(("dp", "mp")),
            P(("dp", "mp")),
            P(("dp", "mp")),
            P(("dp", "mp")),
            P(("dp", "mp")),
            P(("dp", "mp")),
            P(("dp", "mp")),
            P(("dp", "mp"), None),
            P(("dp", "mp"), None),
            P(("dp", "mp"), None),
            P(("dp", "mp"), None),
            P(("dp", "mp")),
            P(("dp", "mp")),
            P(("dp", "mp")),
            P(("dp", "mp")),
            P("dp", "mp"),
            P("mp", "dp"),
            P(("dp", "mp"), None),
        ),
        check_vma=False,
    )
```

profile of v0, /device:TPU:0, one launch (start us, length us, event | category | flops | bytes accessed | tf_op | source)
XLA Modules:
  0.0 2040.1 jit_solution(10784038127895882358)
XLA Ops:
  53.8 14.0 all-gather.17
  67.8 14.0 all-gather.14
  81.8 14.0 all-gather.15
  95.9 14.0 all-gather.12
  109.9 14.0 all-gather.13
  123.9 14.0 all-gather.16
  155.1 30.3 %all-gather.45.cloned.1.call-done = bf16[1024,1024]{1,0:T(8,128)(2,1)} async-done(((bf16[128,1024]{1,0:T(8,128)(2,1)}), bf16[1024,1024]{1,0:T(8,128)(2,1)}) %all-gather.45.cloned.1.call-update) | async-done | bytes 2097168 | tf_op jit(solution)/shard_map/all_gather | solution.py:194
  193.0 34.9 %reduce-scatter.20.cloned.1.call-done = bf16[128,1024]{1,0:T(8,128)(2,1)} async-done(((bf16[1024,1024]{1,0:T(8,128)(2,1)}), bf16[128,1024]{1,0:T(8,128)(2,1)}) %reduce-scatter.20.cloned.1.call-update) | async-done | bytes 262160 | tf_op jit(solution)/shard_map/reduce_scatter | solution.py:198
  231.4 27.9 %all-gather.53.cloned.1.call-done = bf16[1024,1024]{1,0:T(8,128)(2,1)} async-done(((bf16[128,1024]{1,0:T(8,128)(2,1)}), bf16[1024,1024]{1,0:T(8,128)(2,1)}) %all-gather.53.cloned.1.call-update) | async-done | bytes 2097168 | tf_op jit(solution)/shard_map/all_gather | solution.py:206
  273.1 29.2 %reduce-scatter.28.cloned.1.call-done = bf16[128,1024]{1,0:T(8,128)(2,1)} async-done(((bf16[1024,1024]{1,0:T(8,128)(2,1)}), bf16[128,1024]{1,0:T(8,128)(2,1)}) %reduce-scatter.28.cloned.1.call-update) | async-done | bytes 262160 | tf_op jit(solution)/shard_map/reduce_scatter | solution.py:211
  334.2 14.0 all-gather.28
  369.2 14.1 all-gather.11
  383.3 14.0 all-gather.8
  397.4 14.0 all-gather.9
  411.4 14.0 all-gather.6
  425.4 14.0 all-gather.7
  439.4 14.0 all-gather.10
  470.6 31.4 %all-gather.43.cloned.1.call-done = bf16[1024,1024]{1,0:T(8,128)(2,1)} async-done(((bf16[128,1024]{1,0:T(8,128)(2,1)}), bf16[1024,1024]{1,0:T(8,128)(2,1)}) %all-gather.43.cloned.1.call-update) | async-done | bytes 2097168 | tf_op jit(solution)/shard_map/all_gather | solution.py:194
  509.2 35.4 %reduce-scatter.18.cloned.1.call-done = bf16[128,1024]{1,0:T(8,128)(2,1)} async-done(((bf16[1024,1024]{1,0:T(8,128)(2,1)}), bf16[128,1024]{1,0:T(8,128)(2,1)}) %reduce-scatter.18.cloned.1.call-update) | async-done | bytes 262160 | tf_op jit(solution)/shard_map/reduce_scatter | solution.py:198
  548.3 27.8 %all-gather.51.cloned.1.call-done = bf16[1024,1024]{1,0:T(8,128)(2,1)} async-done(((bf16[128,1024]{1,0:T(8,128)(2,1)}), bf16[1024,1024]{1,0:T(8,128)(2,1)}) %all-gather.51.cloned.1.call-update) | async-done | bytes 2097168 | tf_op jit(solution)/shard_map/all_gather | solution.py:206
  583.7 35.4 %reduce-scatter.26.cloned.1.call-done = bf16[128,1024]{1,0:T(8,128)(2,1)} async-done(((bf16[1024,1024]{1,0:T(8,128)(2,1)}), bf16[128,1024]{1,0:T(8,128)(2,1)}) %reduce-scatter.26.cloned.1.call-update) | async-done | bytes 262160 | tf_op jit(solution)/shard_map/reduce_scatter | solution.py:211
  656.8 14.0 all-gather.26
  693.4 15.5 all-gather.5
  708.9 14.2 all-gather.2
  723.1 14.0 all-gather.3
  737.2 14.0 all-gather.1
  751.2 14.0 all-gather.4
  796.4 32.1 %all-gather.41.cloned.1.call-done = bf16[1024,1024]{1,0:T(8,128)(2,1)} async-done(((bf16[128,1024]{1,0:T(8,128)(2,1)}), bf16[1024,1024]{1,0:T(8,128)(2,1)}) %all-gather.41.cloned.1.call-update) | async-done | bytes 2097168 | tf_op jit(solution)/shard_map/all_gather | solution.py:194
  835.7 35.4 %reduce-scatter.16.cloned.1.call-done = bf16[128,1024]{1,0:T(8,128)(2,1)} async-done(((bf16[1024,1024]{1,0:T(8,128)(2,1)}), bf16[128,1024]{1,0:T(8,128)(2,1)}) %reduce-scatter.16.cloned.1.call-update) | async-done | bytes 262160 | tf_op jit(solution)/shard_map/reduce_scatter | solution.py:198
  874.9 27.8 %all-gather.49.cloned.1.call-done = bf16[1024,1024]{1,0:T(8,128)(2,1)} async-done(((bf16[128,1024]{1,0:T(8,128)(2,1)}), bf16[1024,1024]{1,0:T(8,128)(2,1)}) %all-gather.49.cloned.1.call-update) | async-done | bytes 2097168 | tf_op jit(solution)/shard_map/all_gather | solution.py:206
  910.3 35.3 %reduce-scatter.24.cloned.1.call-done = bf16[128,1024]{1,0:T(8,128)(2,1)} async-done(((bf16[1024,1024]{1,0:T(8,128)(2,1)}), bf16[128,1024]{1,0:T(8,128)(2,1)}) %reduce-scatter.24.cloned.1.call-update) | async-done | bytes 262160 | tf_op jit(solution)/shard_map/reduce_scatter | solution.py:211
  979.6 14.0 all-gather.24
  1014.6 14.1 all-gather.23
  1028.7 14.0 all-gather.20
  1042.7 14.0 all-gather.21
  1056.8 14.0 all-gather.18
  1070.8 14.0 all-gather.19
  1084.8 14.0 all-gather.22
  1109.4 31.4 %all-gather.47.cloned.1.call-done = bf16[1024,1024]{1,0:T(8,128)(2,1)} async-done(((bf16[128,1024]{1,0:T(8,128)(2,1)}), bf16[1024,1024]{1,0:T(8,128)(2,1)}) %all-gather.47.cloned.1.call-update) | async-done | bytes 2097168 | tf_op jit(solution)/shard_map/all_gather | solution.py:194
  1148.1 35.5 %reduce-scatter.22.cloned.1.call-done = bf16[128,1024]{1,0:T(8,128)(2,1)} async-done(((bf16[1024,1024]{1,0:T(8,128)(2,1)}), bf16[128,1024]{1,0:T(8,128)(2,1)}) %reduce-scatter.22.cloned.1.call-update) | async-done | bytes 262160 | tf_op jit(solution)/shard_map/reduce_scatter | solution.py:198
  1187.5 27.4 %all-gather.55.cloned.1.call-done = bf16[1024,1024]{1,0:T(8,128)(2,1)} async-done(((bf16[128,1024]{1,0:T(8,128)(2,1)}), bf16[1024,1024]{1,0:T(8,128)(2,1)}) %all-gather.55.cloned.1.call-update) | async-done | bytes 2097168 | tf_op jit(solution)/shard_map/all_gather | solution.py:206
  1313.3 14.0 all-gather.31
  1376.4 43.6 %all-reduce.11 = (f32[1024]{0:T(1024)S(1)}, f32[1024]{0:T(1024)S(1)}, f32[1024]{0:T(1024)S(1)}, f32[1024]{0:T(1024)S(1)}, f32[1024]{0:T(1024)S(1)}, /*index=5*/f...) all-reduce(f32[1024]{0:T(1024)S(1)} %add_add_fusion.18, ...), channel_id=42, replica_groups=mesh['dp'=4,'mp'=8] {'dp','mp'}, use_global_device_ids=true, to_apply=%region_60.61.clone | all-reduce | flops 11264 | bytes 90112
  1430.4 33.2 %reduce-scatter.44.cloned.1.call-done = f32[32,1024]{1,0:T(8,128)} async-done(((f32[1024,1024]{1,0:T(8,128)}), f32[32,1024]{1,0:T(8,128)}) %reduce-scatter.44.cloned.1.call-update) | async-done | bytes 131088 | tf_op jit(solution)/shard_map/reduce_scatter | solution.py:393
  1463.6 142.4 %reduce-scatter.38.cloned.1.call-done = f32[32,1024]{1,0:T(8,128)} async-done(((f32[1024,1024]{1,0:T(8,128)}), f32[32,1024]{1,0:T(8,128)}) %reduce-scatter.38.cloned.1.call-update) | async-done | bytes 131088 | tf_op jit(solution)/shard_map/reduce_scatter | solution.py:388
  1606.0 142.1 %reduce-scatter.36.cloned.1.call-done = f32[32,1024]{1,0:T(8,128)} async-done(((f32[1024,1024]{1,0:T(8,128)}), f32[32,1024]{1,0:T(8,128)}) %reduce-scatter.36.cloned.1.call-update) | async-done | bytes 131088 | tf_op jit(solution)/shard_map/reduce_scatter | solution.py:387
  1748.1 142.2 %reduce-scatter.34.cloned.1.call-done = f32[32,1024]{1,0:T(8,128)} async-done(((f32[1024,1024]{1,0:T(8,128)}), f32[32,1024]{1,0:T(8,128)}) %reduce-scatter.34.cloned.1.call-update) | async-done | bytes 131088 | tf_op jit(solution)/shard_map/reduce_scatter | solution.py:386
  1890.3 142.8 %reduce-scatter.32.cloned.1.call-done = f32[32,1024]{1,0:T(8,128)} async-done(((f32[1024,1024]{1,0:T(8,128)}), f32[32,1024]{1,0:T(8,128)}) %reduce-scatter.32.cloned.1.call-update) | async-done | bytes 131088 | tf_op jit(solution)/shard_map/reduce_scatter | solution.py:385
  (1255 shorter events, 528.5 us)
Async XLA Ops:
  7.3 178.1 %all-gather.45.cloned.1.call-start = ((), (), s32[]{:S(2)}) async-start(), calls=%async_computation.19 | async-start | bytes 2359296 | tf_op jit(solution)/shard_map/all_gather | solution.py:194
  9.3 29.5 %collective-permute-start.1 = (f32[1]{0:T(128)}, f32[1]{0:T(128)}, u32[]{:S(2)}, u32[]{:S(2)}) collective-permute-start(f32[1]{0:T(128)} %get-tuple-element.2344), channel_id=1, source_target_pairs={{0,1},{1,2},{2,3},{3,4},{4,5},{5,6},{6,7},{8,9},{9,10},{10,11},{11... | collective-permute-start | bytes 20 | tf_op jit(solution)/shard_map/ppermute | solution.py:13
  12.7 27.3 %collective-permute-start.4 = (f32[1]{0:T(128)}, f32[1]{0:T(128)}, u32[]{:S(2)}, u32[]{:S(2)}) collective-permute-start(f32[1]{0:T(128)} %get-tuple-element.2342), channel_id=1, source_target_pairs={{0,1},{1,2},{2,3},{3,4},{4,5},{5,6},{6,7},{8,9},{9,10},{10,11},{11... | collective-permute-start | bytes 20 | tf_op jit(solution)/shard_map/ppermute | solution.py:13
  17.9 23.4 %collective-permute-start.7 = (f32[1]{0:T(128)}, f32[1]{0:T(128)}, u32[]{:S(2)}, u32[]{:S(2)}) collective-permute-start(f32[1]{0:T(128)} %get-tuple-element.2340), channel_id=1, source_target_pairs={{0,1},{1,2},{2,3},{3,4},{4,5},{5,6},{6,7},{8,9},{9,10},{10,11},{11... | collective-permute-start | bytes 20 | tf_op jit(solution)/shard_map/ppermute | solution.py:13
  20.5 22.2 %collective-permute-start.10 = (f32[1]{0:T(128)}, f32[1]{0:T(128)}, u32[]{:S(2)}, u32[]{:S(2)}) collective-permute-start(f32[1]{0:T(128)} %get-tuple-element.2346), channel_id=1, source_target_pairs={{0,1},{1,2},{2,3},{3,4},{4,5},{5,6},{6,7},{8,9},{9,10},{10,11},{11... | collective-permute-start | bytes 20 | tf_op jit(solution)/shard_map/ppermute | solution.py:13
  25.9 655.3 %copy-start.186 = (f32[128]{0:T(128)}, f32[128]{0:T(128)S(1)}, u32[]{:S(2)}) copy-start(f32[128]{0:T(128)S(1)} %broadcast_multiply_fusion.23) | copy-start | bytes 1540
  27.1 654.1 %copy-start.205 = (f32[128]{0:T(128)}, f32[128]{0:T(128)S(1)}, u32[]{:S(2)}) copy-start(f32[128]{0:T(128)S(1)} %add_rsqrt_fusion.3) | copy-start | bytes 1540
  30.5 16.6 collective-permute-start.6
  47.0 629.5 %copy-start.182 = (f32[128]{0:T(128)}, f32[128]{0:T(128)S(1)}, u32[]{:S(2)}) copy-start(f32[128]{0:T(128)S(1)} %get-tuple-element.2378) | copy-start | bytes 1540
  150.9 3.0 collective-permute-start.8
  155.0 72.9 %reduce-scatter.20.cloned.1.call-start = ((), (), s32[]{:S(2)}) async-start(), calls=%async_computation.20 | async-start | bytes 2359296 | tf_op jit(solution)/shard_map/reduce_scatter | solution.py:198
  192.5 66.8 %all-gather.53.cloned.1.call-start = ((), (), s32[]{:S(2)}) async-start(), calls=%async_computation.27 | async-start | bytes 2359296 | tf_op jit(solution)/shard_map/all_gather | solution.py:206
  231.4 70.9 %reduce-scatter.28.cloned.1.call-start = ((), (), s32[]{:S(2)}) async-start(), calls=%async_computation.28 | async-start | bytes 2359296 | tf_op jit(solution)/shard_map/reduce_scatter | solution.py:211
  266.8 235.1 %all-gather.43.cloned.1.call-start = ((), (), s32[]{:S(2)}) async-start(), calls=%async_computation.17 | async-start | bytes 2359296 | tf_op jit(solution)/shard_map/all_gather | solution.py:194
  305.9 4.3 collective-permute-start.16
  359.5 3.0 collective-permute-start.3
  362.0 637.3 %copy-start.188 = (f32[128]{0:T(128)}, f32[128]{0:T(128)S(1)}, u32[]{:S(2)}) copy-start(f32[128]{0:T(128)S(1)} %get-tuple-element.2380) | copy-start | bytes 1540
  466.3 3.0 collective-permute-start.5
  470.5 74.1 %reduce-scatter.18.cloned.1.call-start = ((), (), s32[]{:S(2)}) async-start(), calls=%async_computation.18 | async-start | bytes 2359296 | tf_op jit(solution)/shard_map/reduce_scatter | solution.py:198
  509.1 67.0 %all-gather.51.cloned.1.call-start = ((), (), s32[]{:S(2)}) async-start(), calls=%async_computation.25 | async-start | bytes 2359296 | tf_op jit(solution)/shard_map/all_gather | solution.py:206
  548.1 71.0 %reduce-scatter.26.cloned.1.call-start = ((), (), s32[]{:S(2)}) async-start(), calls=%async_computation.26 | async-start | bytes 2359296 | tf_op jit(solution)/shard_map/reduce_scatter | solution.py:211
  583.6 244.9 %all-gather.41.cloned.1.call-start = ((), (), s32[]{:S(2)}) async-start(), calls=%async_computation.15 | async-start | bytes 2359296 | tf_op jit(solution)/shard_map/all_gather | solution.py:194
  624.1 7.8 collective-permute-start.14
  629.5 51.7 %collective-permute-start.17 = (f32[1,1024]{1,0:T(1,128)S(1)}, f32[1,1024]{1,0:T(1,128)S(1)}, u32[]{:S(2)}, u32[]{:S(2)}) collective-permute-start(f32[1,1024]{1,0:T(1,128)S(1)} %slice.671), channel_id=1, source_target_pairs={{1,0},{2,1},{3,2},{4,3},{5,4},{6,5},{7,6},{9,8},{10,9},{11,10},{12... | collective-permute-start | bytes 12296 | tf_op jit(solution)/shard_map/ppermute | solution.py:13
  681.2 318.1 %copy-start.207 = (f32[128]{0:T(128)}, f32[128]{0:T(128)S(1)}, u32[]{:S(2)}) copy-start(f32[128]{0:T(128)S(1)} %add_rsqrt_fusion.7) | copy-start | bytes 1540
  683.7 3.0 collective-permute-start
  792.1 3.0 collective-permute-start.2
  796.3 74.8 %reduce-scatter.16.cloned.1.call-start = ((), (), s32[]{:S(2)}) async-start(), calls=%async_computation.16 | async-start | bytes 2359296 | tf_op jit(solution)/shard_map/reduce_scatter | solution.py:198
  835.6 67.0 %all-gather.49.cloned.1.call-start = ((), (), s32[]{:S(2)}) async-start(), calls=%async_computation.23 | async-start | bytes 2359296 | tf_op jit(solution)/shard_map/all_gather | solution.py:206
  874.6 70.9 %reduce-scatter.24.cloned.1.call-start = ((), (), s32[]{:S(2)}) async-start(), calls=%async_computation.24 | async-start | bytes 2359296 | tf_op jit(solution)/shard_map/reduce_scatter | solution.py:211
  910.2 230.7 %all-gather.47.cloned.1.call-start = ((), (), s32[]{:S(2)}) async-start(), calls=%async_computation.21 | async-start | bytes 2359296 | tf_op jit(solution)/shard_map/all_gather | solution.py:194
  950.7 3.7 collective-permute-start.12
  1004.9 3.0 collective-permute-start.9
  1105.2 3.0 collective-permute-start.11
  1109.4 74.2 %reduce-scatter.22.cloned.1.call-start = ((), (), s32[]{:S(2)}) async-start(), calls=%async_computation.22 | async-start | bytes 2359296 | tf_op jit(solution)/shard_map/reduce_scatter | solution.py:198
  1148.1 66.9 %all-gather.55.cloned.1.call-start = ((), (), s32[]{:S(2)}) async-start(), calls=%async_computation.29 | async-start | bytes 2359296 | tf_op jit(solution)/shard_map/all_gather | solution.py:206
  1187.1 70.9 %reduce-scatter.30.cloned.1.call-start = ((), (), s32[]{:S(2)}) async-start(), calls=%async_computation.30 | async-start | bytes 2359296 | tf_op jit(solution)/shard_map/reduce_scatter | solution.py:211
  1222.5 136.4 %reduce-scatter.42.cloned.1.call-start = ((), (), s32[]{:S(2)}) async-start(), calls=%async_computation.36 | async-start | bytes 1310720 | tf_op jit(solution)/shard_map/reduce_scatter | solution.py:399
  1233.2 127.5 %reduce-scatter.40.cloned.1.call-start = ((), (), s32[]{:S(2)}) async-start(), calls=%async_computation.35 | async-start | bytes 1310720 | tf_op jit(solution)/shard_map/reduce_scatter | solution.py:396
  1242.7 220.9 %reduce-scatter.44.cloned.1.call-start = ((), (), s32[]{:S(2)}) async-start(), calls=%async_computation.37 | async-start | bytes 4325376 | tf_op jit(solution)/shard_map/reduce_scatter | solution.py:393
  1249.6 356.4 %reduce-scatter.38.cloned.1.call-start = ((), (), s32[]{:S(2)}) async-start(), calls=%async_computation.34 | async-start | bytes 4325376 | tf_op jit(solution)/shard_map/reduce_scatter | solution.py:388
  1261.5 3.2 collective-permute-start.18
  1270.9 477.2 %reduce-scatter.36.cloned.1.call-start = ((), (), s32[]{:S(2)}) async-start(), calls=%async_computation.33 | async-start | bytes 4325376 | tf_op jit(solution)/shard_map/reduce_scatter | solution.py:387
  1284.9 605.5 %reduce-scatter.34.cloned.1.call-start = ((), (), s32[]{:S(2)}) async-start(), calls=%async_computation.32 | async-start | bytes 4325376 | tf_op jit(solution)/shard_map/reduce_scatter | solution.py:386
  1338.9 694.3 %reduce-scatter.32.cloned.1.call-start = ((), (), s32[]{:S(2)}) async-start(), calls=%async_computation.31 | async-start | bytes 4325376 | tf_op jit(solution)/shard_map/reduce_scatter | solution.py:385
  1350.2 20.5 %collective-permute-start.15 = (f32[1,1024]{1,0:T(1,128)}, f32[1,1024]{1,0:T(1,128)S(1)}, u32[]{:S(2)}, u32[]{:S(2)}) collective-permute-start(f32[1,1024]{1,0:T(1,128)} %slice.663), channel_id=1, source_target_pairs={{1,0},{2,1},{3,2},{4,3},{5,4},{6,5},{7,6},{9,8},{10,9},{11,10},{12... | collective-permute-start | bytes 12296 | tf_op jit(solution)/shard_map/ppermute | solution.py:13
  1355.8 15.0 collective-permute-start.13
  1369.1 4.3 collective-permute-start.19
  (302 other events, 4213.9 us)
Sparse Core Ops, SparseCore 0:
  155.2 30.1 all-gather.44
  192.7 35.2 reduce-scatter.19
  231.5 27.7 all-gather.52
  266.9 35.3 reduce-scatter.27
  470.6 31.2 all-gather.42
  509.2 35.2 reduce-scatter.17
  548.2 27.8 all-gather.50
  583.7 35.2 reduce-scatter.25
  796.4 32.0 all-gather.40
  835.7 35.2 reduce-scatter.15
  874.8 27.8 all-gather.48
  910.3 35.2 reduce-scatter.23
  1109.5 31.3 all-gather.46
  1148.2 35.3 reduce-scatter.21
  1187.2 27.6 all-gather.54
  1222.6 35.2 reduce-scatter.29
  1260.7 26.4 reduce-scatter.41
  1290.2 27.7 reduce-scatter.39
  1320.8 142.7 reduce-scatter.43
  1466.3 139.6 reduce-scatter.37
  1608.8 139.2 reduce-scatter.35
  1750.9 139.3 reduce-scatter.33
  1893.2 139.8 reduce-scatter.31
where the time goes:
time: 2050 us; the launch traced here: 2040 us
  waiting for transfers between devices  1090 us (53%)
  blocking collectives  494 us (24%)
  matrix products  226 us (11%)
  local copies, waits for them, and re-layouts  83.3 us (4%)
  other arithmetic  71.6 us (3%)
  starting transfers between devices  43.8 us (2%)
  between operations  29 us (1%)
    all_gather x32, blocking collectives, carried_in(): everything = jax.tree.map(lambda part: lax.all_gather(part, axis), shard)  450 us
    reduce_scatter x1, waiting for transfers between devices, body(): lax.psum_scatter(totals[7], ('dp', 'mp'), scatter_dimension=0, tiled=True)  143 us
    reduce_scatter x1, waiting for transfers between devices, body(): lax.psum_scatter(totals[10], ('dp', 'mp'), scatter_dimension=0, tiled=True)  142 us
    reduce_scatter x1, waiting for transfers between devices, body(): lax.psum_scatter(totals[8], ('dp', 'mp'), scatter_dimension=0, tiled=True)  142 us
    reduce_scatter x1, waiting for transfers between devices, body(): lax.psum_scatter(totals[9], ('dp', 'mp'), scatter_dimension=0, tiled=True)  142 us
    reduce_scatter x4, waiting for transfers between devices, one_micro(): lax.psum_scatter(product(squared, return_w).astype(jnp.bfloat16), 'mp', s...  141 us
    all_gather x4, waiting for transfers between devices, one_micro(): hidden_rows = lax.all_gather(low_hidden, 'mp', axis=0, tiled=True)  125 us
    all_gather x4, waiting for transfers between devices, one_micro(): grad_rows = lax.all_gather(grad_ret, 'mp', axis=0, tiled=True)  111 us
  transfers between devices with their start and end apart: 43, of which 30 were waited for; matrix products, arithmetic and copies ran while one was open for 8% of the time, Pallas kernels for 0%

commit v1 on v0

--- a/solution.py
+++ b/solution.py
@@ -201,13 +201,13 @@
     output = block_mid + gate_two * returned
     grad_ret = reduced_precision(grad_out * gate_two)
     grad_gate_pre = reduced_precision(grad_out * returned * gate_two * (1.0 - gate_two))
-    d_gate_w = product_tn(low_gate, grad_gate_pre)
+    d_gate_w = (low_gate, grad_gate_pre)
     grad_low_gate = product_nt(grad_gate_pre, gate_w)
     grad_rows = lax.all_gather(grad_ret, "mp", axis=0, tiled=True)
     grad_squared = product_nt(grad_rows, return_w)
-    d_return = product_tn(squared, grad_rows)
+    d_return = (squared, grad_rows)
     grad_pre = reduced_precision(grad_squared * 2.0 * rectified)
-    d_hidden = product_tn(hidden_rows, grad_pre)
+    d_hidden = (hidden_rows, grad_pre)
     grad_low_hidden = lax.psum_scatter(
         product_nt(grad_pre, hidden_w).astype(jnp.bfloat16), "mp", scatter_dimension=0, tiled=True
     ).astype(jnp.float32)
@@ -225,11 +225,11 @@
     grad_mid_norm, d_gain_two, d_bias_two = norm_back(grad_norm_b, unit_b, inv_b, gain_two)
     grad_mid = grad_out + grad_mid_norm
     grad_att = reduced_precision(grad_mid)
-    d_output_w = product_tn(gated, grad_att)
+    d_output_w = (gated, grad_att)
     grad_gated = product_nt(grad_att, output_w)
     grad_recept_pre = reduced_precision(grad_gated * mixture_result * recept * (1.0 - recept))
     grad_mixed = grad_gated * recept
-    d_recept_w = product_tn(low_recept, grad_recept_pre)
+    d_recept_w = (low_recept, grad_recept_pre)
     grad_low_recept = product_nt(grad_recept_pre, recept_w)
     dividend_adjoint = grad_mixed / divisor_complete
     divisor_adjoint = -dividend_adjoint * mixture_result
@@ -259,8 +259,8 @@
         + cumulative_dividend * weighted_average
         + running_denominator * raised_lookup
     )
-    d_key_w = product_tn(low_key, key_gradient)
-    d_value_w = product_tn(low_value, value_gradient)
+    d_key_w = (low_key, key_gradient)
+    d_value_w = (low_value, value_gradient)
     grad_low_key = product_nt(key_gradient, key_w)
     grad_low_value = product_nt(value_gradient, value_w)
     d_mix_key = jnp.sum(grad_low_key * delta_a, axis=0)
@@ -326,7 +326,6 @@
     feedforward_content_matrix,
     feedforward_admit_matrix,
 ):
-    micro_count = incoming_signal.shape[0]
     hidden_full, return_full = (feedforward_lookup_matrix, feedforward_content_matrix)
     vectors = tuple(
         (
@@ -353,45 +352,39 @@
         attention_result_matrix,
         feedforward_admit_matrix,
     )
-    totals = None
-    outputs_list = []
-    grads_list = []
-    for step_index in range(micro_count):
-        ultimate_result = one_micro(
-            incoming_signal[step_index, 0].astype(jnp.float32),
-            series_number_table[step_index, 0],
-            upstream_adjoint[step_index, 0].astype(jnp.float32),
-            vectors,
-            matrices,
-            hidden_full,
-            return_full,
+    output, input_grad, grads = jax.vmap(
+        lambda rows, ids, adjoint: one_micro(
+            rows, ids, adjoint, vectors, matrices, hidden_full, return_full
         )
-        outputs_list.append(ultimate_result[0])
-        grads_list.append(ultimate_result[1])
-        if totals is None:
-            totals = ultimate_result[2]
-        else:
-            totals = jax.tree.map(jnp.add, totals, ultimate_result[2])
-    output = jnp.stack(outputs_list)[:, None]
-    input_grad = jnp.stack(grads_list)[:, None]
-    owned = (
-        lax.psum_scatter(totals[0], ("dp", "mp"), scatter_dimension=0, tiled=True),
-        lax.psum_scatter(totals[1], ("dp", "mp"), scatter_dimension=0, tiled=True),
-        lax.psum_scatter(totals[2], ("dp", "mp"), scatter_dimension=0, tiled=True),
-        lax.psum_scatter(totals[3], ("dp", "mp"), scatter_dimension=0, tiled=True),
-        lax.psum_scatter(totals[4], ("dp", "mp"), scatter_dimension=0, tiled=True),
-        lax.psum_scatter(totals[5], ("dp", "mp"), scatter_dimension=0, tiled=True),
-        lax.psum_scatter(totals[6], ("dp", "mp"), scatter_dimension=0, tiled=True),
-        lax.psum_scatter(totals[7], ("dp", "mp"), scatter_dimension=0, tiled=True),
-        lax.psum_scatter(totals[8], ("dp", "mp"), scatter_dimension=0, tiled=True),
-        lax.psum_scatter(totals[9], ("dp", "mp"), scatter_dimension=0, tiled=True),
-        lax.psum_scatter(totals[10], ("dp", "mp"), scatter_dimension=0, tiled=True),
-        lax.psum_scatter(totals[11], ("dp", "mp"), scatter_dimension=0, tiled=True),
-        lax.psum_scatter(totals[12], ("dp", "mp"), scatter_dimension=0, tiled=True),
-        lax.psum_scatter(totals[13], ("dp", "mp"), scatter_dimension=0, tiled=True),
-        lax.psum_scatter(totals[14], ("dp", "mp"), scatter_dimension=0, tiled=True),
-        lax.psum_scatter(totals[17], ("dp", "mp"), scatter_dimension=0, tiled=True),
-    )
+    )(
+        incoming_signal[:, 0].astype(jnp.float32),
+        series_number_table[:, 0],
+        upstream_adjoint[:, 0].astype(jnp.float32),
+    )
+    totals = tuple(
+        product_tn(*(side.reshape(-1, side.shape[-1]) for side in grad))
+        if isinstance(grad, tuple)
+        else jnp.sum(grad, axis=0)
+        for grad in grads
+    )
+    square = [index for index in range(18) if totals[index].shape == totals[7].shape]
+    lines = [index for index in range(18) if totals[index].ndim == 1]
+    wide = lax.psum_scatter(
+        jnp.concatenate([reduced_precision(totals[index]) for index in square], axis=1),
+        ("dp", "mp"),
+        scatter_dimension=0,
+        tiled=True,
+    ).astype(jnp.float32)
+    thin = lax.psum_scatter(
+        jnp.stack([totals[index] for index in lines], axis=1),
+        ("dp", "mp"),
+        scatter_dimension=0,
+        tiled=True,
+    )
+    held = dict(zip(square, jnp.split(wide, len(square), axis=1)))
+    held.update({index: thin[:, place] for place, index in enumerate(lines)})
+    output, input_grad = (output[:, None], input_grad[:, None])
+    owned = tuple(held[index] for index in sorted(held))
     hidden_own, return_own = (
         lax.psum_scatter(
             totals[15].astype(jnp.bfloat16), "dp", scatter_dimension=0, tiled=True

time: 2050 us -> 989 us (0.48)
  waiting for transfers between devices: 1090 us -> 580 us
  blocking collectives: 494 us -> 118 us
  matrix products: 226 us -> 114 us
  starting transfers between devices: 43.8 us -> 13.6 us
    reduce_scatter x5 -> x0, waiting for transfers between devices: 603 us -> none  [the longest x1 143 us: body(): lax.psum_scatter(totals[7], ('dp', 'mp'), scatter_dimension=0, tiled=True)]
    all_gather x32 -> x8, blocking collectives: 450 us -> 118 us  [carried_in(): everything = jax.tree.map(lambda part: lax.all_gather(part, axis), shard)]
    unnamed x23 -> x10, waiting for transfers between devices: 0.38 us -> 257 us
    reduce_scatter x4 -> x1, waiting for transfers between devices: 141 us -> 87.9 us  [one_micro(): lax.psum_scatter(product(squared, return_w).astype(jnp.bfloat16), 'mp', s...]
    unnamed x1 -> x0, blocking collectives: 43.6 us -> none
    dot_general x28 -> x7, matrix products: 79.9 us -> 37.6 us  [product_nt(): lax.dot_general(left, right, (((1,), (1,)), ((), ())), preferred_element_...]
    all_gather x4 -> x1, waiting for transfers between devices: 125 us -> 83.2 us  [one_micro(): hidden_rows = lax.all_gather(low_hidden, 'mp', axis=0, tiled=True)]
    dot_general x28 -> x7, matrix products: 72.8 us -> 37.2 us  [product(): return jnp.dot(left, right, preferred_element_type=jnp.float32)]
  transfers between devices with their start and end apart: 43 -> 13, of which waited for: 30 -> 7; matrix products, arithmetic and copies ran while one was open for 8% -> 13% of each run, Pallas kernels for 0% -> 0%
where the time goes in v1:
time: 989 us; the launch traced here: 978 us
  waiting for transfers between devices  580 us (59%)
  blocking collectives  118 us (12%)
  matrix products  114 us (12%)
  other arithmetic  72.8 us (7%)
  local copies, waits for them, and re-layouts  64 us (6%)
  between operations  16 us (2%)
  starting transfers between devices  13.6 us (1%)
    unnamed x10, waiting for transfers between devices  257 us
    all_gather x8, blocking collectives, carried_in(): everything = jax.tree.map(lambda part: lax.all_gather(part, axis), shard)  118 us
    reduce_scatter x1, waiting for transfers between devices, one_micro(): lax.psum_scatter(product(squared, return_w).astype(jnp.bfloat16), 'mp', s...  87.9 us
    all_gather x1, waiting for transfers between devices, one_micro(): hidden_rows = lax.all_gather(low_hidden, 'mp', axis=0, tiled=True)  83.2 us
    all_gather x1, waiting for transfers between devices, one_micro(): grad_rows = lax.all_gather(grad_ret, 'mp', axis=0, tiled=True)  80.5 us
    reduce_scatter x1, waiting for transfers between devices, one_micro(): lax.psum_scatter(product_nt(grad_pre, hidden_w).astype(jnp.bfloat16), 'mp...  70.1 us
    unnamed x242, local copies, waits for them, and re-layouts  56.4 us
    dot_general x7, matrix products, product_nt(): lax.dot_general(left, right, (((1,), (1,)), ((), ())), preferred_element_...  37.6 us
  transfers between devices with their start and end apart: 13, of which 7 were waited for; matrix products, arithmetic and copies ran while one was open for 13% of the time, Pallas kernels for 0%

profile of v1, /device:TPU:0, one launch (start us, length us, event | category | flops | bytes accessed | tf_op | source)
XLA Modules:
  0.0 978.5 jit_solution(23520644371781199)
XLA Ops:
  8.2 2.3 collective-permute-start.1
  16.2 5.2 collective-permute-start
  26.1 15.0 %all_gather.53 = f32[4,8,1024]{2,0,1:T(4,128)} all-gather(f32[4,1,1024]{2,0,1:T(4,128)S(1)} %get-tuple-element.853), channel_id=1, replica_groups=mesh['dp'=4,'mp'=8] {'mp'}, dimensions={1}, use_global_device_ids=true | all-gather | bytes 147456 | tf_op jit(solution)/shard_map/vmap()/all_gather | solution.py:18
  41.8 14.0 %all_gather.48 = f32[4,8,1024]{2,0,1:T(4,128)S(1)} all-gather(f32[4,1,1024]{2,0,1:T(4,128)S(1)} %get-tuple-element.854), channel_id=1, replica_groups=mesh['dp'=4,'mp'=8] {'mp'}, dimensions={1}, use_global_device_ids=true | all-gather | bytes 147456 | tf_op jit(solution)/shard_map/vmap()/all_gather | solution.py:18
  55.8 4.7 add_convert_fusion.3
  61.9 4.2 broadcast_multiply_fusion.1
  66.2 6.6 fusion.9
  72.7 3.5 copy-done.10
  76.4 15.1 %all-gather.3 = f32[4,8192]{1,0:T(4,128)} all-gather(f32[4,1024]{1,0:T(4,128)S(1)} %get-tuple-element.838), channel_id=5, replica_groups=mesh['dp'=4,'mp'=8] {'mp'}, dimensions={1}, use_global_device_ids=true | all-gather | bytes 147456 | tf_op jit(solution)/shard_map/vmap()/all_gather | solution.py:18
  91.4 15.1 %all-gather.2 = f32[4,8192]{1,0:T(4,128)} all-gather(f32[4,1024]{1,0:T(4,128)S(1)} %get-tuple-element.839), channel_id=4, replica_groups=mesh['dp'=4,'mp'=8] {'mp'}, dimensions={1}, use_global_device_ids=true | all-gather | bytes 147456 | tf_op jit(solution)/shard_map/vmap()/all_gather | solution.py:18
  106.5 15.1 %all-gather.1 = f32[4,8192]{1,0:T(4,128)} all-gather(f32[4,1024]{1,0:T(4,128)S(1)} %get-tuple-element.840), channel_id=3, replica_groups=mesh['dp'=4,'mp'=8] {'mp'}, dimensions={1}, use_global_device_ids=true | all-gather | bytes 147456 | tf_op jit(solution)/shard_map/vmap()/all_gather | solution.py:18
  121.6 15.3 %all-gather = f32[4,8192]{1,0:T(4,128)} all-gather(f32[4,1024]{1,0:T(4,128)S(1)} %get-tuple-element.841), channel_id=2, replica_groups=mesh['dp'=4,'mp'=8] {'mp'}, dimensions={1}, use_global_device_ids=true | all-gather | bytes 147456 | tf_op jit(solution)/shard_map/vmap()/all_gather | solution.py:18
  136.8 12.7 %while.47 = (s32[]{:T(128)}, f32[4,1024]{1,0:T(4,128)}, f32[4,1024]{1,0:T(4,128)}, f32[4,1024]{1,0:T(4,128)}, f32[4,1024]{1,0:T(4,128)S(1)}, /*index=5*/s32[]{:T...) while((s32[]{:T(128)}, f32[4,1024]{1,0:T(4,128)}, ...), condition=%wide.region_3.4_spmd.clone, body=%wide.region_2.3_spmd.clone.sunk | while | flops 81926 | bytes 229565 | solution.py:31
  149.6 9.0 multiply_convert_fusion.3
  161.1 2.2 collective-permute-start.2
  164.1 4.2 add_convert_fusion.1
  168.4 83.2 %all-gather.7.cloned.1.call-done = bf16[4,1024,1024]{2,1,0:T(8,128)(2,1)} async-done(((bf16[4,128,1024]{2,1,0:T(8,128)(2,1)}), bf16[4,1024,1024]{2,1,0:T(8,128)(2,1)}) %all-gather.7.cloned.1.call-update) | async-done | bytes 8388624 | tf_op jit(solution)/shard_map/vmap()/all_gather | solution.py:194
  251.6 7.4 fusion.101
  259.1 3.3 copy-done.14
  262.4 6.7 convolution_convert_fusion.1
  269.6 87.9 %reduce-scatter.11.cloned.1.call-done = bf16[4,128,1024]{2,1,0:T(8,128)(2,1)} async-done(((bf16[4,1024,1024]{2,1,0:T(8,128)(2,1)}), bf16[4,128,1024]{2,1,0:T(8,128)(2,1)}) %reduce-scatter.11.cloned.1.call-update) | async-done | bytes 1048592 | tf_op jit(solution)/shard_map/vmap()/reduce_scatter | solution.py:198
  357.5 7.2 fusion.52
  364.8 80.5 %all-gather.9.cloned.1.call-done = bf16[4,1024,1024]{2,1,0:T(8,128)(2,1)} async-done(((bf16[4,128,1024]{2,1,0:T(8,128)(2,1)}), bf16[4,1024,1024]{2,1,0:T(8,128)(2,1)}) %all-gather.9.cloned.1.call-update) | async-done | bytes 8388624 | tf_op jit(solution)/shard_map/vmap()/all_gather | solution.py:206
  445.3 11.0 %multiply_convert_fusion = bf16[4,1024,512]{2,1,0:T(8,128)(2,1)S(1)} fusion(f32[4,1024,512]{2,1,0:T(8,128)} %copy-done.14, bf16[4,1024,1024]{2,1,0:T(8,128)(2,1)} %all-gather.9.cloned.1.call-done, bf16[512,1024]{1,0:T(8,128)(2,1)} %param.44), kind=kOutput, calls=%fused_computation.32 | convolution fusion | flops 4303355904 | bytes 22020096 | tf_op jit(solution)/shard_map/vmap()/dot_general | solution.py:49
  456.3 2.1 copy-done.106
  458.4 7.2 convolution_convert_fusion
  471.1 11.3 %bitcast_convert_fusion.5 = bf16[512,1024]{1,0:T(8,128)(2,1)} fusion(bf16[4,1024,1024]{2,1,0:T(8,128)(2,1)} %all-gather.9.cloned.1.call-done, f32[4,1024,512]{2,1,0:T(8,128)} %copy-done.14), kind=kOutput, calls=%fused_computation.114 | convolution fusion | flops 4301783040 | bytes 17825792 | tf_op jit(solution)/shard_map/dot_general | solution.py:43
  483.8 70.1 %reduce-scatter.13.cloned.1.call-done = bf16[4,128,1024]{2,1,0:T(8,128)(2,1)} async-done(((bf16[4,1024,1024]{2,1,0:T(8,128)(2,1)}), bf16[4,128,1024]{2,1,0:T(8,128)(2,1)}) %reduce-scatter.13.cloned.1.call-update) | async-done | bytes 1048592 | tf_op jit(solution)/shard_map/vmap()/reduce_scatter | solution.py:211
  553.9 7.2 multiply_reduce_fusion
  564.4 8.2 bitcast_convert_fusion.6
  573.0 2.0 slice.304
  575.9 3.5 multiply_reduce_fusion.1
  583.3 8.0 fusion.112
  592.7 4.2 fusion.17
  597.0 2.1 copy-done.8
  599.1 14.1 %all_gather.61 = f32[4,8,1024]{2,0,1:T(4,128)S(1)} all-gather(f32[4,1,1024]{2,0,1:T(4,128)S(1)} %get-tuple-element.860), channel_id=1, replica_groups=mesh['dp'=4,'mp'=8] {'mp'}, dimensions={1}, use_global_device_ids=true | all-gather | bytes 147456 | tf_op jit(solution)/shard_map/vmap()/all_gather | solution.py:18
  613.2 14.2 %all_gather.60 = f32[4,8,1024]{2,0,1:T(4,128)S(1)} all-gather(f32[4,1,1024]{2,0,1:T(4,128)S(1)} %get-tuple-element.861), channel_id=1, replica_groups=mesh['dp'=4,'mp'=8] {'mp'}, dimensions={1}, use_global_device_ids=true | all-gather | bytes 147456 | tf_op jit(solution)/shard_map/vmap()/all_gather | solution.py:18
  627.4 10.9 %while.48 = (s32[]{:T(128)}, f32[4,1024]{1,0:T(4,128)}, f32[4,1024]{1,0:T(4,128)S(1)}, s32[]{:T(128)}, f32[4,8,1024]{2,0,1:T(4,128)S(1)}, /*index=5*/f32[4,8,102...) while((s32[]{:T(128)}, f32[4,1024]{1,0:T(4,128)}, ...), condition=%wide.region_11.12_spmd.clone, body=%wide.region_10.11_spmd.clone.sunk | while | flops 32778 | bytes 114899 | solution.py:31
  638.3 5.9 add_convert_fusion
  656.5 4.0 copy-done.9
  662.2 4.9 fusion.35
  668.3 4.2 fusion.90
  672.5 13.9 %copy.160 = bf16[1024,5120]{1,0:T(8,128)(2,1)} copy(bf16[1024,5120]{0,1:T(8,128)(2,1)} %fusion.90) | data formatting | bytes 20971520
  690.0 4.3 fusion.34
  694.3 108.3 %reduce-scatter.19.cloned.1.call-done = f32[32,11]{1,0:T(8,128)} async-done(((f32[1024,11]{1,0:T(8,128)}), f32[32,11]{1,0:T(8,128)}) %reduce-scatter.19.cloned.1.call-update) | async-done | bytes 1424
  810.2 149.0 %reduce-scatter.21.cloned.1.call-done = bf16[32,5120]{1,0:T(8,128)(2,1)} async-done(((bf16[1024,5120]{1,0:T(8,128)(2,1)}), bf16[32,5120]{1,0:T(8,128)(2,1)}) %reduce-scatter.21.cloned.1.call-update) | async-done | bytes 327696
  959.2 2.3 copy.161
  961.5 2.4 fusion.127
  (365 shorter events, 90.3 us)
Async XLA Ops:
  7.2 54.7 %copy-start = (bf16[1024,1024]{1,0:T(8,128)(2,1)S(1)}, bf16[1024,1024]{1,0:T(8,128)(2,1)}, u32[]{:S(2)}) copy-start(bf16[1024,1024]{1,0:T(8,128)(2,1)} %param.36) | copy-start | bytes 6291460
  7.2 6.6 copy-start.3
  7.2 244.4 %all-gather.7.cloned.1.call-start = ((), (), s32[]{:S(2)}) async-start(), calls=%async_computation.6 | async-start | bytes 9437184 | tf_op jit(solution)/shard_map/vmap()/all_gather | solution.py:194
  8.2 17.7 %collective-permute-start.1 = (f32[4,1]{1,0:T(4,128)S(1)}, f32[4,1]{1,0:T(4,128)S(1)}, u32[]{:S(2)}, u32[]{:S(2)}) collective-permute-start(f32[4,1]{1,0:T(4,128)S(1)} %slice.128), channel_id=1, source_target_pairs={{0,1},{1,2},{2,3},{3,4},{4,5},{5,6},{6,7},{8,9},{9,10},{10,11},{11... | collective-permute-start | bytes 56 | tf_op jit(solution)/shard_map/vmap()/ppermute | solution.py:13
  12.0 9.4 copy-start.37
  12.0 9.9 %copy-start.93 = (bf16[1024]{0:T(1024)(128)(2,1)S(1)}, bf16[1024]{0:T(1024)(128)(2,1)}, u32[]{:S(2)}) copy-start(bf16[1024]{0:T(1024)(128)(2,1)} %param.39) | copy-start | bytes 6148
  12.0 10.5 %copy-start.94 = (bf16[1024]{0:T(1024)(128)(2,1)S(1)}, bf16[1024]{0:T(1024)(128)(2,1)}, u32[]{:S(2)}) copy-start(bf16[1024]{0:T(1024)(128)(2,1)} %param.31) | copy-start | bytes 6148
  12.0 11.1 %copy-start.95 = (bf16[1024]{0:T(1024)(128)(2,1)S(1)}, bf16[1024]{0:T(1024)(128)(2,1)}, u32[]{:S(2)}) copy-start(bf16[1024]{0:T(1024)(128)(2,1)} %param.40) | copy-start | bytes 6148
  12.0 11.6 %copy-start.82 = (bf16[1024]{0:T(1024)(128)(2,1)S(1)}, bf16[1024]{0:T(1024)(128)(2,1)}, u32[]{:S(2)}) copy-start(bf16[1024]{0:T(1024)(128)(2,1)} %param.32) | copy-start | bytes 6148
  12.1 11.6 %copy-start.83 = (bf16[1024]{0:T(1024)(128)(2,1)S(1)}, bf16[1024]{0:T(1024)(128)(2,1)}, u32[]{:S(2)}) copy-start(bf16[1024]{0:T(1024)(128)(2,1)} %param.33) | copy-start | bytes 6148
  12.1 11.6 %copy-start.84 = (bf16[1024]{0:T(1024)(128)(2,1)S(1)}, bf16[1024]{0:T(1024)(128)(2,1)}, u32[]{:S(2)}) copy-start(bf16[1024]{0:T(1024)(128)(2,1)} %param.34) | copy-start | bytes 6148
  12.1 11.7 %copy-start.96 = (bf16[1024]{0:T(1024)(128)(2,1)S(1)}, bf16[1024]{0:T(1024)(128)(2,1)}, u32[]{:S(2)}) copy-start(bf16[1024]{0:T(1024)(128)(2,1)} %param.30) | copy-start | bytes 6148
  13.8 7.9 copy-start.57
  13.8 7.8 copy-start.40
  13.8 7.8 copy-start.52
  16.2 39.5 %collective-permute-start = (f32[4,1,1024]{2,1,0:T(1,128)}, f32[4,1,1024]{2,1,0:T(1,128)}, u32[]{:S(2)}, u32[]{:S(2)}) collective-permute-start(f32[4,1,1024]{2,1,0:T(1,128)} %slice.293), channel_id=1, source_target_pairs={{0,1},{1,2},{2,3},{3,4},{4,5},{5,6},{6,7},{8,9},{9,10},{10,11},{11... | collective-permute-start | bytes 49160 | tf_op jit(solution)/shard_map/vmap()/ppermute | solution.py:13
  21.4 20.3 %copy-start.98 = (f32[128]{0:T(128)}, f32[128]{0:T(128)S(1)}, u32[]{:S(2)}) copy-start(f32[128]{0:T(128)S(1)} %add_negate_fusion) | copy-start | bytes 1540
  21.6 20.1 %copy-start.87 = (s32[4]{0:T(128)}, s32[4]{0:T(128)S(1)}, u32[]{:S(2)}) copy-start(s32[4]{0:T(128)S(1)} %get-tuple-element.759) | copy-start | bytes 52
  21.6 20.1 %copy-start.88 = (s32[4]{0:T(128)}, s32[4]{0:T(128)S(1)}, u32[]{:S(2)}) copy-start(s32[4]{0:T(128)S(1)} %get-tuple-element.760) | copy-start | bytes 52
  21.8 34.0 %copy-start.6 = (f32[4,128,1024]{2,1,0:T(8,128)S(1)}, f32[4,128,1024]{2,1,0:T(8,128)}, u32[]{:S(2)}) copy-start(f32[4,128,1024]{2,1,0:T(8,128)} %copy-done.5) | copy-start | bytes 6291460
  21.8 34.0 %copy-start.41 = (f32[1024]{0:T(1024)S(1)}, f32[1024]{0:T(1024)}, u32[]{:S(2)}) copy-start(f32[1024]{0:T(1024)} %copy-done.40) | copy-start | bytes 12292
  21.8 34.0 %copy-start.49 = (f32[4,128]{1,0:T(4,128)S(1)}, f32[4,128]{1,0:T(4,128)}, u32[]{:S(2)}) copy-start(f32[4,128]{1,0:T(4,128)} %copy-done.48) | copy-start | bytes 6148
  21.8 33.9 %copy-start.53 = (f32[1024]{0:T(1024)S(1)}, f32[1024]{0:T(1024)}, u32[]{:S(2)}) copy-start(f32[1024]{0:T(1024)} %copy-done.52) | copy-start | bytes 12292
  21.8 33.9 %copy-start.58 = (f32[4,128]{1,0:T(4,128)S(1)}, f32[4,128]{1,0:T(4,128)}, u32[]{:S(2)}) copy-start(f32[4,128]{1,0:T(4,128)} %copy-done.57) | copy-start | bytes 6148
  23.7 36.8 %copy-start.65 = (f32[1024]{0:T(1024)}, f32[1024]{0:T(1024)S(1)}, u32[]{:S(2)}) copy-start(f32[1024]{0:T(1024)S(1)} %convert_element_type.164) | copy-start | bytes 12292
  23.7 36.8 %copy-start.67 = (f32[1024]{0:T(1024)}, f32[1024]{0:T(1024)S(1)}, u32[]{:S(2)}) copy-start(f32[1024]{0:T(1024)S(1)} %convert_element_type.166) | copy-start | bytes 12292
  23.8 36.8 %copy-start.69 = (f32[1024]{0:T(1024)}, f32[1024]{0:T(1024)S(1)}, u32[]{:S(2)}) copy-start(f32[1024]{0:T(1024)S(1)} %convert_element_type.161) | copy-start | bytes 12292
  24.4 16.8 %copy-start.63 = (f32[1024]{0:T(1024)}, f32[1024]{0:T(1024)S(1)}, u32[]{:S(2)}) copy-start(f32[1024]{0:T(1024)S(1)} %get-tuple-element.865) | copy-start | bytes 12292
  25.8 36.0 %copy-start.21 = (f32[128,1024]{1,0:T(8,128)}, f32[128,1024]{1,0:T(8,128)S(1)}, u32[]{:S(2)}) copy-start(f32[128,1024]{1,0:T(8,128)S(1)} %get-tuple-element.857) | copy-start | bytes 1572868
  26.0 15.7 %copy-start.89 = (f32[4]{0:T(128)}, f32[4]{0:T(128)S(1)}, u32[]{:S(2)}) copy-start(f32[4]{0:T(128)S(1)} %get-tuple-element.761) | copy-start | bytes 52
  41.8 18.8 %copy-start.45 = (f32[4,128]{1,0:T(4,128)}, f32[4,128]{1,0:T(4,128)S(1)}, u32[]{:S(2)}) copy-start(f32[4,128]{1,0:T(4,128)S(1)} %get-tuple-element.875) | copy-start | bytes 6148
  149.6 9.0 copy-start.32
  149.6 9.0 copy-start.100
  161.0 7.3 copy-start.4
  161.1 3.1 collective-permute-start.2
  168.4 189.1 %reduce-scatter.11.cloned.1.call-start = ((), (), s32[]{:S(2)}) async-start(), calls=%async_computation.7 | async-start | bytes 9437184 | tf_op jit(solution)/shard_map/vmap()/reduce_scatter | solution.py:198
  251.6 10.8 %copy-start.104 = (bf16[512,1024]{1,0:T(8,128)(2,1)S(1)}, bf16[512,1024]{1,0:T(8,128)(2,1)}, u32[]{:S(2)}) copy-start(bf16[512,1024]{1,0:T(8,128)(2,1)} %param.44) | copy-start | bytes 3145732
  269.2 176.1 %all-gather.9.cloned.1.call-start = ((), (), s32[]{:S(2)}) async-start(), calls=%async_computation.8 | async-start | bytes 9437184 | tf_op jit(solution)/shard_map/vmap()/all_gather | solution.py:206
  364.7 189.2 %reduce-scatter.13.cloned.1.call-start = ((), (), s32[]{:S(2)}) async-start(), calls=%async_computation.9 | async-start | bytes 9437184 | tf_op jit(solution)/shard_map/vmap()/reduce_scatter | solution.py:211
  445.3 13.1 %copy-start.105 = (bf16[1024,512]{1,0:T(8,128)(2,1)S(1)}, bf16[1024,512]{1,0:T(8,128)(2,1)}, u32[]{:S(2)}) copy-start(bf16[1024,512]{1,0:T(8,128)(2,1)} %param.43) | copy-start | bytes 3145732
  465.6 220.8 %reduce-scatter.17.cloned.1.call-start = ((), (), s32[]{:S(2)}) async-start(), calls=%async_computation.11 | async-start | bytes 1310720 | tf_op jit(solution)/shard_map/reduce_scatter | solution.py:392
  482.4 205.8 %reduce-scatter.15.cloned.1.call-start = ((), (), s32[]{:S(2)}) async-start(), calls=%async_computation.10 | async-start | bytes 1310720 | tf_op jit(solution)/shard_map/reduce_scatter | solution.py:389
  553.9 10.5 %copy-start.107 = (bf16[4,1024,512]{2,1,0:T(8,128)(2,1)S(1)}, bf16[4,1024,512]{2,1,0:T(8,128)(2,1)}, u32[]{:S(2)}) copy-start(bf16[4,1024,512]{2,1,0:T(8,128)(2,1)} %copy-done.106) | copy-start | bytes 12582916
  563.2 11.8 %collective-permute-start.3 = (f32[4,1,1024]{2,1,0:T(1,128)}, f32[4,1,1024]{2,1,0:T(1,128)}, u32[]{:S(2)}, u32[]{:S(2)}) collective-permute-start(f32[4,1,1024]{2,1,0:T(1,128)} %slice.305), channel_id=1, source_target_pairs={{1,0},{2,1},{3,2},{4,3},{5,4},{6,5},{7,6},{9,8},{10,9},{11,10},{12... | collective-permute-start | bytes 49160 | tf_op jit(solution)/shard_map/vmap()/ppermute | solution.py:13
  572.7 229.9 %reduce-scatter.19.cloned.1.call-start = ((), (), s32[]{:S(2)}) async-start(), calls=%async_computation.12 | async-start | bytes 540672
  580.3 11.0 %copy-start.19 = (f32[4,128,1024]{2,1,0:T(8,128)}, f32[4,128,1024]{2,1,0:T(8,128)S(1)}, u32[]{:S(2)}) copy-start(f32[4,128,1024]{2,1,0:T(8,128)S(1)} %convert_add_fusion) | copy-start | bytes 6291460
  649.2 11.7 %collective-permute-start.4 = (f32[4,1,1024]{2,1,0:T(1,128)S(1)}, f32[4,1,1024]{2,1,0:T(1,128)S(1)}, u32[]{:S(2)}, u32[]{:S(2)}) collective-permute-start(f32[4,1,1024]{2,1,0:T(1,128)S(1)} %slice.311), channel_id=1, source_target_pairs={{1,0},{2,1},{3,2},{4,3},{5,4},{6,5},{7,6},{9,8},{10,9},{11,10},{12... | collective-permute-start | bytes 49160 | tf_op jit(solution)/shard_map/vmap()/ppermute | solution.py:13
  668.3 291.0 %reduce-scatter.21.cloned.1.call-start = ((), (), s32[]{:S(2)}) async-start(), calls=%async_computation.13 | async-start | bytes 10813440
  (76 other events, 236.7 us)
Sparse Core Ops, SparseCore 0:
  168.5 83.0 all-gather.6
  269.3 88.1 reduce-scatter.10
  364.8 80.3 all-gather.8
  465.8 88.1 reduce-scatter.12
  556.7 26.0 reduce-scatter.16
  585.8 27.7 reduce-scatter.14
  668.4 134.0 reduce-scatter.18
  805.0 154.2 reduce-scatter.20

commit v2 on v1

--- a/solution.py
+++ b/solution.py
@@ -1,6 +1,10 @@
+import functools
+
 import jax
 import jax.numpy as jnp
 from jax import lax
+from jax.experimental import pallas as pl
+from jax.experimental.pallas import tpu as pltpu
 from jax.sharding import PartitionSpec as P
 
 EPS = 1e-05
@@ -86,6 +90,676 @@
         latter[1] + latter[2] * earlier[1],
         latter[2] * earlier[2],
     )
+
+
+BF = jnp.bfloat16
+F32 = jnp.float32
+MESH = pl.DeviceIdType.MESH
+NN = (((1,), (0,)), ((), ()))
+NT = (((1,), (1,)), ((), ()))
+TN = (((0,), (0,)), ((), ()))
+
+
+def dot(left, right, form=NN):
+    return lax.dot_general(left, right, form, preferred_element_type=F32)
+
+
+def dot_exact_left(left, right):
+    high = right.astype(BF)
+    rest = (right - high.astype(F32)).astype(BF)
+    return dot(left, high) + dot(left, rest)
+
+
+def wide(lanes, width):
+    return jnp.concatenate([lanes] * (width // 128), axis=1)
+
+
+def tile(index, size):
+    return pl.ds(pl.multiple_of(index * size, size), size)
+
+
+def unit_of(values):
+    average = jnp.mean(values, axis=-1, keepdims=True)
+    centre = values - average
+    inverse = lax.rsqrt(jnp.mean(centre * centre, axis=-1, keepdims=True) + EPS)
+    return (centre * inverse, inverse)
+
+
+def remote(source, target, send, receive, device):
+    return pltpu.make_async_remote_copy(
+        src_ref=source,
+        dst_ref=target,
+        send_sem=send,
+        recv_sem=receive,
+        device_id=device,
+        device_id_type=MESH,
+    )
+
+
+class Place:
+    def __init__(self, planes):
+        self.planes = planes
+        self.dp, self.mp = (lax.axis_index("dp"), lax.axis_index("mp"))
+        self.z = lax.div(self.mp, 2)
+        self.core = lax.rem(self.mp, 2)
+        self.count = 2 * planes
+        self.other = (self.dp, self.mp + 1 - 2 * self.core)
+        self.side_x = (self.dp + 1 - 2 * lax.rem(self.dp, 2), self.mp)
+        self.side_y = (lax.rem(self.dp + 2, 4), self.mp)
+
+    def ahead(self, steps):
+        return (self.dp, lax.rem(self.mp + steps + self.count, self.count))
+
+    def plane(self, steps):
+        return (self.dp, lax.rem(self.z + steps + self.planes, self.planes) * 2 + self.core)
+
+
+def greet(devices):
+    barrier = pltpu.get_barrier_semaphore()
+    for device in devices:
+        pl.semaphore_signal(barrier, inc=1, device_id=device, device_id_type=MESH)
+    pl.semaphore_wait(barrier, len(devices))
+
+
+def forward_kernel(
+    planes,
+    micros,
+    rows,
+    x_ref,
+    last_ref,
+    segcol_ref,
+    segrow_ref,
+    segpay_ref,
+    vec_ref,
+    adj_ref,
+    key_w,
+    value_w,
+    recept_w,
+    output_w,
+    gate_w,
+    w1_ref,
+    w2_ref,
+    k_out,
+    v_out,
+    r_out,
+    num_out,
+    den_out,
+    mid_out,
+    gate_out,
+    mk_out,
+    mv_out,
+    mr_out,
+    gated_out,
+    mg_out,
+    small_out,
+    mh_all,
+    ret_all,
+    w1_all,
+    w2_all,
+    wk,
+    wv,
+    wr,
+    wo,
+    wg,
+    k_s,
+    v_s,
+    r_s,
+    num_s,
+    den_s,
+    mid_s,
+    gate_s,
+    xb_s,
+    mk_s,
+    mv_s,
+    mr_s,
+    gated_s,
+    mg_s,
+    mh_s,
+    ret_s,
+    keep_s,
+    mask_s,
+    halo_a,
+    near_a,
+    pay_b,
+    halo_b,
+    segs_s,
+    state_own,
+    state_other,
+    state_chip,
+    state_in,
+    carry_s,
+    w_sem,
+    out_sem,
+    small_sem,
+    z_sem,
+    s_sem,
+):
+    at = Place(planes)
+    dp, mp, z, core = (at.dp, at.mp, at.z, at.core)
+    tokens = micros * rows
+    peers = [at.ahead(step) for step in range(1, at.count)]
+    greet(peers + [at.side_x, at.side_y])
+
+    quarter1, quarter2 = (w1_ref.shape[0] // 4, w2_ref.shape[0] // 4)
+    q1, q2 = (tile(dp, quarter1), tile(dp, quarter2))
+    z_copies = []
+    for step in range(1, planes):
+        to = at.plane(-step)
+        z_copies.append(
+            (
+                remote(w1_ref.at[q1], w1_all.at[step - 1, q1], z_sem.at[step - 1, 0, 0], z_sem.at[step - 1, 0, 1], to),
+                remote(w2_ref.at[q2], w2_all.at[step - 1, q2], z_sem.at[step - 1, 1, 0], z_sem.at[step - 1, 1, 1], to),
+            )
+        )
+
+    halo_copy = remote(last_ref, halo_a, small_sem.at[0, 0], small_sem.at[0, 1], at.ahead(1))
+    halo_copy.start()
+    seg_copies = [
+        remote(segpay_ref, segs_s.at[mp], small_sem.at[1 + step, 0], small_sem.at[1 + step, 1], device)
+        for step, device in enumerate(peers)
+    ]
+    for copy in seg_copies:
+        copy.start()
+    segs_s[mp] = segpay_ref[...]
+    loads = []
+    for index, (source, target) in enumerate(
+        ((key_w, wk), (value_w, wv), (recept_w, wr), (output_w, wo), (gate_w, wg))
+    ):
+        loads.append(pltpu.make_async_copy(source, target, w_sem.at[index]))
+        loads[-1].start()
+    for copy in z_copies[0]:
+        copy.start()
+    halo_copy.wait()
+    for copy in seg_copies:
+        copy.wait()
+
+    before = lax.rem(mp + at.count - 1, at.count)
+    has_before = mp > 0
+    first_row = lax.broadcasted_iota(jnp.int32, (rows, 128), 0) == 0
+    row_at = lax.broadcasted_iota(jnp.int32, (rows, rows), 0)
+    col_at = lax.broadcasted_iota(jnp.int32, (rows, rows), 1)
+    for m in range(micros):
+        here = segcol_ref[m * rows : (m + 1) * rows, :]
+        behind = jnp.where(
+            first_row, segs_s[before, m : m + 1, :], pltpu.roll(here, 1, 0)
+        )
+        same = jnp.logical_and(
+            here == behind, jnp.logical_or(jnp.logical_not(first_row), has_before)
+        )
+        keep_s[m * rows : (m + 1) * rows, :] = same.astype(F32)
+        mask_s[m] = jnp.logical_and(
+            here == segrow_ref[m : m + 1, :], col_at < row_at
+        ).astype(F32).astype(BF)
+
+    block = 16
+    at_first = lax.broadcasted_iota(jnp.int32, (block, 1024), 0) == 0
+    gain, bias = (vec_ref[0:1, :], vec_ref[1:2, :])
+    near_a[...] = unit_of(halo_a[...])[0] * gain + bias
+    for m in range(micros):
+
+        def mix_a(b, prev, m=m):
+            span = tile(m * (rows // block) + b, block)
+            normed = unit_of(x_ref[span, :].astype(F32))[0] * gain + bias
+            shifted = jnp.where(at_first, prev, pltpu.roll(normed, 1, 0)) * wide(
+                keep_s[span, :], 1024
+            )
+            delta = normed - shifted
+            mk_s[span, :] = (shifted + delta * vec_ref[4:5, :]).astype(BF)
+            mv_s[span, :] = (shifted + delta * vec_ref[5:6, :]).astype(BF)
+            mr_s[span, :] = (shifted + delta * vec_ref[6:7, :]).astype(BF)
+            return normed[block - 1 : block, :]
+
+        lax.fori_loop(0, rows // block, mix_a, near_a[m : m + 1, :])
+
+    outs = []
+
+    def put(source, target):
+        copy = pltpu.make_async_copy(source, target, out_sem.at[len(outs)])
+        copy.start()
+        outs.append(copy)
+
+    put(mk_s, mk_out)
+    put(mv_s, mv_out)
+    put(mr_s, mr_out)
+
+    loads[0].wait()
+    loads[1].wait()
+    width = 256
+    place = lax.broadcasted_iota(jnp.int32, (rows, width), 0).astype(F32)
+
+    @pl.loop(0, 1024 // width)
+    def _(i):
+        cols = tile(i, width)
+        rate = jnp.exp(vec_ref[2:3, cols])
+        rising = jnp.exp(place * rate)
+        falling = jnp.exp((1.0 - place) * rate)
+        step_back = jnp.exp(-rate)
+        keys = dot(mk_s[...], wk[:, cols])
+        values = dot(mv_s[...], wv[:, cols])
+        for m in range(micros):
+            span = slice(m * rows, (m + 1) * rows)
+            key, value = (keys[span], values[span])
+            raised = jnp.exp(key)
+            weighted = raised * value
+            num = falling * dot_exact_left(mask_s[m], rising * weighted)
+            den = falling * dot_exact_left(mask_s[m], rising * raised)
+            k_s[span, cols] = key
+            v_s[span, cols] = value
+            num_s[span, cols] = num
+            den_s[span, cols] = den
+            state_own[m : m + 1, cols] = step_back * num[rows - 1 :] + weighted[rows - 1 :]
+            state_own[micros + m : micros + m + 1, cols] = (
+                step_back * den[rows - 1 :] + raised[rows - 1 :]
+            )
+
+    put(k_s, k_out)
+    put(v_s, v_out)
+    core_copy = remote(state_own, state_other, s_sem.at[0, 0], s_sem.at[0, 1], at.other)
+    core_copy.start()
+    for copy in z_copies[0]:
+        copy.wait()
+    xy_copies = []
+
+    def along(step):
+        group = []
+        own1, own2 = (w1_all.at[step, q1], w2_all.at[step, q2])
+        return (
+            remote(own1, own1, z_sem.at[step, 2, 0], z_sem.at[step, 2, 1], at.side_x),
+            remote(own2, own2, z_sem.at[step, 3, 0], z_sem.at[step, 3, 1], at.side_y),
+        )
+
+    def across(step):
+        both1 = w1_all.at[step, tile(lax.div(dp, 2), 2 * quarter1)]
+        own2 = w2_all.at[step, q2]
+        far2 = w2_all.at[step, tile(lax.rem(dp + 2, 4), quarter2)]
+        return (
+            remote(both1, both1, z_sem.at[step, 4, 0], z_sem.at[step, 4, 1], at.side_y),
+            remote(own2, own2, z_sem.at[step, 5, 0], z_sem.at[step, 5, 1], at.side_x),
+            remote(far2, far2, z_sem.at[step, 6, 0], z_sem.at[step, 6, 1], at.side_x),
+        )
+
+    def start(group):
+        for copy in group:
+            copy.start()
+
+    def finish(group):
+        for copy in group:
+            copy.wait()
+
+    along_0, along_1, along_2 = (along(0), along(1), along(2))
+    across_0, across_1, across_2 = (across(0), across(1), across(2))
+    start(along_0)
+    start(z_copies[2])
+    loads[2].wait()
+
+    @pl.loop(0, 2)
+    def _(i):
+        span = tile(i, tokens // 2)
+        r_s[span, :] = jax.nn.sigmoid(dot(mr_s[span, :], wr[...]))
+
+    put(r_s, r_out)
+
+    pair = lax.div(mp, 2) * 2
+    decay_all = jnp.exp(-float(rows) * jnp.exp(vec_ref[2:3, :]))
+    core_copy.wait()
+
+    def last_of(device):
+        return wide(segs_s[lax.rem(device + at.count, at.count), 0 : 2 * micros, :], 1024)
+
+    even = jnp.where(core == 0, state_own[...], state_other[...])
+    odd = jnp.where(core == 0, state_other[...], state_own[...])
+    state_chip[...] = odd + jnp.where(last_of(pair) == last_of(pair + 1), decay_all * even, 0.0)
+    chip_copies = [
+        remote(state_chip, state_in.at[step - 1], s_sem.at[step, 0], s_sem.at[step, 1], at.plane(step))
+        for step in range(1, planes)
+    ]
+    start(chip_copies)
+    finish(along_0)
+    start(across_0)
+    finish(chip_copies)
+    total = jnp.zeros_like(state_chip[...])
+    power = jnp.ones_like(decay_all)
+    for step in range(1, planes):
+        fits = jnp.logical_and(
+            last_of(pair - 2 * step + 1) == last_of(pair - 1), z >= step
+        )
+        total = total + jnp.where(fits, power * state_in[step - 1], 0.0)
+        power = power * decay_all * decay_all
+    joined = state_other[...] + jnp.where(last_of(pair) == last_of(pair - 1), decay_all * total, 0.0)
+    carry_s[...] = jnp.where(core == 0, total, joined)
+
+    @pl.loop(0, 1024 // width)
+    def _(i):
+        cols = tile(i, width)
+        rate = jnp.exp(vec_ref[2:3, cols])
+        falling = jnp.exp(-place * rate)
+        extra = vec_ref[3:4, cols]
+        for m in range(micros):
+            span = slice(m * rows, (m + 1) * rows)
+            fits = jnp.logical_and(
+                segcol_ref[span, :] == segs_s[before, m : m + 1, :], has_before
+            ).astype(F32)
+            carried = wide(fits, width) * falling
+            num = num_s[span, cols] + carried * carry_s[m : m + 1, cols]
+            den = den_s[span, cols] + carried * carry_s[micros + m : micros + m + 1, cols]
+            bonus = jnp.exp(extra + k_s[span, cols])
+            mixed = (num + bonus * v_s[span, cols]) / (den + bonus)
+            num_s[span, cols] = num
+            den_s[span, cols] = den
+            gated_s[span, cols] = (r_s[span, cols] * mixed).astype(BF)
+
+    put(num_s, num_out)
+    put(den_s, den_out)
+    put(gated_s, gated_out)
+    loads[3].wait()
+
+    @pl.loop(0, 2)
+    def _(i):
+        span = tile(i, tokens // 2)
+        mid_s[span, :] = x_ref[span, :].astype(F32) + dot(gated_s[span, :], wo[...])
+
+    put(mid_s, mid_out)
+    gain_b, bias_b = (vec_ref[7:8, :], vec_ref[8:9, :])
+
+    def norm_b(b):
+        span = tile(b, block)
+        xb_s[span, :] = unit_of(mid_s[span, :])[0] * gain_b + bias_b
+
+    for m in range(micros):
+        norm_b((m + 1) * (rows // block) - 1)
+        pay_b[m : m + 1, :] = xb_s[(m + 1) * rows - 1 : (m + 1) * rows, :]
+    pay_b[micros:, :] = jnp.zeros((8 - micros, 1024), F32)
+    halo_b_copy = remote(pay_b, halo_b, s_sem.at[planes, 0], s_sem.at[planes, 1], at.ahead(1))
+    halo_b_copy.start()
+    for m in range(micros):
+
+        @pl.loop(m * (rows // block), (m + 1) * (rows // block) - 1)
+        def _(b):
+            norm_b(b)
+
+    finish(z_copies[2])
+    start(along_2)
+    start(z_copies[1])
+    halo_b_copy.wait()
+    for m in range(micros):
+
+        def mix_b(b, prev, m=m):
+            span = tile(m * (rows // block) + b, block)
+            normed = xb_s[span, :]
+            shifted = jnp.where(at_first, prev, pltpu.roll(normed, 1, 0)) * wide(
+                keep_s[span, :], 1024
+            )
+            delta = normed - shifted
+            mh_s[span, :] = (shifted + delta * vec_ref[9:10, :]).astype(BF)
+            mg_s[span, :] = (shifted + delta * vec_ref[10:11, :]).astype(BF)
+            return normed[block - 1 : block, :]
+
+        lax.fori_loop(0, rows // block, mix_b, halo_b[m : m + 1, :])
+
+    mh_copy = remote(
+        mh_s, mh_all.at[1], s_sem.at[planes + 1, 0], s_sem.at[planes + 1, 1], at.other
+    )
+    mh_copy.start()
+    put(mh_s, mh_all.at[0])
+    put(mg_s, mg_out)
+    loads[4].wait()
+
+    @pl.loop(0, 2)
+    def _(i):
+        span = tile(i, tokens // 2)
+        gate = jax.nn.sigmoid(dot(mg_s[span, :], wg[...]))
+        gate_s[span, :] = gate
+        ret_s[span, :] = (adj_ref[span, :].astype(F32) * gate).astype(BF)
+
+    ret_copy = remote(
+        ret_s, ret_all.at[1], s_sem.at[planes + 2, 0], s_sem.at[planes + 2, 1], at.other
+    )
+    ret_copy.start()
+    put(ret_s, ret_all.at[0])
+    put(gate_s, gate_out)
+    finish(across_0)
+    finish(along_2)
+    start(across_2)
+    finish(z_copies[1])
+    start(along_1)
+    finish(across_2)
+    finish(along_1)
+    start(across_1)
+    put(near_a, small_out.at[0])
+    put(halo_b, small_out.at[1])
+    finish(across_1)
+    mh_copy.wait()
+    ret_copy.wait()
+    for copy in outs:
+        copy.wait()
+
+
+ANY = pl.BlockSpec(memory_space=pl.ANY)
+VM = pl.BlockSpec(memory_space=pltpu.VMEM)
+
+
+def forward_call(planes, micros, rows, operands):
+    tokens = micros * rows
+    hidden = operands[-1].shape[0]
+
+    def big(kind):
+        return jax.ShapeDtypeStruct((tokens, 1024), kind)
+
+    def hold(kind):
+        return pltpu.VMEM((tokens, 1024), kind)
+
+    square = pltpu.VMEM((1024, 1024), BF)
+    few = pltpu.VMEM((8, 1024), F32)
+    pair = pltpu.SemaphoreType.DMA
+    return pl.pallas_call(
+        functools.partial(forward_kernel, planes, micros, rows),
+        out_shape=[big(F32)] * 7
+        + [big(BF)] * 5
+        + [jax.ShapeDtypeStruct((2, 8, 1024), F32)]
+        + [jax.ShapeDtypeStruct((2, tokens, 1024), BF)] * 2
+        + [
+            jax.ShapeDtypeStruct((planes - 1, 1024, hidden), BF),
+            jax.ShapeDtypeStruct((planes - 1, hidden, 1024), BF),
+        ],
+        in_specs=[VM] * 7 + [ANY] * 7,
+        out_specs=[ANY] * 17,
+        scratch_shapes=[square] * 5
+        + [hold(F32)] * 8
+        + [hold(BF)] * 7
+        + [
+            pltpu.VMEM((tokens, 128), F32),
+            pltpu.VMEM((micros, rows, rows), BF),
+            few,
+            few,
+            few,
+            few,
+            pltpu.VMEM((2 * planes, 16, 128), F32),
+            few,
+            few,
+            few,
+            pltpu.VMEM((planes - 1, 8, 1024), F32),
+            few,
+            pair((5,)),
+            pair((18,)),
+            pair((2 * planes + 1, 2)),
+            pair((planes - 1, 7, 2)),
+            pair((planes + 3, 2)),
+        ],
+        compiler_params=pltpu.CompilerParams(
+            collective_id=0, has_side_effects=True, vmem_limit_bytes=58 << 20
+        ),
+        cost_estimate=pl.CostEstimate(
+            flops=10 * tokens * 1024 * 1024, bytes_accessed=40 << 20, transcendentals=6 * tokens * 1024
+        ),
+        name="time_mix_forward",
+    )(*operands)
+
+
+def one_micro_back(block_in, seg_ids, grad_out, kept, vectors, matrices, hidden_w, return_w):
+    lookup_start, content_start, recept, dividend, divisor_portion, block_mid, gate_two, low_key, low_value, low_recept, gated, low_gate, low_hidden, grad_ret = kept
+    (
+        gain_one,
+        bias_one,
+        decay_vec,
+        extra_array,
+        mix_key,
+        mix_value,
+        mix_recept,
+        gain_two,
+        bias_two,
+        mix_hidden,
+        mix_gate,
+    ) = vectors
+    key_w, value_w, recept_w, output_w, gate_w = matrices
+    row_count = block_in.shape[0]
+    model_width = block_in.shape[1]
+    seg_float = seg_ids.astype(jnp.float32)
+    normed_a, unit_a, inv_a = layer_norm(block_in, gain_one, bias_one)
+    prev_row, prev_seg = from_behind((normed_a[-1:], seg_float[-1:]), "mp", 1)
+    same_row = jnp.concatenate(
+        [
+            (seg_float[:1] == prev_seg).astype(jnp.float32),
+            (seg_ids[1:] == seg_ids[:-1]).astype(jnp.float32),
+        ]
+    )
+    same_col = same_row[:, None]
+    shifted_a = jnp.concatenate([prev_row, normed_a[:-1]], axis=0) * same_col
+    delta_a = normed_a - shifted_a
+    feature_fading = jnp.exp(decay_vec)
+    positions = jnp.arange(row_count, dtype=jnp.float32)[:, None]
+    rising = jnp.exp(positions * feature_fading)
+    falling = jnp.exp(-(positions - 1.0) * feature_fading)
+    falling_zero = jnp.exp(-positions * feature_fading)
+    raised_lookup = jnp.exp(lookup_start)
+    weighted_average = raised_lookup * content_start
+    order_rows = jnp.arange(row_count)
+    lower_tri = jnp.logical_and(
+        seg_ids[:, None] == seg_ids[None, :], order_rows[None, :] < order_rows[:, None]
+    ).astype(jnp.float32)
+    last_mask = (seg_ids == seg_ids[-1]).astype(jnp.float32)
+    first_mask = (seg_ids == seg_ids[0]).astype(jnp.float32) * same_row[0]
+    uniform_flag = (seg_ids[-1] == seg_ids[0]).astype(jnp.float32) * same_row[0]
+    carry_pass = uniform_flag * jnp.exp(-row_count * feature_fading)
+    zero_vec = jnp.zeros_like(feature_fading)
+    one_vec = jnp.ones_like(feature_fading)
+    extra_summand = jnp.exp(extra_array + lookup_start)
+    divisor_complete = divisor_portion + extra_summand
+    mixture_result = (dividend + extra_summand * content_start) / divisor_complete
+    normed_b, unit_b, inv_b = layer_norm(block_mid, gain_two, bias_two)
+    prev_mid = from_behind(normed_b[-1:], "mp", 1)
+    shifted_b = jnp.concatenate([prev_mid, normed_b[:-1]], axis=0) * same_col
+    delta_b = normed_b - shifted_b
+    hidden_rows = lax.all_gather(low_hidden, "mp", axis=0, tiled=True)
+    pre_act = product(hidden_rows, hidden_w)
+    rectified = jnp.maximum(pre_act, 0.0)
+    squared = reduced_precision(rectified * rectified)
+    returned = lax.psum_scatter(
+        product(squared, return_w).astype(jnp.bfloat16), "mp", scatter_dimension=0, tiled=True
+    ).astype(jnp.float32)
+    output = block_mid + gate_two * returned
+    grad_gate_pre = reduced_precision(grad_out * returned * gate_two * (1.0 - gate_two))
+    d_gate_w = (low_gate, grad_gate_pre)
+    grad_low_gate = product_nt(grad_gate_pre, gate_w)
+    grad_rows = lax.all_gather(grad_ret, "mp", axis=0, tiled=True)
+    grad_squared = product_nt(grad_rows, return_w)
+    d_return = (squared, grad_rows)
+    grad_pre = reduced_precision(grad_squared * 2.0 * rectified)
+    d_hidden = (hidden_rows, grad_pre)
+    grad_low_hidden = lax.psum_scatter(
+        product_nt(grad_pre, hidden_w).astype(jnp.bfloat16), "mp", scatter_dimension=0, tiled=True
+    ).astype(jnp.float32)
+    d_mix_hidden = jnp.sum(grad_low_hidden * delta_b, axis=0)
+    d_mix_gate = jnp.sum(grad_low_gate * delta_b, axis=0)
+    grad_shift_b = (
+        grad_low_hidden * (1.0 - mix_hidden) + grad_low_gate * (1.0 - mix_gate)
+    ) * same_col
+    from_next_b = from_behind(grad_shift_b[:1], "mp", -1)
+    grad_norm_b = (
+        grad_low_hidden * mix_hidden
+        + grad_low_gate * mix_gate
+        + jnp.concatenate([grad_shift_b[1:], from_next_b], axis=0)
+    )
+    grad_mid_norm, d_gain_two, d_bias_two = norm_back(grad_norm_b, unit_b, inv_b, gain_two)
+    grad_mid = grad_out + grad_mid_norm
+    grad_att = reduced_precision(grad_mid)
+    d_output_w = (gated, grad_att)
+    grad_gated = product_nt(grad_att, output_w)
+    grad_recept_pre = reduced_precision(grad_gated * mixture_result * recept * (1.0 - recept))
+    grad_mixed = grad_gated * recept
+    d_recept_w = (low_recept, grad_recept_pre)
+    grad_low_recept = product_nt(grad_recept_pre, recept_w)
+    dividend_adjoint = grad_mixed / divisor_complete
+    divisor_adjoint = -dividend_adjoint * mixture_result
+    extra_derivative_part = dividend_adjoint * content_start + divisor_adjoint
+    extra_derivative = jnp.sum(extra_derivative_part * extra_summand, axis=0)
+    backward_mat = jnp.concatenate([lower_tri.T, first_mask[None]], axis=0)
+    back_sum = jnp.dot(
+        backward_mat,
+        jnp.concatenate([falling * dividend_adjoint, falling * divisor_adjoint], axis=1),
+        precision=HIGH,
+    )
+    step_back = jnp.exp(-feature_fading)
+    from_num = step_back * back_sum[row_count, :model_width]
+    from_den = step_back * back_sum[row_count, model_width:]
+    out_num, out_den, out_pass = carried_in(
+        (from_num, from_den, carry_pass), "mp", suffix_join, (zero_vec, zero_vec, one_vec), True
+    )
+    tail_fall = last_mask[:, None] * jnp.exp(-(row_count - 1.0 - positions) * feature_fading)
+    cumulative_dividend = rising * back_sum[:row_count, :model_width] + tail_fall * out_num
+    running_denominator = rising * back_sum[:row_count, model_width:] + tail_fall * out_den
+    d_rate = -step_back * jnp.sum(
+        cumulative_dividend * dividend + running_denominator * divisor_portion, axis=0
+    )
+    value_gradient = reduced_precision(
+        dividend_adjoint * extra_summand + cumulative_dividend * raised_lookup
+    )
+    key_gradient = reduced_precision(
+        extra_derivative_part * extra_summand
+        + cumulative_dividend * weighted_average
+        + running_denominator * raised_lookup
+    )
+    d_key_w = (low_key, key_gradient)
+    d_value_w = (low_value, value_gradient)
+    grad_low_key = product_nt(key_gradient, key_w)
+    grad_low_value = product_nt(value_gradient, value_w)
+    d_mix_key = jnp.sum(grad_low_key * delta_a, axis=0)
+    d_mix_value = jnp.sum(grad_low_value * delta_a, axis=0)
+    d_mix_recept = jnp.sum(grad_low_recept * delta_a, axis=0)
+    grad_shift_a = (
+        grad_low_key * (1.0 - mix_key)
+        + grad_low_value * (1.0 - mix_value)
+        + grad_low_recept * (1.0 - mix_recept)
+    ) * same_col
+    from_next_a = from_behind(grad_shift_a[:1], "mp", -1)
+    grad_norm_a = (
+        grad_low_key * mix_key
+        + grad_low_value * mix_value
+        + grad_low_recept * mix_recept
+        + jnp.concatenate([grad_shift_a[1:], from_next_a], axis=0)
+    )
+    grad_in_norm, d_gain_one, d_bias_one = norm_back(grad_norm_a, unit_a, inv_a, gain_one)
+    input_grad = grad_mid + grad_in_norm
+    grads = (
+        d_gain_one,
+        d_bias_one,
+        d_rate * feature_fading,
+        extra_derivative,
+        d_mix_key,
+        d_mix_value,
+        d_mix_recept,
+        d_key_w,
+        d_value_w,
+        d_recept_w,
+        d_output_w,
+        d_gain_two,
+        d_bias_two,
+        d_mix_hidden,
+        d_mix_gate,
+        d_hidden,
+        d_return,
+        d_gate_w,
+    )
+    return (output, input_grad, grads)
 
 
 def one_micro(block_in, seg_ids, grad_out, vectors, matrices, hidden_w, return_w):
@@ -303,7 +977,7 @@
     return (output, input_grad, grads)
 
 
-def body(
+def generic_body(
     incoming_signal,
     series_number_table,
     upstream_adjoint,
@@ -417,6 +1091,142 @@
     )
 
 
+def kernel_body(
+    incoming_signal,
+    series_number_table,
+    upstream_adjoint,
+    first_scaling_factor,
+    first_scaling_offset,
+    logarithmic_fading_speeds,
+    present_step_extra,
+    lookup_shift_mixture,
+    content_shift_mixture,
+    admit_lookup_shift_mixture,
+    attention_lookup_matrix,
+    attention_content_matrix,
+    attention_admit_matrix,
+    attention_result_matrix,
+    second_scaling_factor,
+    second_scaling_offset,
+    inner_shift_mixture,
+    admit_shift_mixture,
+    feedforward_lookup_matrix,
+    feedforward_content_matrix,
+    feedforward_admit_matrix,
+):
+    hidden_full, return_full = (feedforward_lookup_matrix, feedforward_content_matrix)
+    vectors = tuple(
+        (
+            start_item.astype(jnp.float32)
+            for start_item in (
+                first_scaling_factor,
+                first_scaling_offset,
+                logarithmic_fading_speeds,
+                present_step_extra,
+                lookup_shift_mixture,
+                content_shift_mixture,
+                admit_lookup_shift_mixture,
+                second_scaling_factor,
+                second_scaling_offset,
+                inner_shift_mixture,
+                admit_shift_mixture,
+            )
+        )
+    )
+    matrices = (
+        attention_lookup_matrix,
+        attention_content_matrix,
+        attention_admit_matrix,
+        attention_result_matrix,
+        feedforward_admit_matrix,
+    )
+    micros, _, rows, depth = incoming_signal.shape
+    planes = lax.axis_size("mp") // 2
+    numbers = series_number_table[:, 0].astype(jnp.float32)
+    firsts, lasts = (numbers[:, :1], numbers[:, -1:])
+    operands = (
+        incoming_signal.reshape(micros * rows, depth),
+        jnp.pad(incoming_signal[:, 0, -1].astype(jnp.float32), ((0, 8 - micros), (0, 0))),
+        jnp.broadcast_to(numbers.reshape(-1, 1), (micros * rows, 128)),
+        jnp.pad(numbers, ((0, 8 - micros), (0, 0))),
+        jnp.broadcast_to(
+            jnp.concatenate([lasts, lasts, firsts, firsts], axis=0), (4 * micros, 128)
+        ),
+        jnp.pad(jnp.stack(vectors), ((0, 5), (0, 0))),
+        upstream_adjoint.reshape(micros * rows, depth),
+        *matrices,
+        hidden_full,
+        return_full,
+    )
+    made = forward_call(planes, micros, rows, operands)
+    kept = [part.reshape(micros, rows, depth) for part in made[:12]]
+    kept += [made[13][0].reshape(micros, rows, depth), made[14][0].reshape(micros, rows, depth)]
+    output, input_grad, grads = jax.vmap(
+        lambda rows, ids, adjoint, kept: one_micro_back(
+            rows, ids, adjoint, kept, vectors, matrices, hidden_full, return_full
+        )
+    )(
+        incoming_signal[:, 0].astype(jnp.float32),
+        series_number_table[:, 0],
+        upstream_adjoint[:, 0].astype(jnp.float32),
+        kept,
+    )
+    totals = tuple(
+        product_tn(*(side.reshape(-1, side.shape[-1]) for side in grad))
+        if isinstance(grad, tuple)
+        else jnp.sum(grad, axis=0)
+        for grad in grads
+    )
+    square = [index for index in range(18) if totals[index].shape == totals[7].shape]
+    lines = [index for index in range(18) if totals[index].ndim == 1]
+    wide = lax.psum_scatter(
+        jnp.concatenate([reduced_precision(totals[index]) for index in square], axis=1),
+        ("dp", "mp"),
+        scatter_dimension=0,
+        tiled=True,
+    ).astype(jnp.float32)
+    thin = lax.psum_scatter(
+        jnp.stack([totals[index] for index in lines], axis=1),
+        ("dp", "mp"),
+        scatter_dimension=0,
+        tiled=True,
+    )
+    held = dict(zip(square, jnp.split(wide, len(square), axis=1)))
+    held.update({index: thin[:, place] for place, index in enumerate(lines)})
+    output, input_grad = (output[:, None], input_grad[:, None])
+    owned = tuple(held[index] for index in sorted(held))
+    hidden_own, return_own = (
+        lax.psum_scatter(
+            totals[15].astype(jnp.bfloat16), "dp", scatter_dimension=0, tiled=True
+        ).astype(jnp.float32),
+        lax.psum_scatter(
+            totals[16].astype(jnp.bfloat16), "dp", scatter_dimension=1, tiled=True
+        ).astype(jnp.float32),
+    )
+    return (
+        output,
+        input_grad,
+        owned[0],
+        owned[1],
+        owned[2],
+        owned[3],
+        owned[4],
+        owned[5],
+        owned[6],
+        owned[7],
+        owned[8],
+        owned[9],
+        owned[10],
+        owned[11],
+        owned[12],
+        owned[13],
+        owned[14],
+        hidden_own,
+        return_own,
+        owned[15],
+    )
+
+
 def solution(mesh):
     placed = (
         P(None, "dp", "mp", None),
@@ -441,8 +1251,9 @@
         P("mp", None),
         P(),
     )
+    fits = mesh.shape["dp"] == 4 and mesh.shape["mp"] == 8
     return jax.shard_map(
-        body,
+        kernel_body if fits else generic_body,
         mesh=mesh,
         in_specs=placed,
         out_specs=(

time: 989 us -> 889 us (0.90)
  Pallas kernels: 0 us -> 93.4 us
  waiting for transfers between devices: 580 us -> 505 us
  blocking collectives: 118 us -> 57 us
  matrix products: 114 us -> 83.3 us
  other arithmetic: 72.8 us -> 54.4 us
    pallas_call x0 -> x1, Pallas kernels: none -> 93.4 us  [forward_call(): pl.pallas_call(functools.partial(forward_kernel, planes, micros, rows), o...]
    all_gather x8 -> x3, blocking collectives: 118 us -> 57 us  [carried_in(): everything = jax.tree.map(lambda part: lax.all_gather(part, axis), shard)]
    reduce_scatter x4, waiting for transfers between devices: 158 us -> 102 us  [the longest x1 53.8 us: one_micro_back(): lax.psum_scatter(product_nt(grad_pre, hidden_w).astype(jnp.bfloat16), 'mp...]
    dot_general x7 -> x2, matrix products: 37.2 us -> 13.9 us  [product(): return jnp.dot(left, right, preferred_element_type=jnp.float32)]
    all_gather x2, waiting for transfers between devices: 164 us -> 146 us  [the longest x1 81.3 us: one_micro_back(): hidden_rows = lax.all_gather(low_hidden, 'mp', axis=0, tiled=True)]
    select_n x16 -> x8, other arithmetic: 22.4 us -> 6.25 us  [step(): return jax.tree.map(lambda a, b: jnp.where(reached, a, b), new, before)]
    unnamed x242 -> x132, local copies, waits for them, and re-layouts: 56.4 us -> 47.2 us
  transfers between devices with their start and end apart: 13 -> 13, of which waited for: 7 -> 6; matrix products, arithmetic and copies ran while one was open for 13% -> 19% of each run, Pallas kernels for 0% -> 0%
where the time goes in v2:
time: 889 us; the launch traced here: 880 us
  waiting for transfers between devices  505 us (57%)
  Pallas kernels  93.4 us (11%)
  matrix products  83.3 us (9%)
  local copies, waits for them, and re-layouts  61.9 us (7%)
  blocking collectives  57 us (6%)
  other arithmetic  54.4 us (6%)
  between operations  15.2 us (2%)
  starting transfers between devices  9.73 us (1%)
    unnamed x10, waiting for transfers between devices  258 us
    pallas_call x1, Pallas kernels, forward_call(): pl.pallas_call(functools.partial(forward_kernel, planes, micros, rows), o...  93.4 us
    all_gather x1, waiting for transfers between devices, one_micro_back(): hidden_rows = lax.all_gather(low_hidden, 'mp', axis=0, tiled=True)  81.3 us
    all_gather x1, waiting for transfers between devices, one_micro_back(): grad_rows = lax.all_gather(grad_ret, 'mp', axis=0, tiled=True)  64.6 us
    all_gather x3, blocking collectives, carried_in(): everything = jax.tree.map(lambda part: lax.all_gather(part, axis), shard)  57 us
    reduce_scatter x1, waiting for transfers between devices, one_micro_back(): lax.psum_scatter(product_nt(grad_pre, hidden_w).astype(jnp.bfloat16), 'mp...  53.8 us
    reduce_scatter x1, waiting for transfers between devices, one_micro_back(): lax.psum_scatter(product(squared, return_w).astype(jnp.bfloat16), 'mp', s...  47.8 us
    unnamed x132, local copies, waits for them, and re-layouts  47.2 us
  transfers between devices with their start and end apart: 13, of which 6 were waited for; matrix products, arithmetic and copies ran while one was open for 19% of the time, Pallas kernels for 0%

profile of v2, /device:TPU:0, one launch (start us, length us, event | category | flops | bytes accessed | tf_op | source)
XLA Modules:
  0.0 880.4 jit_solution(14728534623673740405)
XLA Ops:
  8.0 2.3 collective-permute-start
  21.5 2.0 select_reduce_fusion
  25.1 93.4 %time_mix_forward.1 = (f32[512,1024]{1,0:T(8,128)}, f32[512,1024]{1,0:T(8,128)}, f32[512,1024]{1,0:T(8,128)}, f32[512,1024]{1,0:T(8,128)}, f32[512,1024]{1,0:T(8...) custom-call(bf16[512,1024]{1,0:T(8,128)(2,1)} %bitcast.247, ...), custom_call_target="tpu_custom_call" | custom-call | flops 5368709120 | bytes 41943040 | tf_op jit(solution)/shard_map/time_mix_forward/pallas_call | solution.py:554
  118.6 2.4 slice.107
  122.2 81.3 %all-gather.3.cloned.1.call-done = bf16[4,1024,1024]{2,1,0:T(8,128)(2,1)} async-done(((bf16[4,128,1024]{2,1,0:T(8,128)(2,1)}), bf16[4,1024,1024]{2,1,0:T(8,128)(2,1)}) %all-gather.3.cloned.1.call-update) | async-done | bytes 8388624 | tf_op jit(solution)/shard_map/vmap()/all_gather | solution.py:652
  203.5 7.0 fusion.50
  210.6 4.0 copy-done.11
  214.5 6.8 convolution_convert_fusion.1
  221.7 64.6 %all-gather.5.cloned.1.call-done = bf16[4,1024,1024]{2,1,0:T(8,128)(2,1)} async-done(((bf16[4,128,1024]{2,1,0:T(8,128)(2,1)}), bf16[4,1024,1024]{2,1,0:T(8,128)(2,1)}) %all-gather.5.cloned.1.call-update) | async-done | bytes 8388624 | tf_op jit(solution)/shard_map/vmap()/all_gather | solution.py:663
  286.3 9.5 %multiply_convert_fusion = bf16[4,1024,512]{2,1,0:T(8,128)(2,1)S(1)} fusion(f32[4,1024,512]{2,1,0:T(8,128)} %copy-done.11, bf16[4,1024,1024]{2,1,0:T(8,128)(2,1)} %all-gather.5.cloned.1.call-done, bf16[512,1024]{1,0:T(8,128)(2,1)S(1)} %copy-done.48), kind=kOutput, calls=%fused_computation.7 | convolution fusion | flops 4303355904 | bytes 22020096 | tf_op jit(solution)/shard_map/vmap()/dot_general | solution.py:53
  295.8 1.9 copy-done.50
  297.7 7.2 convolution_convert_fusion
  309.2 2.1 collective-permute-start.3
  317.6 11.3 %bitcast_convert_fusion = bf16[512,1024]{1,0:T(8,128)(2,1)} fusion(bf16[4,1024,1024]{2,1,0:T(8,128)(2,1)} %all-gather.5.cloned.1.call-done, f32[4,1024,512]{2,1,0:T(8,128)} %copy-done.11), kind=kOutput, calls=%fused_computation.59 | convolution fusion | flops 4301783040 | bytes 17825792 | tf_op jit(solution)/shard_map/dot_general | solution.py:47
  329.0 47.8 %reduce-scatter.11.cloned.1.call-done = bf16[4,128,1024]{2,1,0:T(8,128)(2,1)} async-done(((bf16[4,1024,1024]{2,1,0:T(8,128)(2,1)}), bf16[4,128,1024]{2,1,0:T(8,128)(2,1)}) %reduce-scatter.11.cloned.1.call-update) | async-done | bytes 1048592 | tf_op jit(solution)/shard_map/vmap()/reduce_scatter | solution.py:656
  376.8 4.7 fusion.26
  383.4 1.9 collective-permute-start.4
  385.3 29.1 %all_gather.21 = f32[4,8,1024]{2,0,1:T(4,128)} all-gather(f32[4,1,1024]{2,0,1:T(4,128)S(1)} %broadcast_multiply_fusion.2), channel_id=1, replica_groups=mesh['dp'=4,'mp'=8] {'mp'}, dimensions={1}, use_global_device_ids=true | all-gather | bytes 147456 | tf_op jit(solution)/shard_map/vmap()/all_gather | solution.py:22
  414.4 53.8 %reduce-scatter.13.cloned.1.call-done = bf16[4,128,1024]{2,1,0:T(8,128)(2,1)} async-done(((bf16[4,1024,1024]{2,1,0:T(8,128)(2,1)}), bf16[4,128,1024]{2,1,0:T(8,128)(2,1)}) %reduce-scatter.13.cloned.1.call-update) | async-done | bytes 1048592 | tf_op jit(solution)/shard_map/vmap()/reduce_scatter | solution.py:668
  468.2 7.2 multiply_reduce_fusion
  478.7 8.2 bitcast_convert_fusion.1
  486.9 2.0 slice.181
  489.4 2.2 multiply_reduce_fusion.1
  493.1 1.5 copy-done.17
  495.9 3.2 fusion.55
  499.1 2.6 broadcast_multiply_fusion.1
  501.7 4.2 fusion.3
  506.0 2.0 copy-done.4
  508.1 14.0 %all_gather.22 = f32[4,8,1024]{2,0,1:T(4,128)S(1)} all-gather(f32[4,1,1024]{2,0,1:T(4,128)S(1)} %get-tuple-element.471), channel_id=1, replica_groups=mesh['dp'=4,'mp'=8] {'mp'}, dimensions={1}, use_global_device_ids=true | all-gather | bytes 147456 | tf_op jit(solution)/shard_map/vmap()/all_gather | solution.py:22
  522.0 13.9 %all_gather.20 = f32[4,8,1024]{2,0,1:T(4,128)S(1)} all-gather(f32[4,1,1024]{2,0,1:T(4,128)S(1)} %get-tuple-element.472), channel_id=1, replica_groups=mesh['dp'=4,'mp'=8] {'mp'}, dimensions={1}, use_global_device_ids=true | all-gather | bytes 147456 | tf_op jit(solution)/shard_map/vmap()/all_gather | solution.py:22
  536.0 7.0 while.21
  543.0 7.6 add_convert_fusion
  554.2 1.4 add_multiply_fusion
  555.6 1.5 collective-permute-start.2
  557.2 2.6 convert_dynamic-update-slice_fusion.4
  559.8 2.6 convert_dynamic-update-slice_fusion.3
  562.4 2.6 convert_dynamic-update-slice_fusion.2
  565.0 2.6 convert_dynamic-update-slice_fusion.1
  569.3 3.8 fusion.21
  574.4 4.2 convert_dynamic-update-slice_fusion
  578.5 13.8 %copy.127 = bf16[1024,5120]{1,0:T(8,128)(2,1)} copy(bf16[1024,5120]{0,1:T(8,128)(2,1)} %convert_dynamic-update-slice_fusion) | data formatting | bytes 20971520
  592.3 1.8 convert_element_type.196
  594.1 1.8 convert_element_type.194
  595.9 4.2 fusion.20
  600.1 108.7 %reduce-scatter.19.cloned.1.call-done = f32[32,11]{1,0:T(8,128)} async-done(((f32[1024,11]{1,0:T(8,128)}), f32[32,11]{1,0:T(8,128)}) %reduce-scatter.19.cloned.1.call-update) | async-done | bytes 1424
  716.5 148.9 %reduce-scatter.21.cloned.1.call-done = bf16[32,5120]{1,0:T(8,128)(2,1)} async-done(((bf16[1024,5120]{1,0:T(8,128)(2,1)}), bf16[32,5120]{1,0:T(8,128)(2,1)}) %reduce-scatter.21.cloned.1.call-update) | async-done | bytes 327696
  865.4 1.6 copy.128
  868.0 1.9 copy.122
  (233 shorter events, 59.2 us)
Async XLA Ops:
  7.2 196.3 %all-gather.3.cloned.1.call-start = ((), (), s32[]{:S(2)}) async-start(), calls=%async_computation.6 | async-start | bytes 9437184 | tf_op jit(solution)/shard_map/vmap()/all_gather | solution.py:652
  8.0 13.5 %collective-permute-start = (f32[4,1]{1,0:T(4,128)S(1)}, f32[4,1]{1,0:T(4,128)S(1)}, u32[]{:S(2)}, u32[]{:S(2)}) collective-permute-start(f32[4,1]{1,0:T(4,128)S(1)} %slice.105), channel_id=1, source_target_pairs={{0,1},{1,2},{2,3},{3,4},{4,5},{5,6},{6,7},{8,9},{9,10},{10,11},{11... | collective-permute-start | bytes 56 | tf_op jit(solution)/shard_map/vmap()/ppermute | solution.py:17
  121.0 82.5 %copy-start.49 = (bf16[1024,512]{1,0:T(8,128)(2,1)S(1)}, bf16[1024,512]{1,0:T(8,128)(2,1)}, u32[]{:S(2)}) copy-start(bf16[1024,512]{1,0:T(8,128)(2,1)} %w1_ref.1) | copy-start | bytes 3145732
  121.0 165.3 %all-gather.5.cloned.1.call-start = ((), (), s32[]{:S(2)}) async-start(), calls=%async_computation.8 | async-start | bytes 9437184 | tf_op jit(solution)/shard_map/vmap()/all_gather | solution.py:663
  122.2 92.4 %copy-start.48 = (bf16[512,1024]{1,0:T(8,128)(2,1)S(1)}, bf16[512,1024]{1,0:T(8,128)(2,1)}, u32[]{:S(2)}) copy-start(bf16[512,1024]{1,0:T(8,128)(2,1)} %w2_ref.1) | copy-start | bytes 3145732
  122.2 254.6 %reduce-scatter.11.cloned.1.call-start = ((), (), s32[]{:S(2)}) async-start(), calls=%async_computation.7 | async-start | bytes 9437184 | tf_op jit(solution)/shard_map/vmap()/reduce_scatter | solution.py:656
  210.5 4.0 copy-start.11
  221.4 246.8 %reduce-scatter.13.cloned.1.call-start = ((), (), s32[]{:S(2)}) async-start(), calls=%async_computation.9 | async-start | bytes 9437184 | tf_op jit(solution)/shard_map/vmap()/reduce_scatter | solution.py:668
  304.9 287.4 %reduce-scatter.17.cloned.1.call-start = ((), (), s32[]{:S(2)}) async-start(), calls=%async_computation.11 | async-start | bytes 1310720 | tf_op jit(solution)/shard_map/reduce_scatter | solution.py:1202
  306.3 5.1 copy-start.25
  306.3 6.4 copy-start.35
  306.3 6.4 copy-start.37
  306.3 6.4 copy-start.38
  306.4 6.4 copy-start.39
  306.4 6.4 copy-start.40
  306.4 7.0 copy-start.36
  306.8 8.6 copy-start
  309.2 259.0 %collective-permute-start.3 = (f32[4,1,1024]{2,1,0:T(1,128)}, f32[4,1,1024]{2,1,0:T(1,128)S(1)}, u32[]{:S(2)}, u32[]{:S(2)}) collective-permute-start(f32[4,1,1024]{2,1,0:T(1,128)} %slice.189), channel_id=1, source_target_pairs={{0,1},{1,2},{2,3},{3,4},{4,5},{5,6},{6,7},{8,9},{9,10},{10,11},{11... | collective-permute-start | bytes 49160 | tf_op jit(solution)/shard_map/vmap()/ppermute | solution.py:17
  328.9 265.2 %reduce-scatter.15.cloned.1.call-start = ((), (), s32[]{:S(2)}) async-start(), calls=%async_computation.10 | async-start | bytes 1310720 | tf_op jit(solution)/shard_map/reduce_scatter | solution.py:1199
  376.8 91.4 %copy-start.29 = (f32[1024]{0:T(1024)S(1)}, f32[1024]{0:T(1024)}, u32[]{:S(2)}) copy-start(f32[1024]{0:T(1024)} %get-tuple-element.484) | copy-start | bytes 12292
  383.4 84.7 %collective-permute-start.4 = (f32[4,1,1024]{2,1,0:T(1,128)}, f32[4,1,1024]{2,1,0:T(1,128)}, u32[]{:S(2)}, u32[]{:S(2)}) collective-permute-start(f32[4,1,1024]{2,1,0:T(1,128)} %slice.191), channel_id=1, source_target_pairs={{0,1},{1,2},{2,3},{3,4},{4,5},{5,6},{6,7},{8,9},{9,10},{10,11},{11... | collective-permute-start | bytes 49160 | tf_op jit(solution)/shard_map/vmap()/ppermute | solution.py:17
  468.2 10.5 %copy-start.51 = (bf16[4,1024,512]{2,1,0:T(8,128)(2,1)S(1)}, bf16[4,1024,512]{2,1,0:T(8,128)(2,1)}, u32[]{:S(2)}) copy-start(bf16[4,1024,512]{2,1,0:T(8,128)(2,1)} %copy-done.50) | copy-start | bytes 12582916
  477.4 11.6 %collective-permute-start.1 = (f32[4,1,1024]{2,1,0:T(1,128)}, f32[4,1,1024]{2,1,0:T(1,128)S(1)}, u32[]{:S(2)}, u32[]{:S(2)}) collective-permute-start(f32[4,1,1024]{2,1,0:T(1,128)} %slice.182), channel_id=1, source_target_pairs={{1,0},{2,1},{3,2},{4,3},{5,4},{6,5},{7,6},{9,8},{10,9},{11,10},{12... | collective-permute-start | bytes 49160 | tf_op jit(solution)/shard_map/vmap()/ppermute | solution.py:17
  486.9 222.0 %reduce-scatter.19.cloned.1.call-start = ((), (), s32[]{:S(2)}) async-start(), calls=%async_computation.12 | async-start | bytes 540672
  489.4 3.6 copy-start.20
  489.4 3.6 copy-start.21
  489.4 3.7 copy-start.45
  491.6 2.9 copy-start.17
  491.6 3.6 copy-start.18
  491.6 4.2 copy-start.19
  493.0 6.1 copy-start.22
  495.9 3.3 copy-start.15
  499.1 2.6 copy-start.9
  499.1 2.6 copy-start.10
  499.1 2.6 copy-start.34
  501.7 6.3 copy-start.31
  501.7 41.3 %copy-start.33 = (f32[4,128]{1,0:T(4,128)S(1)}, f32[4,128]{1,0:T(4,128)}, u32[]{:S(2)}) copy-start(f32[4,128]{1,0:T(4,128)} %compare_convert_fusion) | copy-start | bytes 6148
  543.0 7.6 copy-start.46
  554.2 3.0 copy-start.55
  555.6 12.5 %collective-permute-start.2 = (f32[4,1,1024]{2,1,0:T(1,128)S(1)}, f32[4,1,1024]{2,1,0:T(1,128)S(1)}, u32[]{:S(2)}, u32[]{:S(2)}) collective-permute-start(f32[4,1,1024]{2,1,0:T(1,128)S(1)} %slice.188), channel_id=1, source_target_pairs={{1,0},{2,1},{3,2},{4,3},{5,4},{6,5},{7,6},{9,8},{10,9},{11,10},{12... | collective-permute-start | bytes 49160 | tf_op jit(solution)/shard_map/vmap()/ppermute | solution.py:17
  557.1 2.6 copy-start.54
  559.8 2.6 copy-start.53
  565.0 2.7 copy-start.30
  569.3 3.8 copy-start.26
  569.3 3.8 copy-start.27
  569.3 3.8 copy-start.28
  569.3 3.8 copy-start.41
  574.3 291.1 %reduce-scatter.21.cloned.1.call-start = ((), (), s32[]{:S(2)}) async-start(), calls=%async_computation.13 | async-start | bytes 10813440
  (21 other events, 38.0 us)
Sparse Core Ops, SparseCore 0:
  121.2 82.2 all-gather.2
  205.7 80.5 all-gather.4
  288.6 88.1 reduce-scatter.10
  378.9 89.1 reduce-scatter.12
  470.9 26.2 reduce-scatter.16
  500.2 27.7 reduce-scatter.14
  574.4 134.3 reduce-scatter.18
  711.2 154.1 reduce-scatter.20

commit v3 on v2

--- a/solution.py
+++ b/solution.py
@@ -191,7 +191,10 @@
     mr_out,
     gated_out,
     mg_out,
-    small_out,
+    da_out,
+    db_out,
+    keep_out,
+    segs_out,
     mh_all,
     ret_all,
     w1_all,
@@ -209,6 +212,7 @@
     mid_s,
     gate_s,
     xb_s,
+    da_s,
     mk_s,
     mv_s,
     mr_s,
@@ -304,6 +308,7 @@
                 keep_s[span, :], 1024
             )
             delta = normed - shifted
+            da_s[span, :] = delta
             mk_s[span, :] = (shifted + delta * vec_ref[4:5, :]).astype(BF)
             mv_s[span, :] = (shifted + delta * vec_ref[5:6, :]).astype(BF)
             mr_s[span, :] = (shifted + delta * vec_ref[6:7, :]).astype(BF)
@@ -318,6 +323,9 @@
         copy.start()
         outs.append(copy)
 
+    put(da_s, da_out)
+    put(keep_s, keep_out)
+    put(segs_s, segs_out)
     put(mk_s, mk_out)
     put(mv_s, mv_out)
     put(mr_s, mr_out)
@@ -490,6 +498,7 @@
                 keep_s[span, :], 1024
             )
             delta = normed - shifted
+            xb_s[span, :] = delta
             mh_s[span, :] = (shifted + delta * vec_ref[9:10, :]).astype(BF)
             mg_s[span, :] = (shifted + delta * vec_ref[10:11, :]).astype(BF)
             return normed[block - 1 : block, :]
@@ -502,6 +511,7 @@
     mh_copy.start()
     put(mh_s, mh_all.at[0])
     put(mg_s, mg_out)
+    put(xb_s, db_out)
     loads[4].wait()
 
     @pl.loop(0, 2)
@@ -525,8 +535,6 @@
     finish(across_2)
     finish(along_1)
     start(across_1)
-    put(near_a, small_out.at[0])
-    put(halo_b, small_out.at[1])
     finish(across_1)
     mh_copy.wait()
     ret_copy.wait()
@@ -555,16 +563,20 @@
         functools.partial(forward_kernel, planes, micros, rows),
         out_shape=[big(F32)] * 7
         + [big(BF)] * 5
-        + [jax.ShapeDtypeStruct((2, 8, 1024), F32)]
+        + [big(F32)] * 2
+        + [
+            jax.ShapeDtypeStruct((tokens, 128), F32),
+            jax.ShapeDtypeStruct((2 * planes, 16, 128), F32),
+        ]
         + [jax.ShapeDtypeStruct((2, tokens, 1024), BF)] * 2
         + [
             jax.ShapeDtypeStruct((planes - 1, 1024, hidden), BF),
             jax.ShapeDtypeStruct((planes - 1, hidden, 1024), BF),
         ],
         in_specs=[VM] * 7 + [ANY] * 7,
-        out_specs=[ANY] * 17,
+        out_specs=[ANY] * 20,
         scratch_shapes=[square] * 5
-        + [hold(F32)] * 8
+        + [hold(F32)] * 9
         + [hold(BF)] * 7
         + [
             pltpu.VMEM((tokens, 128), F32),
@@ -580,7 +592,7 @@
             pltpu.VMEM((planes - 1, 8, 1024), F32),
             few,
             pair((5,)),
-            pair((18,)),
+            pair((20,)),
             pair((2 * planes + 1, 2)),
             pair((planes - 1, 7, 2)),
             pair((planes + 3, 2)),
@@ -595,171 +607,852 @@
     )(*operands)
 
 
-def one_micro_back(block_in, seg_ids, grad_out, kept, vectors, matrices, hidden_w, return_w):
-    lookup_start, content_start, recept, dividend, divisor_portion, block_mid, gate_two, low_key, low_value, low_recept, gated, low_gate, low_hidden, grad_ret = kept
-    (
-        gain_one,
-        bias_one,
-        decay_vec,
-        extra_array,
-        mix_key,
-        mix_value,
-        mix_recept,
-        gain_two,
-        bias_two,
-        mix_hidden,
-        mix_gate,
-    ) = vectors
-    key_w, value_w, recept_w, output_w, gate_w = matrices
-    row_count = block_in.shape[0]
-    model_width = block_in.shape[1]
-    seg_float = seg_ids.astype(jnp.float32)
-    normed_a, unit_a, inv_a = layer_norm(block_in, gain_one, bias_one)
-    prev_row, prev_seg = from_behind((normed_a[-1:], seg_float[-1:]), "mp", 1)
-    same_row = jnp.concatenate(
-        [
-            (seg_float[:1] == prev_seg).astype(jnp.float32),
-            (seg_ids[1:] == seg_ids[:-1]).astype(jnp.float32),
+class Reduce:
+    def __init__(self, at, parts, first, second, far, sems, slot, x_first):
+        self.at, self.parts, self.slot = (at, parts, slot)
+        side = lax.rem(at.dp, 2)
+        line = lax.div(at.dp, 2)
+        self.one, self.two = (side, line) if x_first else (line, side)
+        near, next_to = (at.side_x, at.side_y) if x_first else (at.side_y, at.side_x)
+        self.first, self.second, self.far = (first, second, far)
+        self.copy_1 = remote(parts.at[1 - self.one], first, sems.at[0, 0], sems.at[0, 1], near)
+        self.copy_2 = remote(
+            parts.at[self.one, 1 - self.two], second, sems.at[1, 0], sems.at[1, 1], next_to
+        )
+        if slot:
+            self.copy_3 = remote(
+                parts.at[self.one, self.two], far, sems.at[2, 0], sems.at[2, 1], at.plane(slot)
+            )
+
+    def start(self):
+        self.copy_1.start()
+
+    def add(self, half, other):
+        mine = self.parts.at[self.one, half]
+
+        @pl.loop(0, mine.shape[0] // 64)
+        def _(i):
+            span = tile(i, 64)
+            mine[span, :] = (mine[span, :].astype(F32) + other[span, :].astype(F32)).astype(BF)
+
+    def middle(self):
+        self.copy_1.wait()
+        self.add(1 - self.two, self.first.at[1 - self.two])
+        self.copy_2.start()
+        self.add(self.two, self.first.at[self.two])
+
+    def last(self):
+        self.copy_2.wait()
+        self.add(self.two, self.second)
+        if self.slot:
+            self.copy_3.start()
+
+    def close(self):
+        if self.slot:
+            self.copy_3.wait()
+
+
+def sum_rows(into, index, values):
+    total = values[0:8]
+    for start in range(8, values.shape[0], 8):
+        total = total + values[start : start + 8]
+    into[index] = into[index] + total
+
+
+def norm_back_rows(grad, unit, inverse, gain):
+    scaled = grad * gain
+    return inverse * (
+        scaled
+        - jnp.mean(scaled, axis=-1, keepdims=True)
+        - unit * jnp.mean(scaled * unit, axis=-1, keepdims=True)
+    )
+
+
+def middle_kernel(
+    planes,
+    micros,
+    rows,
+    vec_ref,
+    keep_ref,
+    segs_ref,
+    segcol_ref,
+    segrow_ref,
+    w1_ref,
+    w2_ref,
+    w1_all,
+    w2_all,
+    mh_all,
+    ret_all,
+    mid_ref,
+    gate_ref,
+    adj_ref,
+    db_ref,
+    k_ref,
+    v_ref,
+    r_ref,
+    num_ref,
+    den_ref,
+    gate_w,
+    output_w,
+    out_ref,
+    gmid_out,
+    ggp_out,
+    gatt_out,
+    grp_out,
+    gk_out,
+    gv_out,
+    sums_out,
+    own1_out,
+    own2_out,
+    parts1,
+    parts2,
+    first1,
+    first2,
+    second1,
+    second2,
+    far1,
+    far2,
+    ret_acc,
+    gmh_acc,
+    ret_send,
+    gmh_send,
+    ret_recv,
+    gmh_recv,
+    mid_s,
+    gate_s,
+    adj_s,
+    db_s,
+    sums_s,
+    sums_flat,
+    mask_s,
+    pay_b,
+    halo_b,
+    state_own,
+    state_other,
+    state_chip,
+    state_in,
+    carry_s,
+    own1_s,
+    own2_s,
+    load_sem,
+    out_sem,
+    rs_sem,
+    s_sem,
+):
+    at = Place(planes)
+    dp, mp, z, core = (at.dp, at.mp, at.z, at.core)
+    tokens = micros * rows
+    hidden = w1_ref.shape[1]
+    outs = []
+
+    def put(source, target):
+        copy = pltpu.make_async_copy(source, target, out_sem.at[len(outs)])
+        copy.start()
+        outs.append(copy)
+
+    loaded = []
+
+    def load(source, target):
+        copy = pltpu.make_async_copy(source, target, load_sem.at[len(loaded)])
+        copy.start()
+        loaded.append(copy)
+        return copy
+
+    greet(
+        [at.other, at.side_x, at.side_y]
+        + [at.plane(step) for step in range(1, planes)]
+        + [at.ahead(1), at.ahead(-1)]
+    )
+    reduces = []
+    for slot in range(planes):
+        reduces.append(
+            (
+                Reduce(at, parts1.at[slot], first1.at[slot], second1.at[slot],
+                       far1.at[max(slot - 1, 0)], rs_sem.at[slot, 0], slot, True),
+                Reduce(at, parts2.at[slot], first2.at[slot], second2.at[slot],
+                       far2.at[max(slot - 1, 0)], rs_sem.at[slot, 1], slot, False),
+            )
+        )
+    ret_copy = remote(ret_send, ret_recv, s_sem.at[0, 0], s_sem.at[0, 1], at.other)
+    gmh_copy = remote(gmh_send, gmh_recv, s_sem.at[1, 0], s_sem.at[1, 1], at.other)
+
+    def feed_forward(w1, w2, mh2, gr2, sq_s, gp_s):
+        slots = []
+        mh_load = [load(mh_all.at[0], mh2.at[0:tokens]), load(ret_all.at[0], gr2.at[0:tokens])]
+        slots.append((load(w1_ref, w1.at[0]), load(w2_ref, w2.at[0])))
+        mh_load += [
+            load(mh_all.at[1], mh2.at[tokens : 2 * tokens]),
+            load(ret_all.at[1], gr2.at[tokens : 2 * tokens]),
         ]
-    )
-    same_col = same_row[:, None]
-    shifted_a = jnp.concatenate([prev_row, normed_a[:-1]], axis=0) * same_col
-    delta_a = normed_a - shifted_a
-    feature_fading = jnp.exp(decay_vec)
-    positions = jnp.arange(row_count, dtype=jnp.float32)[:, None]
-    rising = jnp.exp(positions * feature_fading)
-    falling = jnp.exp(-(positions - 1.0) * feature_fading)
-    falling_zero = jnp.exp(-positions * feature_fading)
-    raised_lookup = jnp.exp(lookup_start)
-    weighted_average = raised_lookup * content_start
-    order_rows = jnp.arange(row_count)
-    lower_tri = jnp.logical_and(
-        seg_ids[:, None] == seg_ids[None, :], order_rows[None, :] < order_rows[:, None]
-    ).astype(jnp.float32)
-    last_mask = (seg_ids == seg_ids[-1]).astype(jnp.float32)
-    first_mask = (seg_ids == seg_ids[0]).astype(jnp.float32) * same_row[0]
-    uniform_flag = (seg_ids[-1] == seg_ids[0]).astype(jnp.float32) * same_row[0]
-    carry_pass = uniform_flag * jnp.exp(-row_count * feature_fading)
-    zero_vec = jnp.zeros_like(feature_fading)
-    one_vec = jnp.ones_like(feature_fading)
-    extra_summand = jnp.exp(extra_array + lookup_start)
-    divisor_complete = divisor_portion + extra_summand
-    mixture_result = (dividend + extra_summand * content_start) / divisor_complete
-    normed_b, unit_b, inv_b = layer_norm(block_mid, gain_two, bias_two)
-    prev_mid = from_behind(normed_b[-1:], "mp", 1)
-    shifted_b = jnp.concatenate([prev_mid, normed_b[:-1]], axis=0) * same_col
-    delta_b = normed_b - shifted_b
-    hidden_rows = lax.all_gather(low_hidden, "mp", axis=0, tiled=True)
-    pre_act = product(hidden_rows, hidden_w)
-    rectified = jnp.maximum(pre_act, 0.0)
-    squared = reduced_precision(rectified * rectified)
-    returned = lax.psum_scatter(
-        product(squared, return_w).astype(jnp.bfloat16), "mp", scatter_dimension=0, tiled=True
-    ).astype(jnp.float32)
-    output = block_mid + gate_two * returned
-    grad_gate_pre = reduced_precision(grad_out * returned * gate_two * (1.0 - gate_two))
-    d_gate_w = (low_gate, grad_gate_pre)
-    grad_low_gate = product_nt(grad_gate_pre, gate_w)
-    grad_rows = lax.all_gather(grad_ret, "mp", axis=0, tiled=True)
-    grad_squared = product_nt(grad_rows, return_w)
-    d_return = (squared, grad_rows)
-    grad_pre = reduced_precision(grad_squared * 2.0 * rectified)
-    d_hidden = (hidden_rows, grad_pre)
-    grad_low_hidden = lax.psum_scatter(
-        product_nt(grad_pre, hidden_w).astype(jnp.bfloat16), "mp", scatter_dimension=0, tiled=True
-    ).astype(jnp.float32)
-    d_mix_hidden = jnp.sum(grad_low_hidden * delta_b, axis=0)
-    d_mix_gate = jnp.sum(grad_low_gate * delta_b, axis=0)
-    grad_shift_b = (
-        grad_low_hidden * (1.0 - mix_hidden) + grad_low_gate * (1.0 - mix_gate)
-    ) * same_col
-    from_next_b = from_behind(grad_shift_b[:1], "mp", -1)
-    grad_norm_b = (
-        grad_low_hidden * mix_hidden
-        + grad_low_gate * mix_gate
-        + jnp.concatenate([grad_shift_b[1:], from_next_b], axis=0)
-    )
-    grad_mid_norm, d_gain_two, d_bias_two = norm_back(grad_norm_b, unit_b, inv_b, gain_two)
-    grad_mid = grad_out + grad_mid_norm
-    grad_att = reduced_precision(grad_mid)
-    d_output_w = (gated, grad_att)
-    grad_gated = product_nt(grad_att, output_w)
-    grad_recept_pre = reduced_precision(grad_gated * mixture_result * recept * (1.0 - recept))
-    grad_mixed = grad_gated * recept
-    d_recept_w = (low_recept, grad_recept_pre)
-    grad_low_recept = product_nt(grad_recept_pre, recept_w)
-    dividend_adjoint = grad_mixed / divisor_complete
-    divisor_adjoint = -dividend_adjoint * mixture_result
-    extra_derivative_part = dividend_adjoint * content_start + divisor_adjoint
-    extra_derivative = jnp.sum(extra_derivative_part * extra_summand, axis=0)
-    backward_mat = jnp.concatenate([lower_tri.T, first_mask[None]], axis=0)
-    back_sum = jnp.dot(
-        backward_mat,
-        jnp.concatenate([falling * dividend_adjoint, falling * divisor_adjoint], axis=1),
-        precision=HIGH,
-    )
-    step_back = jnp.exp(-feature_fading)
-    from_num = step_back * back_sum[row_count, :model_width]
-    from_den = step_back * back_sum[row_count, model_width:]
-    out_num, out_den, out_pass = carried_in(
-        (from_num, from_den, carry_pass), "mp", suffix_join, (zero_vec, zero_vec, one_vec), True
-    )
-    tail_fall = last_mask[:, None] * jnp.exp(-(row_count - 1.0 - positions) * feature_fading)
-    cumulative_dividend = rising * back_sum[:row_count, :model_width] + tail_fall * out_num
-    running_denominator = rising * back_sum[:row_count, model_width:] + tail_fall * out_den
-    d_rate = -step_back * jnp.sum(
-        cumulative_dividend * dividend + running_denominator * divisor_portion, axis=0
-    )
-    value_gradient = reduced_precision(
-        dividend_adjoint * extra_summand + cumulative_dividend * raised_lookup
-    )
-    key_gradient = reduced_precision(
-        extra_derivative_part * extra_summand
-        + cumulative_dividend * weighted_average
-        + running_denominator * raised_lookup
-    )
-    d_key_w = (low_key, key_gradient)
-    d_value_w = (low_value, value_gradient)
-    grad_low_key = product_nt(key_gradient, key_w)
-    grad_low_value = product_nt(value_gradient, value_w)
-    d_mix_key = jnp.sum(grad_low_key * delta_a, axis=0)
-    d_mix_value = jnp.sum(grad_low_value * delta_a, axis=0)
-    d_mix_recept = jnp.sum(grad_low_recept * delta_a, axis=0)
-    grad_shift_a = (
-        grad_low_key * (1.0 - mix_key)
-        + grad_low_value * (1.0 - mix_value)
-        + grad_low_recept * (1.0 - mix_recept)
-    ) * same_col
-    from_next_a = from_behind(grad_shift_a[:1], "mp", -1)
-    grad_norm_a = (
-        grad_low_key * mix_key
-        + grad_low_value * mix_value
-        + grad_low_recept * mix_recept
-        + jnp.concatenate([grad_shift_a[1:], from_next_a], axis=0)
-    )
-    grad_in_norm, d_gain_one, d_bias_one = norm_back(grad_norm_a, unit_a, inv_a, gain_one)
-    input_grad = grad_mid + grad_in_norm
-    grads = (
-        d_gain_one,
-        d_bias_one,
-        d_rate * feature_fading,
-        extra_derivative,
-        d_mix_key,
-        d_mix_value,
-        d_mix_recept,
-        d_key_w,
-        d_value_w,
-        d_recept_w,
-        d_output_w,
-        d_gain_two,
-        d_bias_two,
-        d_mix_hidden,
-        d_mix_gate,
-        d_hidden,
-        d_return,
-        d_gate_w,
-    )
-    return (output, input_grad, grads)
+        for slot in range(1, planes):
+            slots.append(
+                (load(w1_all.at[slot - 1], w1.at[slot]), load(w2_all.at[slot - 1], w2.at[slot]))
+            )
+        late = [load(mid_ref, mid_s), load(gate_ref, gate_s), load(adj_ref, adj_s), load(db_ref, db_s)]
+        for copy in mh_load:
+            copy.wait()
+        for slot in range(planes):
+            for copy in slots[slot]:
+                copy.wait()
+
+            def rows_of(i, slot=slot):
+                span = tile(i, 256)
+                pre = dot(mh2[span, :], w1[slot])
+                rectified = jnp.maximum(pre, 0.0)
+                squared = (rectified * rectified).astype(BF)
+                sq_s[span, :] = squared
+                grad_squared = dot(gr2[span, :], w2[slot], NT)
+                grad_pre = (grad_squared * 2.0 * rectified).astype(BF)
+                gp_s[span, :] = grad_pre
+                if slot == 0:
+                    ret_acc[span, :] = dot(squared, w2[slot])
+                    gmh_acc[span, :] = dot(grad_pre, w1[slot], NT)
+                else:
+                    ret_acc[span, :] += dot(squared, w2[slot])
+                    gmh_acc[span, :] += dot(grad_pre, w1[slot], NT)
+
+            half = tokens // 256
+            pl.loop(half, 2 * half)(rows_of)
+            if slot == planes - 1:
+
+                @pl.loop(0, tokens // 64)
+                def _(i):
+                    span = tile(i, 64)
+                    far_span = tile(tokens // 64 + i, 64)
+                    ret_send[span, :] = ret_acc[far_span, :].astype(BF)
+                    gmh_send[span, :] = gmh_acc[far_span, :].astype(BF)
+
+                ret_copy.start()
+                gmh_copy.start()
+            pl.loop(0, half)(rows_of)
+
+            @pl.loop(0, 4)
+            def _(q, slot=slot):
+                line, side = (lax.div(q, 2), lax.rem(q, 2))
+                cols = tile(q, 256)
+                parts1[slot, side, line] = dot(mh2[:, cols], gp_s[...], TN).astype(BF)
+                parts2[slot, line, side] = dot(gr2[:, cols], sq_s[...], TN).astype(BF)
+
+            for reduce in reduces[slot]:
+                reduce.start()
+            if slot >= 2:
+                for reduce in reduces[slot - 2]:
+                    reduce.middle()
+        for copy in late:
+            copy.wait()
+
+    wide_w = pltpu.VMEM((planes, 1024, hidden), BF)
+    pl.run_scoped(
+        feed_forward,
+        wide_w,
+        pltpu.VMEM((planes, hidden, 1024), BF),
+        pltpu.VMEM((2 * tokens, 1024), BF),
+        pltpu.VMEM((2 * tokens, 1024), BF),
+        pltpu.VMEM((2 * tokens, hidden), BF),
+        pltpu.VMEM((2 * tokens, hidden), BF),
+    )
+    own = slice(0, tokens)
+    far = slice(tokens, 2 * tokens)
+    block = 16
+
+    def attention(k_s, v_s, r_s, num_s, den_s, wg, wo, ggp_s, gatt_s, grp_s, gk_s, gv_s):
+        need_wg = load(gate_w, wg)
+        need_wo = load(output_w, wo)
+        need = [
+            load(k_ref, k_s),
+            load(v_ref, v_s),
+            load(r_ref, r_s),
+            load(num_ref, num_s),
+            load(den_ref, den_s),
+        ]
+        sums_s[...] = jnp.zeros_like(sums_s)
+        row_at = lax.broadcasted_iota(jnp.int32, (rows, rows), 0)
+        col_at = lax.broadcasted_iota(jnp.int32, (rows, rows), 1)
+        for m in range(micros):
+            mask_s[m] = jnp.logical_and(
+                segcol_ref[m * rows : (m + 1) * rows, :] == segrow_ref[m : m + 1, :],
+                col_at > row_at,
+            ).astype(F32).astype(BF)
+        ret_copy.wait()
+
+        @pl.loop(0, tokens // block)
+        def _(b):
+            span = tile(b, block)
+            returned = ret_acc[span, :] + ret_recv[span, :].astype(F32)
+            gate = gate_s[span, :]
+            product_in = gate * returned
+            ret_acc[span, :] = mid_s[span, :] + product_in
+            ggp_s[span, :] = (adj_s[span, :].astype(F32) * product_in * (1.0 - gate)).astype(BF)
+
+        put(ret_acc.at[own], out_ref)
+        put(ggp_s, ggp_out)
+        need_wg.wait()
+
+        @pl.loop(0, 2)
+        def _(i):
+            span = tile(i, tokens // 2)
+            ret_acc[tile(2 + i, tokens // 2), :] = dot(ggp_s[span, :], wg[...], NT)
+
+        for reduce in reduces[planes - 2]:
+            reduce.middle()
+        for reduce in reduces[0]:
+            reduce.last()
+        gmg = ret_acc.at[far]
+        gmh_copy.wait()
+        mix_h, mix_g = (vec_ref[9:10, :], vec_ref[10:11, :])
+        gain = vec_ref[7:8, :]
+
+        def combine(b):
+            span = tile(b, block)
+            grad_h = gmh_acc[span, :] + gmh_recv[span, :].astype(F32)
+            grad_g = gmg[span, :]
+            shift = (grad_h * (1.0 - mix_h) + grad_g * (1.0 - mix_g)) * wide(keep_ref[span, :], 1024)
+            return (span, grad_h, grad_g, shift)
+
+        for m in range(micros):
+            pay_b[m : m + 1, :] = combine(m * (rows // block))[3][0:1, :]
+        pay_b[micros:, :] = jnp.zeros((8 - micros, 1024), F32)
+        halo_copy = remote(pay_b, halo_b, s_sem.at[2, 0], s_sem.at[2, 1], at.ahead(-1))
+        halo_copy.start()
+        at_last = lax.broadcasted_iota(jnp.int32, (block, 1024), 0) == block - 1
+        halo_copy.wait()
+        for m in range(micros):
+
+            def back_b(i, after, m=m):
+                span, grad_h, grad_g, shift = combine((m + 1) * (rows // block) - 1 - i)
+                delta = db_s[span, :]
+                sum_rows(sums_s, 9, grad_h * delta)
+                sum_rows(sums_s, 10, grad_g * delta)
+                moved = jnp.where(at_last, after, pltpu.roll(shift, block - 1, 0))
+                grad = grad_h * mix_h + grad_g * mix_g + moved
+                unit, inverse = unit_of(mid_s[span, :])
+                sum_rows(sums_s, 7, grad * unit)
+                sum_rows(sums_s, 8, grad)
+                total = adj_s[span, :].astype(F32) + norm_back_rows(grad, unit, inverse, gain)
+                gmh_acc[span, :] = total
+                gatt_s[span, :] = total.astype(BF)
+                return shift[0:1, :]
+
+            lax.fori_loop(0, rows // block, back_b, halo_b[m : m + 1, :])
+
+        put(gmh_acc.at[own], gmid_out)
+        put(gatt_s, gatt_out)
+        need_wo.wait()
+
+        @pl.loop(0, 2)
+        def _(i):
+            span = tile(i, tokens // 2)
+            gmh_acc[tile(2 + i, tokens // 2), :] = dot(gatt_s[span, :], wo[...], NT)
+
+        for reduce in reduces[planes - 1]:
+            reduce.middle()
+        for reduce in reduces[1]:
+            reduce.last()
+        for copy in need:
+            copy.wait()
+        width = 256
+        place = lax.broadcasted_iota(jnp.int32, (rows, width), 0).astype(F32)
+
+        @pl.loop(0, 1024 // width)
+        def _(i):
+            cols = tile(i, width)
+            rate = jnp.exp(vec_ref[2:3, cols])
+            rising = jnp.exp(place * rate)
+            falling = jnp.exp((1.0 - place) * rate)
+            step_back = jnp.exp(-rate)
+            extra = vec_ref[3:4, cols]
+            for m in range(micros):
+                span = slice(m * rows, (m + 1) * rows)
+                far_span = slice(tokens + m * rows, tokens + (m + 1) * rows)
+                bonus = jnp.exp(extra + k_s[span, cols])
+                recept = r_s[span, cols]
+                inverse = 1.0 / (den_s[span, cols] + bonus)
+                mixed = (num_s[span, cols] + bonus * v_s[span, cols]) * inverse
+                grad_gated = gmh_acc[far_span, cols]
+                grad_mixed = grad_gated * recept
+                grp_s[span, cols] = (grad_mixed * mixed * (1.0 - recept)).astype(BF)
+                up = grad_mixed * inverse
+                down = -up * mixed
+                up_sum = rising * dot_exact_left(mask_s[m], falling * up)
+                down_sum = rising * dot_exact_left(mask_s[m], falling * down)
+                gmh_acc[far_span, cols] = up
+                db_s[span, cols] = down
+                mid_s[span, cols] = up_sum
+                gate_s[span, cols] = down_sum
+                state_own[m : m + 1, cols] = up[0:1] + step_back * up_sum[0:1]
+                state_own[micros + m : micros + m + 1, cols] = down[0:1] + step_back * down_sum[0:1]
+
+        put(grp_s, grp_out)
+        core_copy = remote(state_own, state_other, s_sem.at[3, 0], s_sem.at[3, 1], at.other)
+        core_copy.start()
+        pair = lax.div(mp, 2) * 2
+        decay_all = jnp.exp(-float(rows) * jnp.exp(vec_ref[2:3, :]))
+
+        def seen(device, last):
+            index = lax.rem(device + at.count, at.count)
+            start = 0 if last else 2 * micros
+            return wide(segs_ref[index, start : start + 2 * micros, :], 1024)
+
+        core_copy.wait()
+        even = jnp.where(core == 0, state_own[...], state_other[...])
+        odd = jnp.where(core == 0, state_other[...], state_own[...])
+        state_chip[...] = even + jnp.where(
+            seen(pair, False) == seen(pair + 1, False), decay_all * odd, 0.0
+        )
+        chip_copies = [
+            remote(state_chip, state_in.at[step - 1], s_sem.at[3 + step, 0], s_sem.at[3 + step, 1], at.plane(-step))
+            for step in range(1, planes)
+        ]
+        for copy in chip_copies:
+            copy.start()
+        for copy in chip_copies:
+            copy.wait()
+        total = jnp.zeros_like(state_chip[...])
+        power = jnp.ones_like(decay_all)
+        for step in range(1, planes):
+            fits = jnp.logical_and(
+                seen(pair + 2 * step, False) == seen(mp, True), z + step < planes
+            )
+            total = total + jnp.where(fits, power * state_in[step - 1], 0.0)
+            power = power * decay_all * decay_all
+        joined = decay_all * total + jnp.where(
+            seen(pair + 1, False) == seen(pair, True), state_other[...], 0.0
+        )
+        carry_s[...] = jnp.where(core == 0, joined, total)
+        for reduce in reduces[2]:
+            reduce.last()
+
+        @pl.loop(0, 1024 // width)
+        def _(i):
+            cols = tile(i, width)
+            rate = jnp.exp(vec_ref[2:3, cols])
+            tail = jnp.exp((place - (rows - 1.0)) * rate)
+            extra = vec_ref[3:4, cols]
+            step_back = jnp.exp(-rate)
+            for m in range(micros):
+                span = slice(m * rows, (m + 1) * rows)
+                far_span = slice(tokens + m * rows, tokens + (m + 1) * rows)
+                fits = (segcol_ref[span, :] == segs_ref[mp, m : m + 1, :]).astype(F32)
+                carried = wide(fits, width) * tail
+                up_sum = mid_s[span, cols] + carried * carry_s[m : m + 1, cols]
+                down_sum = gate_s[span, cols] + carried * carry_s[micros + m : micros + m + 1, cols]
+                up, down = (gmh_acc[far_span, cols], db_s[span, cols])
+                key, value = (k_s[span, cols], v_s[span, cols])
+                bonus = jnp.exp(extra + key)
+                raised = jnp.exp(key)
+                direct = (up * value + down) * bonus
+                gk_s[span, cols] = (direct + raised * (value * up_sum + down_sum)).astype(BF)
+                gv_s[span, cols] = (up * bonus + raised * up_sum).astype(BF)
+                rate_part = -rate * step_back * (up_sum * num_s[span, cols] + down_sum * den_s[span, cols])
+                for index, part in ((2, rate_part), (3, direct)):
+                    summed = part[0:8]
+                    for start in range(8, rows, 8):
+                        summed = summed + part[start : start + 8]
+                    sums_s[index, :, cols] = sums_s[index, :, cols] + summed
+
+        put(gk_s, gk_out)
+        put(gv_s, gv_out)
+        for index in range(16):
+            sums_flat[index : index + 1, :] = jnp.sum(sums_s[index], axis=0, keepdims=True)
+        put(sums_flat, sums_out)
+        for reduce in reduces[3]:
+            reduce.last()
+        for slot in range(planes):
+            for reduce in reduces[slot]:
+                reduce.close()
+        for parts, far_parts, own_s, own_out, one, two, turned in (
+            (parts1, far1, own1_s, own1_out, lax.rem(dp, 2), lax.div(dp, 2), False),
+            (parts2, far2, own2_s, own2_out, lax.div(dp, 2), lax.rem(dp, 2), True),
+        ):
+            total = parts[0, one, two].astype(F32)
+            for slot in range(planes - 1):
+                total = total + far_parts[slot].astype(F32)
+            own_s[...] = total.T if turned else total
+            put(own_s, own_out)
+        for copy in outs:
+            copy.wait()
+
+    def hold(kind):
+        return pltpu.VMEM((tokens, 1024), kind)
+
+    square = pltpu.VMEM((1024, 1024), BF)
+    pl.run_scoped(attention, *([hold(F32)] * 5), square, square, *([hold(BF)] * 5))
+
+
+def middle_call(planes, micros, rows, operands):
+    tokens = micros * rows
+    hidden = operands[5].shape[1]
+
+    def big(kind):
+        return jax.ShapeDtypeStruct((tokens, 1024), kind)
+
+    def hold(count, kind):
+        return pltpu.VMEM((count, 1024), kind)
+
+    few = hold(8, F32)
+    quarter = (256, hidden)
+    sems = pltpu.SemaphoreType.DMA
+    return pl.pallas_call(
+        functools.partial(middle_kernel, planes, micros, rows),
+        out_shape=[big(F32)] * 2
+        + [big(BF)] * 5
+        + [jax.ShapeDtypeStruct((16, 1024), F32)]
+        + [jax.ShapeDtypeStruct(quarter, F32), jax.ShapeDtypeStruct(quarter[::-1], F32)],
+        in_specs=[VM] * 5 + [ANY] * 17,
+        out_specs=[ANY] * 10,
+        scratch_shapes=[pltpu.VMEM((planes, 2, 2) + quarter, BF)] * 2
+        + [pltpu.VMEM((planes, 2) + quarter, BF)] * 2
+        + [pltpu.VMEM((planes,) + quarter, BF)] * 2
+        + [pltpu.VMEM((planes - 1,) + quarter, BF)] * 2
+        + [hold(2 * tokens, F32)] * 2
+        + [hold(tokens, BF)] * 4
+        + [hold(tokens, F32), hold(tokens, F32), hold(tokens, BF), hold(tokens, F32)]
+        + [
+            pltpu.VMEM((16, 8, 1024), F32),
+            pltpu.VMEM((16, 1024), F32),
+            pltpu.VMEM((micros, rows, rows), BF),
+            few,
+            few,
+            few,
+            few,
+            few,
+            pltpu.VMEM((planes - 1, 8, 1024), F32),
+            few,
+            pltpu.VMEM(quarter, F32),
+            pltpu.VMEM(quarter[::-1], F32),
+            sems((24,)),
+            sems((10,)),
+            sems((planes, 2, 3, 2)),
+            sems((3 + planes, 2)),
+        ],
+        compiler_params=pltpu.CompilerParams(
+            collective_id=1, has_side_effects=True, vmem_limit_bytes=62 << 20
+        ),
+        cost_estimate=pl.CostEstimate(
+            flops=52 * tokens * 1024 * 1024, bytes_accessed=60 << 20, transcendentals=6 * tokens * 1024
+        ),
+        name="channel_mix_and_adjoint",
+    )(*operands)
+
+
+class ReduceSquare:
+    def __init__(self, at, parts, across, first, second, far, sems, x_first):
+        self.at, self.across, self.first, self.second, self.far = (at, across, first, second, far)
+        self.x_first = x_first
+        side = lax.rem(at.dp, 2)
+        line = lax.div(at.dp, 2)
+        self.one, self.two = (side, line) if x_first else (line, side)
+        near, next_to = (at.side_x, at.side_y) if x_first else (at.side_y, at.side_x)
+        self.parts = parts
+        self.mine = parts.at[at.core]
+        self.copy_0 = remote(parts.at[1 - at.core], across, sems.at[0, 0], sems.at[0, 1], at.other)
+        self.copy_1 = remote(self.mine.at[1 - self.one], first, sems.at[1, 0], sems.at[1, 1], near)
+        self.copy_2 = remote(
+            self.mine.at[self.one, 1 - self.two], second, sems.at[2, 0], sems.at[2, 1], next_to
+        )
+        self.copies_3 = [
+            remote(
+                self.mine.at[self.one, self.two, lax.rem(at.z + step, at.planes)],
+                far.at[step - 1],
+                sems.at[2 + step, 0],
+                sems.at[2 + step, 1],
+                at.plane(step),
+            )
+            for step in range(1, at.planes)
+        ]
+
+    def fill(self, left, right):
+        planes = self.at.planes
+
+        @pl.loop(0, 4)
+        def _(q):
+            line, side = (lax.div(q, 2), lax.rem(q, 2))
+            one, two = (side, line) if self.x_first else (line, side)
+            made = dot(left[:, tile(q, 256)], right[...], TN).astype(BF)
+            split = made.reshape(planes, 2, 256 // (2 * planes), 1024)
+            self.parts[0, one, two] = split[:, 0]
+            self.parts[1, one, two] = split[:, 1]
+
+        self.copy_0.start()
+
+    def add(self, one, two, other):
+        @pl.loop(0, self.at.planes)
+        def _(i):
+            self.mine[one, two, i] = (
+                self.mine[one, two, i].astype(F32) + other[i].astype(F32)
+            ).astype(BF)
+
+    def begin(self):
+        self.copy_0.wait()
+        for two in range(2):
+            self.add(1 - self.one, two, self.across.at[1 - self.one, two])
+        self.copy_1.start()
+        for two in range(2):
+            self.add(self.one, two, self.across.at[self.one, two])
+
+    def middle(self):
+        self.copy_1.wait()
+        self.add(self.one, 1 - self.two, self.first.at[1 - self.two])
+        self.copy_2.start()
+        self.add(self.one, self.two, self.first.at[self.two])
+
+    def last(self):
+        self.copy_2.wait()
+        self.add(self.one, self.two, self.second)
+        for copy in self.copies_3:
+            copy.start()
+
+    def close(self):
+        for copy in self.copies_3:
+            copy.wait()
+        total = self.mine[self.one, self.two, self.at.z].astype(F32)
+        for step in range(self.at.planes - 1):
+            total = total + self.far[step].astype(F32)
+        return total
+
+
+def last_kernel(
+    planes,
+    micros,
+    rows,
+    vec_ref,
+    keep_ref,
+    sums_ref,
+    gated_ref,
+    gatt_ref,
+    mg_ref,
+    ggp_ref,
+    mr_ref,
+    grp_ref,
+    mv_ref,
+    gv_ref,
+    mk_ref,
+    gk_ref,
+    recept_w,
+    value_w,
+    key_w,
+    x_ref,
+    da_ref,
+    gmid_ref,
+    grad_out,
+    sums_out,
+    own_output,
+    own_gate,
+    own_recept,
+    own_value,
+    own_key,
+    left_s,
+    right_s,
+    w_s,
+    x_s,
+    da_s,
+    total_s,
+    g_s,
+    sums_s,
+    parts,
+    across,
+    first,
+    second,
+    far,
+    own_s,
+    pay_a,
+    halo_a,
+    flat_s,
+    flat_recv,
+    load_sem,
+    out_sem,
+    rs_sem,
+    s_sem,
+):
+    at = Place(planes)
+    tokens = micros * rows
+    outs = []
+
+    def put(source, target):
+        copy = pltpu.make_async_copy(source, target, out_sem.at[len(outs)])
+        copy.start()
+        outs.append(copy)
+
+    loaded = []
+
+    def load(source, target):
+        copy = pltpu.make_async_copy(source, target, load_sem.at[len(loaded)])
+        copy.start()
+        loaded.append(copy)
+        return copy
+
+    sides = (
+        (gated_ref, gatt_ref),
+        (mg_ref, ggp_ref),
+        (mr_ref, grp_ref),
+        (mv_ref, gv_ref),
+        (mk_ref, gk_ref),
+    )
+    side_loads = [
+        (load(left, left_s.at[index]), load(right, right_s.at[index]))
+        for index, (left, right) in enumerate(sides)
+    ]
+    w_loads = [
+        load(source, w_s.at[index]) for index, source in enumerate((recept_w, value_w, key_w))
+    ]
+    row_loads = [load(x_ref, x_s), load(da_ref, da_s), load(gmid_ref, total_s)]
+    greet(
+        [at.other, at.side_x, at.side_y]
+        + [at.plane(step) for step in range(1, planes)]
+        + [at.ahead(1), at.ahead(-1)]
+    )
+    reduces = [
+        ReduceSquare(
+            at, parts.at[index], across.at[index], first.at[index], second.at[index],
+            far.at[index], rs_sem.at[index], index % 2 == 0,
+        )
+        for index in range(5)
+    ]
+    sums_s[...] = jnp.zeros_like(sums_s)
+    for index, reduce in enumerate(reduces):
+        for copy in side_loads[index]:
+            copy.wait()
+        reduce.fill(left_s.at[index], right_s.at[index])
+        if index:
+            reduces[index - 1].begin()
+    for index, copy in enumerate(w_loads):
+        copy.wait()
+
+        @pl.loop(0, 2)
+        def _(i, index=index):
+            span = tile(i, tokens // 2)
+            g_s[index, span, :] = dot(right_s[2 + index, span, :], w_s[index], NT)
+
+        if index == 0:
+            reduces[4].begin()
+    for copy in row_loads:
+        copy.wait()
+    block = 16
+    mixes = (vec_ref[6:7, :], vec_ref[5:6, :], vec_ref[4:5, :])
+    gain = vec_ref[0:1, :]
+
+    def combine(b):
+        span = tile(b, block)
+        grads = [g_s[index, span, :] for index in range(3)]
+        shift = sum(grad * (1.0 - mix) for grad, mix in zip(grads, mixes))
+        return (span, grads, shift * wide(keep_ref[span, :], 1024))
+
+    for m in range(micros):
+        pay_a[m : m + 1, :] = combine(m * (rows // block))[2][0:1, :]
+    pay_a[micros:, :] = jnp.zeros((8 - micros, 1024), F32)
+    halo_copy = remote(pay_a, halo_a, s_sem.at[0, 0], s_sem.at[0, 1], at.ahead(-1))
+    halo_copy.start()
+    at_last = lax.broadcasted_iota(jnp.int32, (block, 1024), 0) == block - 1
+    halo_copy.wait()
+    for m in range(micros):
+
+        def back_a(i, after, m=m):
+            span, grads, shift = combine((m + 1) * (rows // block) - 1 - i)
+            delta = da_s[span, :]
+            for index, grad in enumerate(grads):
+                sum_rows(sums_s, 2 - index, grad * delta)
+            moved = jnp.where(at_last, after, pltpu.roll(shift, block - 1, 0))
+            grad = sum(part * mix for part, mix in zip(grads, mixes)) + moved
+            unit, inverse = unit_of(x_s[span, :].astype(F32))
+            sum_rows(sums_s, 3, grad * unit)
+            sum_rows(sums_s, 4, grad)
+            total_s[span, :] = total_s[span, :] + norm_back_rows(grad, unit, inverse, gain)
+            return shift[0:1, :]
+
+        lax.fori_loop(0, rows // block, back_a, halo_a[m : m + 1, :])
+    put(total_s, grad_out)
+    flat_s[0] = sums_ref[...]
+    for index, row in enumerate((4, 5, 6, 0, 1)):
+        flat_s[0, row : row + 1, :] = jnp.sum(sums_s[index], axis=0, keepdims=True)
+    for step, device in enumerate((at.other, at.side_x, at.side_y)):
+        copy = remote(flat_s.at[step], flat_recv.at[step], s_sem.at[1 + step, 0], s_sem.at[1 + step, 1], device)
+        copy.start()
+        if step == 0:
+            reduces[0].middle()
+            reduces[1].middle()
+        copy.wait()
+        flat_s[step + 1] = flat_s[step] + flat_recv[step]
+    flat_copies = [
+        remote(
+            flat_s.at[3],
+            flat_recv.at[2 + step],
+            s_sem.at[3 + step, 0],
+            s_sem.at[3 + step, 1],
+            at.plane(step),
+        )
+        for step in range(1, planes)
+    ]
+    for copy in flat_copies:
+        copy.start()
+    reduces[2].middle()
+    reduces[3].middle()
+    reduces[0].last()
+    reduces[1].last()
+    reduces[4].middle()
+    reduces[2].last()
+    reduces[3].last()
+    for copy in flat_copies:
+        copy.wait()
+    flat_s[0] = flat_s[3] + sum(flat_recv[2 + step] for step in range(1, planes))
+    put(flat_s.at[0], sums_out)
+    reduces[4].last()
+    for index, target in enumerate((own_output, own_gate, own_recept, own_value, own_key)):
+        own_s[index] = reduces[index].close()
+        put(own_s.at[index], target)
+    for copy in outs:
+        copy.wait()
+
+
+def last_call(planes, micros, rows, operands):
+    tokens = micros * rows
+
+    def hold(count, kind):
+        return pltpu.VMEM((count, tokens, 1024), kind)
+
+    piece = (1024 // (8 * planes), 1024)
+    sems = pltpu.SemaphoreType.DMA
+    few = pltpu.VMEM((8, 1024), F32)
+    return pl.pallas_call(
+        functools.partial(last_kernel, planes, micros, rows),
+        out_shape=[
+            jax.ShapeDtypeStruct((tokens, 1024), F32),
+            jax.ShapeDtypeStruct((16, 1024), F32),
+        ]
+        + [jax.ShapeDtypeStruct(piece, F32)] * 5,
+        in_specs=[VM] * 3 + [ANY] * 16,
+        out_specs=[ANY] * 7,
+        scratch_shapes=[
+            hold(5, BF),
+            hold(5, BF),
+            pltpu.VMEM((3, 1024, 1024), BF),
+            pltpu.VMEM((tokens, 1024), BF),
+            pltpu.VMEM((tokens, 1024), F32),
+            pltpu.VMEM((tokens, 1024), F32),
+            hold(3, F32),
+            pltpu.VMEM((5, 8, 1024), F32),
+            pltpu.VMEM((5, 2, 2, 2, planes) + piece, BF),
+            pltpu.VMEM((5, 2, 2, planes) + piece, BF),
+            pltpu.VMEM((5, 2, planes) + piece, BF),
+            pltpu.VMEM((5, planes) + piece, BF),
+            pltpu.VMEM((5, planes - 1) + piece, BF),
+            pltpu.VMEM((5,) + piece, F32),
+            few,
+            few,
+            pltpu.VMEM((4, 16, 1024), F32),
+            pltpu.VMEM((2 + planes, 16, 1024), F32),
+            sems((16,)),
+            sems((7,)),
+            sems((5, 2 + planes, 2)),
+            sems((3 + planes, 2)),
+        ],
+        compiler_params=pltpu.CompilerParams(
+            collective_id=2, has_side_effects=True, vmem_limit_bytes=62 << 20
+        ),
+        cost_estimate=pl.CostEstimate(
+            flops=16 * tokens * 1024 * 1024, bytes_accessed=30 << 20, transcendentals=0
+        ),
+        name="time_mix_weights",
+    )(*operands)
 
 
 def one_micro(block_in, seg_ids, grad_out, vectors, matrices, hidden_w, return_w):
@@ -1158,72 +1851,52 @@
         hidden_full,
         return_full,
     )
-    made = forward_call(planes, micros, rows, operands)
-    kept = [part.reshape(micros, rows, depth) for part in made[:12]]
-    kept += [made[13][0].reshape(micros, rows, depth), made[14][0].reshape(micros, rows, depth)]
-    output, input_grad, grads = jax.vmap(
-        lambda rows, ids, adjoint, kept: one_micro_back(
-            rows, ids, adjoint, kept, vectors, matrices, hidden_full, return_full
-        )
-    )(
-        incoming_signal[:, 0].astype(jnp.float32),
-        series_number_table[:, 0],
-        upstream_adjoint[:, 0].astype(jnp.float32),
-        kept,
-    )
-    totals = tuple(
-        product_tn(*(side.reshape(-1, side.shape[-1]) for side in grad))
-        if isinstance(grad, tuple)
-        else jnp.sum(grad, axis=0)
-        for grad in grads
-    )
-    square = [index for index in range(18) if totals[index].shape == totals[7].shape]
-    lines = [index for index in range(18) if totals[index].ndim == 1]
-    wide = lax.psum_scatter(
-        jnp.concatenate([reduced_precision(totals[index]) for index in square], axis=1),
-        ("dp", "mp"),
-        scatter_dimension=0,
-        tiled=True,
-    ).astype(jnp.float32)
-    thin = lax.psum_scatter(
-        jnp.stack([totals[index] for index in lines], axis=1),
-        ("dp", "mp"),
-        scatter_dimension=0,
-        tiled=True,
-    )
-    held = dict(zip(square, jnp.split(wide, len(square), axis=1)))
-    held.update({index: thin[:, place] for place, index in enumerate(lines)})
-    output, input_grad = (output[:, None], input_grad[:, None])
-    owned = tuple(held[index] for index in sorted(held))
-    hidden_own, return_own = (
-        lax.psum_scatter(
-            totals[15].astype(jnp.bfloat16), "dp", scatter_dimension=0, tiled=True
-        ).astype(jnp.float32),
-        lax.psum_scatter(
-            totals[16].astype(jnp.bfloat16), "dp", scatter_dimension=1, tiled=True
-        ).astype(jnp.float32),
-    )
+    (
+        keys, values, recept, num, den, mid, gate, mk, mv, mr, gated, mg, delta_a, delta_b,
+        keep, segs, mh_all, ret_all, w1_all, w2_all,
+    ) = forward_call(planes, micros, rows, operands)
+    x, _, segcol, segrow, _, table, adjoint = operands[:7]
+    key_w, value_w, recept_w, output_w, gate_w = matrices
+    (
+        output, grad_mid, grad_gate, grad_att, grad_recept, grad_key, grad_value, sums,
+        own_hidden, own_return,
+    ) = middle_call(
+        planes,
+        micros,
+        rows,
+        (
+            table, keep, segs, segcol, segrow, hidden_full, return_full, w1_all, w2_all,
+            mh_all, ret_all, mid, gate, adjoint, delta_b, keys, values, recept, num, den,
+            gate_w, output_w,
+        ),
+    )
+    input_grad, sums, own_output, own_gate, own_recept, own_value, own_key = last_call(
+        planes,
+        micros,
+        rows,
+        (
+            table, keep, sums, gated, grad_att, mg, grad_gate, mr, grad_recept, mv, grad_value,
+            mk, grad_key, recept_w, value_w, key_w, x, delta_a, grad_mid,
+        ),
+    )
+    span = depth // (lax.axis_size("dp") * lax.axis_size("mp"))
+    mine = lax.dynamic_slice_in_dim(
+        sums, lax.axis_index(("dp", "mp")) * span, span, axis=1
+    )
+    line = [mine[index] for index in range(11)]
+    shape = incoming_signal.shape
     return (
-        output,
-        input_grad,
-        owned[0],
-        owned[1],
-        owned[2],
-        owned[3],
-        owned[4],
-        owned[5],
-        owned[6],
-        owned[7],
-        owned[8],
-        owned[9],
-        owned[10],
-        owned[11],
-        owned[12],
-        owned[13],
-        owned[14],
-        hidden_own,
-        return_own,
-        owned[15],
+        output.reshape(shape),
+        input_grad.reshape(shape),
+        *line[:7],
+        own_key,
+        own_value,
+        own_recept,
+        own_output,
+        *line[7:],
+        own_hidden,
+        own_return,
+        own_gate,
     )
 
 

time: 889 us -> 332 us (0.37)
  waiting for transfers between devices: 505 us -> 0 us
  Pallas kernels: 93.4 us -> 307 us
  matrix products: 83.3 us -> 0 us
  blocking collectives: 57 us -> 0 us
  other arithmetic: 54.4 us -> 2.02 us
  local copies, waits for them, and re-layouts: 61.9 us -> 22 us
  between operations: 15.2 us -> 0.74 us
  starting transfers between devices: 9.73 us -> 0 us
    unnamed x10 -> x0, waiting for transfers between devices: 258 us -> none
    pallas_call x0 -> x2, Pallas kernels: none -> 214 us  [the longest x1 123 us: middle_call(): pl.pallas_call(functools.partial(middle_kernel, planes, micros, rows), ou...]
    all_gather x2 -> x0, waiting for transfers between devices: 146 us -> none  [the longest x1 81.3 us: one_micro_back(): hidden_rows = lax.all_gather(low_hidden, 'mp', axis=0, tiled=True)]
    reduce_scatter x4 -> x0, waiting for transfers between devices: 102 us -> none  [the longest x1 53.8 us: one_micro_back(): lax.psum_scatter(product_nt(grad_pre, hidden_w).astype(jnp.bfloat16), 'mp...]
    dot_general x17 -> x0, matrix products: 83.3 us -> none  [the longest x7 34.2 us: product_tn(): lax.dot_general(left, right, (((0,), (0,)), ((), ())), preferred_element_...]
    all_gather x3 -> x0, blocking collectives: 57 us -> none  [carried_in(): everything = jax.tree.map(lambda part: lax.all_gather(part, axis), shard)]
    unnamed x132 -> x26, local copies, waits for them, and re-layouts: 47.2 us -> 9.53 us
    convert_element_type x19 -> x0, other arithmetic: 25.1 us -> none  [the longest x3 13.1 us: reduced_precision(): return values.astype(jnp.bfloat16)]
  transfers between devices with their start and end apart: 13 -> 0, of which waited for: 6 -> 0; matrix products, arithmetic and copies ran while one was open for 19% -> 0% of each run, Pallas kernels for 0% -> 0%
where the time goes in v3:
time: 332 us
  Pallas kernels  307 us (92%)
  local copies, waits for them, and re-layouts  22 us (7%)
    pallas_call x1, Pallas kernels, middle_call(): pl.pallas_call(functools.partial(middle_kernel, planes, micros, rows), ou...  123 us
    pallas_call x1, Pallas kernels, forward_call(): pl.pallas_call(functools.partial(forward_kernel, planes, micros, rows), o...  93.1 us
    pallas_call x1, Pallas kernels, last_call(): pl.pallas_call(functools.partial(last_kernel, planes, micros, rows), out_...  90.8 us
    unnamed x26, local copies, waits for them, and re-layouts  9.53 us
    another operation x12, local copies, waits for them, and re-layouts, kernel_body(): jnp.stack(vectors)  7.63 us

profile of v3, /device:TPU:0, one launch (start us, length us, event | category | flops | bytes accessed | tf_op | source)
XLA Modules:
  0.0 331.9 jit_solution(2711870148502954583)
XLA Ops:
  0.7 0.7 convert_bitcast_fusion
  1.3 0.1 fusion
  1.4 0.1 copy.51
  1.5 0.1 copy.53
  1.6 0.1 maximum_bitcast_fusion
  1.7 0.7 broadcast_in_dim.14.segpay_ref
  2.4 0.6 pad.20.segrow_ref
  3.0 0.8 broadcast_in_dim.12.segcol_ref
  3.8 0.7 stack.48
  4.5 0.7 stack.49
  5.2 0.7 stack.50
  5.8 0.7 stack.51
  6.5 0.7 stack.52
  7.2 0.7 stack.53
  7.9 0.7 stack.54
  8.6 0.7 stack.55
  9.3 0.7 stack.56
  10.0 0.7 stack.57
  10.6 0.7 stack.58
  11.3 0.1 stack.59
  11.4 0.6 pad_convert_fusion.vec_ref
  12.1 0.9 slice.42
  12.9 0.6 pad_convert_fusion.1.last_ref
  13.6 93.1 %time_mix_forward.1 = (f32[512,1024]{1,0:T(8,128)}, f32[512,1024]{1,0:T(8,128)}, f32[512,1024]{1,0:T(8,128)}, f32[512,1024]{1,0:T(8,128)}, f32[512,1024]{1,0:T(8...) custom-call(bf16[512,1024]{1,0:T(8,128)(2,1)} %bitcast.44, ...), custom_call_target="tpu_custom_call" | custom-call | flops 5368709120 | bytes 41943040 | tf_op jit(solution)/shard_map/time_mix_forward/pallas_call | solution.py:562
  106.7 123.2 %channel_mix_and_adjoint.1 = (f32[512,1024]{1,0:T(8,128)}, f32[512,1024]{1,0:T(8,128)}, bf16[512,1024]{1,0:T(8,128)(2,1)}, bf16[512,1024]{1,0:T(8,128)(2,1)}, bf...) custom-call(f32[16,1024]{1,0:T(8,128)} %pad_convert_fusion.vec_ref, ...), custom_call_target="tpu_custom_call" | custom-call | flops 27917287424 | bytes 62914560 | tf_op jit(solution)/shard_map/channel_mix_and_adjoint/pallas_call | solution.py:1095
  229.9 90.8 %time_mix_weights.1 = (f32[512,1024]{1,0:T(8,128)}, f32[16,1024]{1,0:T(8,128)}, f32[32,1024]{1,0:T(8,128)}, f32[32,1024]{1,0:T(8,128)}, f32[32,1024]{1,0:T(8,128...) custom-call(f32[16,1024]{1,0:T(8,128)} %pad_convert_fusion.vec_ref, f32[512,128]{1,0:T(8,128)} %get-tuple-element.57.keep_ref, ...), custom_call_target="tpu_custom_call" | custom-call | flops 8589934592 | bytes 31457280 | tf_op jit(solution)/shard_map/time_mix_weights/pallas_call | solution.py:1415
  320.7 1.6 dynamic-slice_bitcast_fusion
  322.3 0.0 copy-start
  322.3 3.3 copy.69
  325.7 0.0 copy-done
  325.7 0.0 copy-start.6
  325.7 0.0 copy-start.4
  325.7 0.0 copy-start.2
  325.7 1.3 copy.70
  327.0 0.0 copy-done.7
  327.0 0.7 copy.71
  327.7 0.0 copy-done.6
  327.7 0.7 copy.72
  328.3 0.0 copy-done.5
  328.3 0.7 copy.73
  329.0 0.0 copy-done.4
  329.0 0.7 copy.74
  329.6 0.0 copy-done.2
  329.7 0.8 copy.75
  330.4 0.0 copy-done.1
  330.4 0.8 copy.76
  331.2 0.0 copy-done.3
  331.2 0.7 copy.77
  (5 shorter events, 0.0 us)
Async XLA Ops:
  322.3 3.3 copy-start
  325.7 1.4 copy-start.7
  325.7 2.0 copy-start.6
  325.7 2.7 copy-start.5
  325.7 3.3 %copy-start.4 = (f32[32,1024]{1,0:T(8,128)S(1)}, f32[32,1024]{1,0:T(8,128)}, u32[]{:S(2)}) copy-start(f32[32,1024]{1,0:T(8,128)} %get-tuple-element.201) | copy-start | bytes 393220
  325.7 4.0 %copy-start.2 = (f32[256,512]{1,0:T(8,128)S(1)}, f32[256,512]{1,0:T(8,128)}, u32[]{:S(2)}) copy-start(f32[256,512]{1,0:T(8,128)} %get-tuple-element.206) | copy-start | bytes 1572868
  327.0 3.4 %copy-start.1 = (f32[512,256]{1,0:T(8,128)S(1)}, f32[512,256]{1,0:T(8,128)}, u32[]{:S(2)}) copy-start(f32[512,256]{1,0:T(8,128)} %get-tuple-element.207) | copy-start | bytes 1572868
  327.0 4.2 %copy-start.3 = (f32[32,1024]{1,0:T(8,128)S(1)}, f32[32,1024]{1,0:T(8,128)}, u32[]{:S(2)}) copy-start(f32[32,1024]{1,0:T(8,128)} %get-tuple-element.208) | copy-start | bytes 393220

commit v4 on v3

--- a/solution.py
+++ b/solution.py
@@ -161,17 +161,47 @@
     pl.semaphore_wait(barrier, len(devices))
 
 
+def feed_rows(w1, w2, mh2, gr2, sq_s, gp_s, ret_acc, gmh_acc, fresh):
+    def rows_of(i):
+        span = tile(i, 256)
+        pre = dot(mh2[span, :], w1[...])
+        rectified = jnp.maximum(pre, 0.0)
+        squared = (rectified * rectified).astype(BF)
+        sq_s[span, :] = squared
+        grad_squared = dot(gr2[span, :], w2[...], NT)
+        grad_pre = (grad_squared * 2.0 * rectified).astype(BF)
+        gp_s[span, :] = grad_pre
+        if fresh:
+            ret_acc[span, :] = dot(squared, w2[...])
+            gmh_acc[span, :] = dot(grad_pre, w1[...], NT)
+        else:
+            ret_acc[span, :] += dot(squared, w2[...])
+            gmh_acc[span, :] += dot(grad_pre, w1[...], NT)
+
+    return rows_of
+
+
+def feed_grads(mh2, gr2, sq_s, gp_s, parts1, parts2):
+    @pl.loop(0, 4)
+    def _(q):
+        line, side = (lax.div(q, 2), lax.rem(q, 2))
+        cols = tile(q, 256)
+        parts1[side, line] = dot(mh2[:, cols], gp_s[...], TN).astype(BF)
+        parts2[line, side] = dot(gr2[:, cols], sq_s[...], TN).astype(BF)
+
+
 def forward_kernel(
     planes,
     micros,
     rows,
     x_ref,
-    last_ref,
-    segcol_ref,
-    segrow_ref,
-    segpay_ref,
-    vec_ref,
+    table_ref,
     adj_ref,
+    *refs,
+):
+    (
+    lines, refs) = (refs[:11], refs[11:])
+    (
     key_w,
     value_w,
     recept_w,
@@ -195,10 +225,17 @@
     db_out,
     keep_out,
     segs_out,
+    vec_out,
+    segcol_out,
+    segrow_out,
     mh_all,
     ret_all,
     w1_all,
     w2_all,
+    ret_acc_out,
+    gmh_acc_out,
+    parts1_out,
+    parts2_out,
     wk,
     wv,
     wr,
@@ -218,9 +255,11 @@
     mr_s,
     gated_s,
     mg_s,
-    mh_s,
-    ret_s,
     keep_s,
+    segcol_ref,
+    segrow_ref,
+    segpay_ref,
+    last_ref,
     mask_s,
     halo_a,
     near_a,
@@ -237,24 +276,55 @@
     small_sem,
     z_sem,
     s_sem,
-):
+    vec_ref,
+    mh2,
+    gr2,
+    sq_s,
+    gp_s,
+    ret_acc,
+    gmh_acc,
+    parts1,
+    parts2,
+    ff_sem,
+    ) = refs
     at = Place(planes)
     dp, mp, z, core = (at.dp, at.mp, at.z, at.core)
     tokens = micros * rows
     peers = [at.ahead(step) for step in range(1, at.count)]
     greet(peers + [at.side_x, at.side_y])
 
+    for index, line in enumerate(lines):
+        vec_ref[index : index + 1, :] = line[...].astype(F32).reshape(1, 1024)
+    vec_ref[11:16, :] = jnp.zeros((5, 1024), F32)
+
+    numbers = table_ref[...].astype(F32)
+    rest = jnp.zeros((8 - micros, rows), F32)
+    segrow_ref[...] = jnp.concatenate([numbers, rest], axis=0)
+    columns = segrow_ref[...].T
+    ends = [jnp.broadcast_to(numbers[:, at_end], (micros, 128)) for at_end in (slice(rows - 1, rows), slice(0, 1))]
+    segpay_ref[...] = jnp.concatenate([ends[0], ends[0], ends[1], ends[1]], axis=0)
+    last_ref[...] = jnp.zeros((8, 1024), F32)
+    for m in range(micros):
+        segcol_ref[m * rows : (m + 1) * rows, :] = jnp.broadcast_to(columns[:, m : m + 1], (rows, 128))
+        last_ref[m : m + 1, :] = x_ref[(m + 1) * rows - 16 : (m + 1) * rows, :].astype(F32)[15:16]
+
     quarter1, quarter2 = (w1_ref.shape[0] // 4, w2_ref.shape[0] // 4)
     q1, q2 = (tile(dp, quarter1), tile(dp, quarter2))
-    z_copies = []
-    for step in range(1, planes):
+    z_copies = {}
+    for step in (1, planes - 1):
         to = at.plane(-step)
-        z_copies.append(
-            (
-                remote(w1_ref.at[q1], w1_all.at[step - 1, q1], z_sem.at[step - 1, 0, 0], z_sem.at[step - 1, 0, 1], to),
-                remote(w2_ref.at[q2], w2_all.at[step - 1, q2], z_sem.at[step - 1, 1, 0], z_sem.at[step - 1, 1, 1], to),
-            )
+        z_copies[step - 1] = (
+            remote(w1_ref.at[q1], w1_all.at[step - 1, q1], z_sem.at[step - 1, 0, 0], z_sem.at[step - 1, 0, 1], to),
+            remote(w2_ref.at[q2], w2_all.at[step - 1, q2], z_sem.at[step - 1, 1, 0], z_sem.at[step - 1, 1, 1], to),
         )
+    half1 = tile(lax.div(dp, 2), 2 * quarter1)
+    far2 = tile(lax.rem(dp + 2, 4), quarter2)
+    back = at.plane(-1)
+    onward_1 = remote(w1_all.at[0, half1], w1_all.at[1, half1], z_sem.at[1, 0, 0], z_sem.at[1, 0, 1], back)
+    onward_2 = (
+        remote(w2_all.at[0, q2], w2_all.at[1, q2], z_sem.at[1, 1, 0], z_sem.at[1, 1, 1], back),
+        remote(w2_all.at[0, far2], w2_all.at[1, far2], z_sem.at[1, 2, 0], z_sem.at[1, 2, 1], back),
+    )
 
     halo_copy = remote(last_ref, halo_a, small_sem.at[0, 0], small_sem.at[0, 1], at.ahead(1))
     halo_copy.start()
@@ -271,7 +341,7 @@
     ):
         loads.append(pltpu.make_async_copy(source, target, w_sem.at[index]))
         loads[-1].start()
-    for copy in z_copies[0]:
+    for copy in z_copies[0] + z_copies[2]:
         copy.start()
     halo_copy.wait()
     for copy in seg_copies:
@@ -326,6 +396,9 @@
     put(da_s, da_out)
     put(keep_s, keep_out)
     put(segs_s, segs_out)
+    put(segcol_ref, segcol_out)
+    put(vec_ref, vec_out)
+    put(segrow_ref, segrow_out)
     put(mk_s, mk_out)
     put(mv_s, mv_out)
     put(mr_s, mr_out)
@@ -377,13 +450,13 @@
         )
 
     def across(step):
-        both1 = w1_all.at[step, tile(lax.div(dp, 2), 2 * quarter1)]
+        both1 = w1_all.at[step, half1]
         own2 = w2_all.at[step, q2]
-        far2 = w2_all.at[step, tile(lax.rem(dp + 2, 4), quarter2)]
+        next2 = w2_all.at[step, far2]
         return (
             remote(both1, both1, z_sem.at[step, 4, 0], z_sem.at[step, 4, 1], at.side_y),
             remote(own2, own2, z_sem.at[step, 5, 0], z_sem.at[step, 5, 1], at.side_x),
-            remote(far2, far2, z_sem.at[step, 6, 0], z_sem.at[step, 6, 1], at.side_x),
+            remote(next2, next2, z_sem.at[step, 6, 0], z_sem.at[step, 6, 1], at.side_x),
         )
 
     def start(group):
@@ -394,10 +467,9 @@
         for copy in group:
             copy.wait()
 
-    along_0, along_1, along_2 = (along(0), along(1), along(2))
+    along_0, along_2 = (along(0), along(2))
     across_0, across_1, across_2 = (across(0), across(1), across(2))
     start(along_0)
-    start(z_copies[2])
     loads[2].wait()
 
     @pl.loop(0, 2)
@@ -425,6 +497,7 @@
     finish(along_0)
     start(across_0)
     finish(chip_copies)
+    onward_1.start()
     total = jnp.zeros_like(state_chip[...])
     power = jnp.ones_like(decay_all)
     for step in range(1, planes):
@@ -456,6 +529,8 @@
             den_s[span, cols] = den
             gated_s[span, cols] = (r_s[span, cols] * mixed).astype(BF)
 
+    finish(z_copies[2])
+    start(along_2)
     put(num_s, num_out)
     put(den_s, den_out)
     put(gated_s, gated_out)
@@ -485,10 +560,8 @@
         def _(b):
             norm_b(b)
 
-    finish(z_copies[2])
-    start(along_2)
-    start(z_copies[1])
     halo_b_copy.wait()
+    start(onward_2)
     for m in range(micros):
 
         def mix_b(b, prev, m=m):
@@ -499,17 +572,17 @@
             )
             delta = normed - shifted
             xb_s[span, :] = delta
-            mh_s[span, :] = (shifted + delta * vec_ref[9:10, :]).astype(BF)
+            mh2[span, :] = (shifted + delta * vec_ref[9:10, :]).astype(BF)
             mg_s[span, :] = (shifted + delta * vec_ref[10:11, :]).astype(BF)
             return normed[block - 1 : block, :]
 
         lax.fori_loop(0, rows // block, mix_b, halo_b[m : m + 1, :])
 
+    own, far = (slice(0, tokens), slice(tokens, 2 * tokens))
     mh_copy = remote(
-        mh_s, mh_all.at[1], s_sem.at[planes + 1, 0], s_sem.at[planes + 1, 1], at.other
+        mh2.at[own], mh2.at[far], s_sem.at[planes + 1, 0], s_sem.at[planes + 1, 1], at.other
     )
     mh_copy.start()
-    put(mh_s, mh_all.at[0])
     put(mg_s, mg_out)
     put(xb_s, db_out)
     loads[4].wait()
@@ -519,25 +592,57 @@
         span = tile(i, tokens // 2)
         gate = jax.nn.sigmoid(dot(mg_s[span, :], wg[...]))
         gate_s[span, :] = gate
-        ret_s[span, :] = (adj_ref[span, :].astype(F32) * gate).astype(BF)
+        gr2[span, :] = (adj_ref[span, :].astype(F32) * gate).astype(BF)
 
     ret_copy = remote(
-        ret_s, ret_all.at[1], s_sem.at[planes + 2, 0], s_sem.at[planes + 2, 1], at.other
+        gr2.at[own], gr2.at[far], s_sem.at[planes + 2, 0], s_sem.at[planes + 2, 1], at.other
     )
     ret_copy.start()
-    put(ret_s, ret_all.at[0])
     put(gate_s, gate_out)
-    finish(across_0)
     finish(along_2)
     start(across_2)
-    finish(z_copies[1])
-    start(along_1)
-    finish(across_2)
-    finish(along_1)
-    start(across_1)
-    finish(across_1)
+    hidden = w1_ref.shape[1]
+    w1_own, w2_own = (wk.at[:, 0:hidden], wv.at[0:hidden])
+    w1_next, w2_next = (wk.at[:, hidden : 2 * hidden], wv.at[hidden : 2 * hidden])
+    ff_loads = [
+        pltpu.make_async_copy(source, target, ff_sem.at[index])
+        for index, (source, target) in enumerate(
+            ((w1_ref, w1_own), (w2_ref, w2_own), (w1_all.at[0], w1_next), (w2_all.at[0], w2_next))
+        )
+    ]
+    ff_loads[0].start()
+    ff_loads[1].start()
+    ff_loads[0].wait()
+    ff_loads[1].wait()
+    half = tokens // 256
+    step = feed_rows(w1_own, w2_own, mh2, gr2, sq_s, gp_s, ret_acc, gmh_acc, True)
+    pl.loop(0, half)(step)
     mh_copy.wait()
     ret_copy.wait()
+    put(mh2, mh_all)
+    put(gr2, ret_all)
+    finish(across_0)
+    ff_loads[2].start()
+    ff_loads[3].start()
+    pl.loop(half, 2 * half)(step)
+    finish(onward_2)
+    onward_1.wait()
+    start(across_1)
+    feed_grads(mh2, gr2, sq_s, gp_s, parts1.at[0], parts2.at[0])
+    put(parts1.at[0], parts1_out.at[0])
+    put(parts2.at[0], parts2_out.at[0])
+    ff_loads[2].wait()
+    ff_loads[3].wait()
+    pl.loop(0, 2 * half)(
+        feed_rows(w1_next, w2_next, mh2, gr2, sq_s, gp_s, ret_acc, gmh_acc, False)
+    )
+    put(ret_acc, ret_acc_out)
+    put(gmh_acc, gmh_acc_out)
+    feed_grads(mh2, gr2, sq_s, gp_s, parts1.at[1], parts2.at[1])
+    put(parts1.at[1], parts1_out.at[1])
+    put(parts2.at[1], parts2_out.at[1])
+    finish(across_2)
+    finish(across_1)
     for copy in outs:
         copy.wait()
 
@@ -567,19 +672,28 @@
         + [
             jax.ShapeDtypeStruct((tokens, 128), F32),
             jax.ShapeDtypeStruct((2 * planes, 16, 128), F32),
+            jax.ShapeDtypeStruct((16, 1024), F32),
+            jax.ShapeDtypeStruct((tokens, 128), F32),
+            jax.ShapeDtypeStruct((8, rows), F32),
         ]
-        + [jax.ShapeDtypeStruct((2, tokens, 1024), BF)] * 2
+        + [jax.ShapeDtypeStruct((2 * tokens, 1024), BF)] * 2
         + [
             jax.ShapeDtypeStruct((planes - 1, 1024, hidden), BF),
             jax.ShapeDtypeStruct((planes - 1, hidden, 1024), BF),
-        ],
-        in_specs=[VM] * 7 + [ANY] * 7,
-        out_specs=[ANY] * 20,
+        ]
+        + [jax.ShapeDtypeStruct((2 * tokens, 1024), F32)] * 2
+        + [jax.ShapeDtypeStruct((2, 2, 2, 256, hidden), BF)] * 2,
+        in_specs=[VM] * 14 + [ANY] * 7,
+        out_specs=[ANY] * 27,
         scratch_shapes=[square] * 5
         + [hold(F32)] * 9
-        + [hold(BF)] * 7
+        + [hold(BF)] * 5
         + [
             pltpu.VMEM((tokens, 128), F32),
+            pltpu.VMEM((tokens, 128), F32),
+            pltpu.VMEM((8, rows), F32),
+            pltpu.VMEM((4 * micros, 128), F32),
+            few,
             pltpu.VMEM((micros, rows, rows), BF),
             few,
             few,
@@ -592,16 +706,26 @@
             pltpu.VMEM((planes - 1, 8, 1024), F32),
             few,
             pair((5,)),
-            pair((20,)),
+            pair((29,)),
             pair((2 * planes + 1, 2)),
             pair((planes - 1, 7, 2)),
             pair((planes + 3, 2)),
+            pltpu.VMEM((16, 1024), F32),
+            pltpu.VMEM((2 * tokens, 1024), BF),
+            pltpu.VMEM((2 * tokens, 1024), BF),
+            pltpu.VMEM((2 * tokens, hidden), BF),
+            pltpu.VMEM((2 * tokens, hidden), BF),
+            pltpu.VMEM((2 * tokens, 1024), F32),
+            pltpu.VMEM((2 * tokens, 1024), F32),
+            pltpu.VMEM((2, 2, 2, 256, hidden), BF),
+            pltpu.VMEM((2, 2, 2, 256, hidden), BF),
+            pair((4,)),
         ],
         compiler_params=pltpu.CompilerParams(
-            collective_id=0, has_side_effects=True, vmem_limit_bytes=58 << 20
+            collective_id=0, has_side_effects=True, vmem_limit_bytes=62 << 20
         ),
         cost_estimate=pl.CostEstimate(
-            flops=10 * tokens * 1024 * 1024, bytes_accessed=40 << 20, transcendentals=6 * tokens * 1024
+            flops=36 * tokens * 1024 * 1024, bytes_accessed=40 << 20, transcendentals=6 * tokens * 1024
         ),
         name="time_mix_forward",
     )(*operands)
@@ -609,7 +733,7 @@
 
 class Reduce:
     def __init__(self, at, parts, first, second, far, sems, slot, x_first):
-        self.at, self.parts, self.slot = (at, parts, slot)
+        self.at, self.parts, self.slot = (at, parts, slot if far is not None else 0)
         side = lax.rem(at.dp, 2)
         line = lax.div(at.dp, 2)
         self.one, self.two = (side, line) if x_first else (line, side)
@@ -619,7 +743,7 @@
         self.copy_2 = remote(
             parts.at[self.one, 1 - self.two], second, sems.at[1, 0], sems.at[1, 1], next_to
         )
-        if slot:
+        if self.slot:
             self.copy_3 = remote(
                 parts.at[self.one, self.two], far, sems.at[2, 0], sems.at[2, 1], at.plane(slot)
             )
@@ -677,12 +801,14 @@
     segs_ref,
     segcol_ref,
     segrow_ref,
-    w1_ref,
-    w2_ref,
     w1_all,
     w2_all,
     mh_all,
     ret_all,
+    ret_acc_ref,
+    gmh_acc_ref,
+    parts1_ref,
+    parts2_ref,
     mid_ref,
     gate_ref,
     adj_ref,
@@ -704,6 +830,8 @@
     sums_out,
     own1_out,
     own2_out,
+    rest1_out,
+    rest2_out,
     parts1,
     parts2,
     first1,
@@ -742,7 +870,7 @@
     at = Place(planes)
     dp, mp, z, core = (at.dp, at.mp, at.z, at.core)
     tokens = micros * rows
-    hidden = w1_ref.shape[1]
+    hidden = w1_all.shape[2]
     outs = []
 
     def put(source, target):
@@ -768,52 +896,56 @@
         reduces.append(
             (
                 Reduce(at, parts1.at[slot], first1.at[slot], second1.at[slot],
-                       far1.at[max(slot - 1, 0)], rs_sem.at[slot, 0], slot, True),
+                       far1 if slot == 1 else None, rs_sem.at[slot, 0], slot, True),
                 Reduce(at, parts2.at[slot], first2.at[slot], second2.at[slot],
-                       far2.at[max(slot - 1, 0)], rs_sem.at[slot, 1], slot, False),
+                       far2 if slot == 1 else None, rs_sem.at[slot, 1], slot, False),
             )
         )
     ret_copy = remote(ret_send, ret_recv, s_sem.at[0, 0], s_sem.at[0, 1], at.other)
     gmh_copy = remote(gmh_send, gmh_recv, s_sem.at[1, 0], s_sem.at[1, 1], at.other)
 
+    part_loads = []
+    for slot in (1, 0):
+        part_loads.append(
+            (load(parts1_ref.at[slot], parts1.at[slot]), load(parts2_ref.at[slot], parts2.at[slot]))
+        )
+    acc_loads = [load(ret_acc_ref, ret_acc), load(gmh_acc_ref, gmh_acc)]
+
+    def begin(slot):
+        for reduce in reduces[slot]:
+            reduce.start()
+
+    def middle(slot):
+        for reduce in reduces[slot]:
+            reduce.middle()
+
+    def last(slot):
+        for reduce in reduces[slot]:
+            reduce.last()
+
     def feed_forward(w1, w2, mh2, gr2, sq_s, gp_s):
-        slots = []
-        mh_load = [load(mh_all.at[0], mh2.at[0:tokens]), load(ret_all.at[0], gr2.at[0:tokens])]
-        slots.append((load(w1_ref, w1.at[0]), load(w2_ref, w2.at[0])))
-        mh_load += [
-            load(mh_all.at[1], mh2.at[tokens : 2 * tokens]),
-            load(ret_all.at[1], gr2.at[tokens : 2 * tokens]),
+        mh_load = [load(mh_all, mh2), load(ret_all, gr2)]
+        order = (planes - 1, planes - 2)
+        slots = [
+            (load(w1_all.at[slot - 1], w1.at[index]), load(w2_all.at[slot - 1], w2.at[index]))
+            for index, slot in enumerate(order)
         ]
-        for slot in range(1, planes):
-            slots.append(
-                (load(w1_all.at[slot - 1], w1.at[slot]), load(w2_all.at[slot - 1], w2.at[slot]))
+        late = [load(mid_ref, mid_s), load(gate_ref, gate_s), load(adj_ref, adj_s), load(db_ref, db_s)]
+        for index, slot in enumerate((1, 0)):
+            for copy in part_loads[index]:
+                copy.wait()
+            begin(slot)
+        for copy in mh_load + acc_loads:
+            copy.wait()
+        half = tokens // 256
+        for index, slot in enumerate(order):
+            for copy in slots[index]:
+                copy.wait()
+            step = feed_rows(
+                w1.at[index], w2.at[index], mh2, gr2, sq_s, gp_s, ret_acc, gmh_acc, False
             )
-        late = [load(mid_ref, mid_s), load(gate_ref, gate_s), load(adj_ref, adj_s), load(db_ref, db_s)]
-        for copy in mh_load:
-            copy.wait()
-        for slot in range(planes):
-            for copy in slots[slot]:
-                copy.wait()
-
-            def rows_of(i, slot=slot):
-                span = tile(i, 256)
-                pre = dot(mh2[span, :], w1[slot])
-                rectified = jnp.maximum(pre, 0.0)
-                squared = (rectified * rectified).astype(BF)
-                sq_s[span, :] = squared
-                grad_squared = dot(gr2[span, :], w2[slot], NT)
-                grad_pre = (grad_squared * 2.0 * rectified).astype(BF)
-                gp_s[span, :] = grad_pre
-                if slot == 0:
-                    ret_acc[span, :] = dot(squared, w2[slot])
-                    gmh_acc[span, :] = dot(grad_pre, w1[slot], NT)
-                else:
-                    ret_acc[span, :] += dot(squared, w2[slot])
-                    gmh_acc[span, :] += dot(grad_pre, w1[slot], NT)
-
-            half = tokens // 256
-            pl.loop(half, 2 * half)(rows_of)
-            if slot == planes - 1:
+            pl.loop(half, 2 * half)(step)
+            if index == 1:
 
                 @pl.loop(0, tokens // 64)
                 def _(i):
@@ -824,28 +956,18 @@
 
                 ret_copy.start()
                 gmh_copy.start()
-            pl.loop(0, half)(rows_of)
-
-            @pl.loop(0, 4)
-            def _(q, slot=slot):
-                line, side = (lax.div(q, 2), lax.rem(q, 2))
-                cols = tile(q, 256)
-                parts1[slot, side, line] = dot(mh2[:, cols], gp_s[...], TN).astype(BF)
-                parts2[slot, line, side] = dot(gr2[:, cols], sq_s[...], TN).astype(BF)
-
-            for reduce in reduces[slot]:
-                reduce.start()
-            if slot >= 2:
-                for reduce in reduces[slot - 2]:
-                    reduce.middle()
+            pl.loop(0, half)(step)
+            feed_grads(mh2, gr2, sq_s, gp_s, parts1.at[slot], parts2.at[slot])
+            if index == 0:
+                middle(1)
+            begin(slot)
         for copy in late:
             copy.wait()
 
-    wide_w = pltpu.VMEM((planes, 1024, hidden), BF)
     pl.run_scoped(
         feed_forward,
-        wide_w,
-        pltpu.VMEM((planes, hidden, 1024), BF),
+        pltpu.VMEM((2, 1024, hidden), BF),
+        pltpu.VMEM((2, hidden, 1024), BF),
         pltpu.VMEM((2 * tokens, 1024), BF),
         pltpu.VMEM((2 * tokens, 1024), BF),
         pltpu.VMEM((2 * tokens, hidden), BF),
@@ -893,10 +1015,7 @@
             span = tile(i, tokens // 2)
             ret_acc[tile(2 + i, tokens // 2), :] = dot(ggp_s[span, :], wg[...], NT)
 
-        for reduce in reduces[planes - 2]:
-            reduce.middle()
-        for reduce in reduces[0]:
-            reduce.last()
+        middle(0)
         gmg = ret_acc.at[far]
         gmh_copy.wait()
         mix_h, mix_g = (vec_ref[9:10, :], vec_ref[10:11, :])
@@ -916,6 +1035,7 @@
         halo_copy.start()
         at_last = lax.broadcasted_iota(jnp.int32, (block, 1024), 0) == block - 1
         halo_copy.wait()
+        last(1)
         for m in range(micros):
 
             def back_b(i, after, m=m):
@@ -944,10 +1064,6 @@
             span = tile(i, tokens // 2)
             gmh_acc[tile(2 + i, tokens // 2), :] = dot(gatt_s[span, :], wo[...], NT)
 
-        for reduce in reduces[planes - 1]:
-            reduce.middle()
-        for reduce in reduces[1]:
-            reduce.last()
         for copy in need:
             copy.wait()
         width = 256
@@ -1019,8 +1135,8 @@
             seen(pair + 1, False) == seen(pair, True), state_other[...], 0.0
         )
         carry_s[...] = jnp.where(core == 0, joined, total)
-        for reduce in reduces[2]:
-            reduce.last()
+        middle(3)
+        last(0)
 
         @pl.loop(0, 1024 // width)
         def _(i):
@@ -1055,20 +1171,20 @@
         for index in range(16):
             sums_flat[index : index + 1, :] = jnp.sum(sums_s[index], axis=0, keepdims=True)
         put(sums_flat, sums_out)
-        for reduce in reduces[3]:
-            reduce.last()
-        for slot in range(planes):
-            for reduce in reduces[slot]:
-                reduce.close()
-        for parts, far_parts, own_s, own_out, one, two, turned in (
-            (parts1, far1, own1_s, own1_out, lax.rem(dp, 2), lax.div(dp, 2), False),
-            (parts2, far2, own2_s, own2_out, lax.div(dp, 2), lax.rem(dp, 2), True),
+        for reduce in reduces[1]:
+            reduce.close()
+        middle(2)
+        last(3)
+        for parts, far_parts, own_s, own_out, rest_out, one, two in (
+            (parts1, far1, own1_s, own1_out, rest1_out, lax.rem(dp, 2), lax.div(dp, 2)),
+            (parts2, far2, own2_s, own2_out, rest2_out, lax.div(dp, 2), lax.rem(dp, 2)),
         ):
-            total = parts[0, one, two].astype(F32)
-            for slot in range(planes - 1):
-                total = total + far_parts[slot].astype(F32)
-            own_s[...] = total.T if turned else total
+            own_s[...] = parts[0, one, two].astype(F32) + far_parts[...].astype(F32)
             put(own_s, own_out)
+            put(parts.at[3, one, two], rest_out.at[1])
+        last(2)
+        put(parts1.at[2, lax.rem(dp, 2), lax.div(dp, 2)], rest1_out.at[0])
+        put(parts2.at[2, lax.div(dp, 2), lax.rem(dp, 2)], rest2_out.at[0])
         for copy in outs:
             copy.wait()
 
@@ -1081,7 +1197,7 @@
 
 def middle_call(planes, micros, rows, operands):
     tokens = micros * rows
-    hidden = operands[5].shape[1]
+    hidden = operands[5].shape[2]
 
     def big(kind):
         return jax.ShapeDtypeStruct((tokens, 1024), kind)
@@ -1097,13 +1213,14 @@
         out_shape=[big(F32)] * 2
         + [big(BF)] * 5
         + [jax.ShapeDtypeStruct((16, 1024), F32)]
-        + [jax.ShapeDtypeStruct(quarter, F32), jax.ShapeDtypeStruct(quarter[::-1], F32)],
-        in_specs=[VM] * 5 + [ANY] * 17,
-        out_specs=[ANY] * 10,
+        + [jax.ShapeDtypeStruct(quarter, F32)] * 2
+        + [jax.ShapeDtypeStruct((2,) + quarter, BF)] * 2,
+        in_specs=[VM] * 5 + [ANY] * 19,
+        out_specs=[ANY] * 12,
         scratch_shapes=[pltpu.VMEM((planes, 2, 2) + quarter, BF)] * 2
         + [pltpu.VMEM((planes, 2) + quarter, BF)] * 2
         + [pltpu.VMEM((planes,) + quarter, BF)] * 2
-        + [pltpu.VMEM((planes - 1,) + quarter, BF)] * 2
+        + [pltpu.VMEM(quarter, BF)] * 2
         + [hold(2 * tokens, F32)] * 2
         + [hold(tokens, BF)] * 4
         + [hold(tokens, F32), hold(tokens, F32), hold(tokens, BF), hold(tokens, F32)]
@@ -1119,9 +1236,9 @@
             pltpu.VMEM((planes - 1, 8, 1024), F32),
             few,
             pltpu.VMEM(quarter, F32),
-            pltpu.VMEM(quarter[::-1], F32),
-            sems((24,)),
-            sems((10,)),
+            pltpu.VMEM(quarter, F32),
+            sems((23,)),
+            sems((14,)),
             sems((planes, 2, 3, 2)),
             sems((3 + planes, 2)),
         ],
@@ -1234,6 +1351,10 @@
     x_ref,
     da_ref,
     gmid_ref,
+    part1_ref,
+    part2_ref,
+    rest1_ref,
+    rest2_ref,
     grad_out,
     sums_out,
     own_output,
@@ -1241,6 +1362,8 @@
     own_recept,
     own_value,
     own_key,
+    own_hidden,
+    own_return,
     left_s,
     right_s,
     w_s,
@@ -1263,6 +1386,11 @@
     out_sem,
     rs_sem,
     s_sem,
+    ff_far,
+    ff_total,
+    own1_s,
+    own2_s,
+    ff_sem,
 ):
     at = Place(planes)
     tokens = micros * rows
@@ -1308,23 +1436,42 @@
         )
         for index in range(5)
     ]
+    ff_loads = [load(part1_ref, ff_total.at[0]), load(part2_ref, ff_total.at[1])]
+    ff_copies = [
+        remote(rest.at[slot], ff_far.at[slot, index], ff_sem.at[slot, index, 0], ff_sem.at[slot, index, 1], at.plane(planes - 2 + slot))
+        for slot in (1, 0)
+        for index, rest in enumerate((rest1_ref, rest2_ref))
+    ]
+    for copy in ff_copies:
+        copy.start()
     sums_s[...] = jnp.zeros_like(sums_s)
-    for index, reduce in enumerate(reduces):
+    def fill(index):
         for copy in side_loads[index]:
             copy.wait()
-        reduce.fill(left_s.at[index], right_s.at[index])
-        if index:
-            reduces[index - 1].begin()
-    for index, copy in enumerate(w_loads):
-        copy.wait()
+        reduces[index].fill(left_s.at[index], right_s.at[index])
+
+    def back(index):
+        w_loads[index].wait()
 
         @pl.loop(0, 2)
-        def _(i, index=index):
+        def _(i):
             span = tile(i, tokens // 2)
             g_s[index, span, :] = dot(right_s[2 + index, span, :], w_s[index], NT)
 
-        if index == 0:
-            reduces[4].begin()
+    fill(0)
+    fill(1)
+    reduces[0].begin()
+    fill(2)
+    reduces[1].begin()
+    fill(3)
+    fill(4)
+    back(0)
+    back(1)
+    reduces[0].middle()
+    reduces[1].middle()
+    reduces[2].begin()
+    reduces[3].begin()
+    back(2)
     for copy in row_loads:
         copy.wait()
     block = 16
@@ -1364,37 +1511,49 @@
     flat_s[0] = sums_ref[...]
     for index, row in enumerate((4, 5, 6, 0, 1)):
         flat_s[0, row : row + 1, :] = jnp.sum(sums_s[index], axis=0, keepdims=True)
-    for step, device in enumerate((at.other, at.side_x, at.side_y)):
-        copy = remote(flat_s.at[step], flat_recv.at[step], s_sem.at[1 + step, 0], s_sem.at[1 + step, 1], device)
-        copy.start()
-        if step == 0:
-            reduces[0].middle()
-            reduces[1].middle()
-        copy.wait()
-        flat_s[step + 1] = flat_s[step] + flat_recv[step]
-    flat_copies = [
-        remote(
-            flat_s.at[3],
-            flat_recv.at[2 + step],
-            s_sem.at[3 + step, 0],
-            s_sem.at[3 + step, 1],
-            at.plane(step),
+
+    def flat_copy(level, slot, device):
+        return remote(
+            flat_s.at[level], flat_recv.at[slot], s_sem.at[1 + slot, 0], s_sem.at[1 + slot, 1], device
         )
-        for step in range(1, planes)
-    ]
+
+    over_core = flat_copy(0, 0, at.other)
+    over_core.start()
+    reduces[0].last()
+    reduces[1].last()
+    reduces[4].begin()
+    over_core.wait()
+    flat_s[1] = flat_s[0] + flat_recv[0]
+    flat_copies = [flat_copy(1, step, at.plane(step)) for step in range(1, planes)]
     for copy in flat_copies:
         copy.start()
+    for copy in flat_copies:
+        copy.wait()
+    flat_s[2] = flat_s[1] + sum(flat_recv[step] for step in range(1, planes))
     reduces[2].middle()
     reduces[3].middle()
-    reduces[0].last()
-    reduces[1].last()
+    over_x = flat_copy(2, planes, at.side_x)
+    over_x.start()
+    over_x.wait()
+    flat_s[3] = flat_s[2] + flat_recv[planes]
+    over_y = flat_copy(3, planes + 1, at.side_y)
+    over_y.start()
     reduces[4].middle()
     reduces[2].last()
     reduces[3].last()
-    for copy in flat_copies:
+    over_y.wait()
+    flat_s[0] = flat_s[3] + flat_recv[planes + 1]
+    put(flat_s.at[0], sums_out)
+    for copy in ff_loads + ff_copies:
         copy.wait()
-    flat_s[0] = flat_s[3] + sum(flat_recv[2 + step] for step in range(1, planes))
-    put(flat_s.at[0], sums_out)
+    totals = [
+        ff_total[index] + ff_far[0, index].astype(F32) + ff_far[1, index].astype(F32)
+        for index in range(2)
+    ]
+    own1_s[...] = totals[0]
+    own2_s[...] = totals[1].T
+    put(own1_s, own_hidden)
+    put(own2_s, own_return)
     reduces[4].last()
     for index, target in enumerate((own_output, own_gate, own_recept, own_value, own_key)):
         own_s[index] = reduces[index].close()
@@ -1409,6 +1568,7 @@
     def hold(count, kind):
         return pltpu.VMEM((count, tokens, 1024), kind)
 
+    quarter = operands[-4].shape
     piece = (1024 // (8 * planes), 1024)
     sems = pltpu.SemaphoreType.DMA
     few = pltpu.VMEM((8, 1024), F32)
@@ -1418,9 +1578,10 @@
             jax.ShapeDtypeStruct((tokens, 1024), F32),
             jax.ShapeDtypeStruct((16, 1024), F32),
         ]
-        + [jax.ShapeDtypeStruct(piece, F32)] * 5,
-        in_specs=[VM] * 3 + [ANY] * 16,
-        out_specs=[ANY] * 7,
+        + [jax.ShapeDtypeStruct(piece, F32)] * 5
+        + [jax.ShapeDtypeStruct(quarter, F32), jax.ShapeDtypeStruct(quarter[::-1], F32)],
+        in_specs=[VM] * 3 + [ANY] * 20,
+        out_specs=[ANY] * 9,
         scratch_shapes=[
             hold(5, BF),
             hold(5, BF),
@@ -1440,10 +1601,15 @@
             few,
             pltpu.VMEM((4, 16, 1024), F32),
             pltpu.VMEM((2 + planes, 16, 1024), F32),
-            sems((16,)),
-            sems((7,)),
+            sems((18,)),
+            sems((9,)),
             sems((5, 2 + planes, 2)),
             sems((3 + planes, 2)),
+            pltpu.VMEM((2, 2) + quarter, BF),
+            pltpu.VMEM((2,) + quarter, F32),
+            pltpu.VMEM(quarter, F32),
+            pltpu.VMEM(quarter[::-1], F32),
+            sems((2, 2, 2)),
         ],
         compiler_params=pltpu.CompilerParams(
             collective_id=2, has_side_effects=True, vmem_limit_bytes=62 << 20
@@ -1784,6 +1950,35 @@
     )
 
 
+def hand_over(count, *refs):
+    sems = refs[3 * count]
+    ins, outs = ([], [])
+    for index in range(count):
+        held = refs[2 * count + index]
+        ins.append(pltpu.make_async_copy(refs[index], held, sems.at[0, index]))
+        outs.append(pltpu.make_async_copy(held, refs[count + index], sems.at[1, index]))
+        ins[-1].start()
+    for index in range(count):
+        ins[index].wait()
+        outs[index].start()
+    for copy in outs:
+        copy.wait()
+
+
+def hand_call(arrays):
+    count = len(arrays)
+    return pl.pallas_call(
+        functools.partial(hand_over, count),
+        out_shape=[jax.ShapeDtypeStruct(part.shape, part.dtype) for part in arrays],
+        in_specs=[ANY] * count,
+        out_specs=[ANY] * count,
+        scratch_shapes=[pltpu.VMEM(part.shape, part.dtype) for part in arrays]
+        + [pltpu.SemaphoreType.DMA((2, count))],
+        compiler_params=pltpu.CompilerParams(vmem_limit_bytes=60 << 20),
+        name="hand_over",
+    )(*arrays)
+
+
 def kernel_body(
     incoming_signal,
     series_number_table,
@@ -1808,24 +2003,6 @@
     feedforward_admit_matrix,
 ):
     hidden_full, return_full = (feedforward_lookup_matrix, feedforward_content_matrix)
-    vectors = tuple(
-        (
-            start_item.astype(jnp.float32)
-            for start_item in (
-                first_scaling_factor,
-                first_scaling_offset,
-                logarithmic_fading_speeds,
-                present_step_extra,
-                lookup_shift_mixture,
-                content_shift_mixture,
-                admit_lookup_shift_mixture,
-                second_scaling_factor,
-                second_scaling_offset,
-                inner_shift_mixture,
-                admit_shift_mixture,
-            )
-        )
-    )
     matrices = (
         attention_lookup_matrix,
         attention_content_matrix,
@@ -1835,49 +2012,67 @@
     )
     micros, _, rows, depth = incoming_signal.shape
     planes = lax.axis_size("mp") // 2
-    numbers = series_number_table[:, 0].astype(jnp.float32)
-    firsts, lasts = (numbers[:, :1], numbers[:, -1:])
+    x = incoming_signal.reshape(micros * rows, depth)
+    adjoint = upstream_adjoint.reshape(micros * rows, depth)
     operands = (
-        incoming_signal.reshape(micros * rows, depth),
-        jnp.pad(incoming_signal[:, 0, -1].astype(jnp.float32), ((0, 8 - micros), (0, 0))),
-        jnp.broadcast_to(numbers.reshape(-1, 1), (micros * rows, 128)),
-        jnp.pad(numbers, ((0, 8 - micros), (0, 0))),
-        jnp.broadcast_to(
-            jnp.concatenate([lasts, lasts, firsts, firsts], axis=0), (4 * micros, 128)
-        ),
-        jnp.pad(jnp.stack(vectors), ((0, 5), (0, 0))),
-        upstream_adjoint.reshape(micros * rows, depth),
+        x,
+        series_number_table.reshape(micros, rows),
+        adjoint,
+        first_scaling_factor,
+        first_scaling_offset,
+        logarithmic_fading_speeds,
+        present_step_extra,
+        lookup_shift_mixture,
+        content_shift_mixture,
+        admit_lookup_shift_mixture,
+        second_scaling_factor,
+        second_scaling_offset,
+        inner_shift_mixture,
+        admit_shift_mixture,
         *matrices,
         hidden_full,
         return_full,
     )
     (
         keys, values, recept, num, den, mid, gate, mk, mv, mr, gated, mg, delta_a, delta_b,
-        keep, segs, mh_all, ret_all, w1_all, w2_all,
+        keep, segs, table, segcol, segrow, mh_all, ret_all, w1_all, w2_all, ret_acc, gmh_acc,
+        parts1, parts2,
     ) = forward_call(planes, micros, rows, operands)
-    x, _, segcol, segrow, _, table, adjoint = operands[:7]
     key_w, value_w, recept_w, output_w, gate_w = matrices
     (
         output, grad_mid, grad_gate, grad_att, grad_recept, grad_key, grad_value, sums,
-        own_hidden, own_return,
+        part1, part2, rest1, rest2,
     ) = middle_call(
         planes,
         micros,
         rows,
         (
-            table, keep, segs, segcol, segrow, hidden_full, return_full, w1_all, w2_all,
-            mh_all, ret_all, mid, gate, adjoint, delta_b, keys, values, recept, num, den,
+            table, keep, segs, segcol, segrow, w1_all, w2_all, mh_all, ret_all, ret_acc, gmh_acc,
+            parts1, parts2, mid, gate, adjoint, delta_b, keys, values, recept, num, den,
             gate_w, output_w,
         ),
     )
-    input_grad, sums, own_output, own_gate, own_recept, own_value, own_key = last_call(
+    (
+        input_grad, sums, own_output, own_gate, own_recept, own_value, own_key, own_hidden,
+        own_return,
+    ) = last_call(
         planes,
         micros,
         rows,
         (
             table, keep, sums, gated, grad_att, mg, grad_gate, mr, grad_recept, mv, grad_value,
             mk, grad_key, recept_w, value_w, key_w, x, delta_a, grad_mid,
+            part1, part2, rest1, rest2,
         ),
+    )
+    (
+        output, input_grad, own_key, own_value, own_recept, own_output, own_hidden, own_return,
+        own_gate,
+    ) = hand_call(
+        (
+            output, input_grad, own_key, own_value, own_recept, own_output, own_hidden,
+            own_return, own_gate,
+        )
     )
     span = depth // (lax.axis_size("dp") * lax.axis_size("mp"))
     mine = lax.dynamic_slice_in_dim(

time: 332 us -> 252 us (0.76)
  Pallas kernels: 307 us -> 249 us
  local copies, waits for them, and re-layouts: 22 us -> 1.62 us
    pallas_call x1, Pallas kernels: 123 us -> 80.1 us  [middle_call(): pl.pallas_call(functools.partial(middle_kernel, planes, micros, rows), ou...]
    pallas_call x1, Pallas kernels: 93.1 us -> 80.5 us  [forward_call(): pl.pallas_call(functools.partial(forward_kernel, planes, micros, rows), o...]
    unnamed x26 -> x0, local copies, waits for them, and re-layouts: 9.53 us -> none
    another operation x12 -> x0, local copies, waits for them, and re-layouts: 7.63 us -> none  [kernel_body(): jnp.stack(vectors)]
    pallas_call x1, Pallas kernels: 90.8 us -> 84.4 us  [last_call(): pl.pallas_call(functools.partial(last_kernel, planes, micros, rows), out_...]
    pallas_call x0 -> x1, Pallas kernels: none -> 4.26 us  [hand_call(): pl.pallas_call(functools.partial(hand_over, count), out_shape=[jax.ShapeD...]
where the time goes in v4:
time: 252 us
  Pallas kernels  249 us (99%)
    pallas_call x1, Pallas kernels, last_call(): pl.pallas_call(functools.partial(last_kernel, planes, micros, rows), out_...  84.4 us
    pallas_call x1, Pallas kernels, forward_call(): pl.pallas_call(functools.partial(forward_kernel, planes, micros, rows), o...  80.5 us
    pallas_call x1, Pallas kernels, middle_call(): pl.pallas_call(functools.partial(middle_kernel, planes, micros, rows), ou...  80.1 us

profile of v4, /device:TPU:0, one launch (start us, length us, event | category | flops | bytes accessed | tf_op | source)
XLA Modules:
  0.0 251.8 jit_solution(7136187311286441667)
XLA Ops:
  0.7 80.5 %time_mix_forward.1 = (f32[512,1024]{1,0:T(8,128)}, f32[512,1024]{1,0:T(8,128)}, f32[512,1024]{1,0:T(8,128)}, f32[512,1024]{1,0:T(8,128)}, f32[512,1024]{1,0:T(8...) custom-call(bf16[512,1024]{1,0:T(8,128)(2,1)} %bitcast.35, ...), custom_call_target="tpu_custom_call" | custom-call | flops 19327352832 | bytes 41943040 | tf_op jit(solution)/shard_map/time_mix_forward/pallas_call | solution.py:667
  81.2 80.1 %channel_mix_and_adjoint.1 = (f32[512,1024]{1,0:T(8,128)}, f32[512,1024]{1,0:T(8,128)}, bf16[512,1024]{1,0:T(8,128)(2,1)}, bf16[512,1024]{1,0:T(8,128)(2,1)}, bf...) custom-call(f32[16,1024]{1,0:T(8,128)} %get-tuple-element.77.vec_ref, ...), custom_call_target="tpu_custom_call" | custom-call | flops 27917287424 | bytes 62914560 | tf_op jit(solution)/shard_map/channel_mix_and_adjoint/pallas_call | solution.py:1211
  161.3 84.4 %time_mix_weights.1 = (f32[512,1024]{1,0:T(8,128)}, f32[16,1024]{1,0:T(8,128)}, f32[32,1024]{1,0:T(8,128)}, f32[32,1024]{1,0:T(8,128)}, f32[32,1024]{1,0:T(8,128...) custom-call(f32[16,1024]{1,0:T(8,128)} %get-tuple-element.77.vec_ref, ...), custom_call_target="tpu_custom_call" | custom-call | flops 8589934592 | bytes 31457280 | tf_op jit(solution)/shard_map/time_mix_weights/pallas_call | solution.py:1575
  245.8 4.3 %hand_over.1 = (f32[512,1024]{1,0:T(8,128)}, f32[512,1024]{1,0:T(8,128)}, f32[32,1024]{1,0:T(8,128)}, f32[32,1024]{1,0:T(8,128)}, f32[32,1024]{1,0:T(8,128)}, /*...) custom-call(f32[512,1024]{1,0:T(8,128)} %get-tuple-element.98.refs_0_, ...), custom_call_target="tpu_custom_call" | custom-call | tf_op jit(solution)/shard_map/hand_over/pallas_call | solution.py:1970
  250.0 1.6 dynamic-slice_bitcast_fusion

commit v5 on v4

--- a/solution.py
+++ b/solution.py
@@ -341,11 +341,40 @@
     ):
         loads.append(pltpu.make_async_copy(source, target, w_sem.at[index]))
         loads[-1].start()
-    for copy in z_copies[0] + z_copies[2]:
+    for copy in z_copies[0]:
         copy.start()
     halo_copy.wait()
     for copy in seg_copies:
         copy.wait()
+
+    def along(step):
+        group = []
+        own1, own2 = (w1_all.at[step, q1], w2_all.at[step, q2])
+        return (
+            remote(own1, own1, z_sem.at[step, 2, 0], z_sem.at[step, 2, 1], at.side_x),
+            remote(own2, own2, z_sem.at[step, 3, 0], z_sem.at[step, 3, 1], at.side_y),
+        )
+
+    def across(step):
+        both1 = w1_all.at[step, half1]
+        own2 = w2_all.at[step, q2]
+        next2 = w2_all.at[step, far2]
+        return (
+            remote(both1, both1, z_sem.at[step, 4, 0], z_sem.at[step, 4, 1], at.side_y),
+            remote(own2, own2, z_sem.at[step, 5, 0], z_sem.at[step, 5, 1], at.side_x),
+            remote(next2, next2, z_sem.at[step, 6, 0], z_sem.at[step, 6, 1], at.side_x),
+        )
+
+    def start(group):
+        for copy in group:
+            copy.start()
+
+    def finish(group):
+        for copy in group:
+            copy.wait()
+
+    along_0, along_2 = (along(0), along(2))
+    across_0, across_1, across_2 = (across(0), across(1), across(2))
 
     before = lax.rem(mp + at.count - 1, at.count)
     has_before = mp > 0
@@ -365,7 +394,7 @@
             here == segrow_ref[m : m + 1, :], col_at < row_at
         ).astype(F32).astype(BF)
 
-    block = 16
+    block = 32
     at_first = lax.broadcasted_iota(jnp.int32, (block, 1024), 0) == 0
     gain, bias = (vec_ref[0:1, :], vec_ref[1:2, :])
     near_a[...] = unit_of(halo_a[...])[0] * gain + bias
@@ -384,7 +413,7 @@
             mr_s[span, :] = (shifted + delta * vec_ref[6:7, :]).astype(BF)
             return normed[block - 1 : block, :]
 
-        lax.fori_loop(0, rows // block, mix_a, near_a[m : m + 1, :])
+        lax.fori_loop(0, rows // block, mix_a, near_a[m : m + 1, :], unroll=2)
 
     outs = []
 
@@ -437,39 +466,10 @@
     put(v_s, v_out)
     core_copy = remote(state_own, state_other, s_sem.at[0, 0], s_sem.at[0, 1], at.other)
     core_copy.start()
-    for copy in z_copies[0]:
-        copy.wait()
-    xy_copies = []
-
-    def along(step):
-        group = []
-        own1, own2 = (w1_all.at[step, q1], w2_all.at[step, q2])
-        return (
-            remote(own1, own1, z_sem.at[step, 2, 0], z_sem.at[step, 2, 1], at.side_x),
-            remote(own2, own2, z_sem.at[step, 3, 0], z_sem.at[step, 3, 1], at.side_y),
-        )
-
-    def across(step):
-        both1 = w1_all.at[step, half1]
-        own2 = w2_all.at[step, q2]
-        next2 = w2_all.at[step, far2]
-        return (
-            remote(both1, both1, z_sem.at[step, 4, 0], z_sem.at[step, 4, 1], at.side_y),
-            remote(own2, own2, z_sem.at[step, 5, 0], z_sem.at[step, 5, 1], at.side_x),
-            remote(next2, next2, z_sem.at[step, 6, 0], z_sem.at[step, 6, 1], at.side_x),
-        )
-
-    def start(group):
-        for copy in group:
-            copy.start()
-
-    def finish(group):
-        for copy in group:
-            copy.wait()
-
-    along_0, along_2 = (along(0), along(2))
-    across_0, across_1, across_2 = (across(0), across(1), across(2))
+    finish(z_copies[0])
     start(along_0)
+    z_copies[2][0].start()
+
     loads[2].wait()
 
     @pl.loop(0, 2)
@@ -494,10 +494,10 @@
         for step in range(1, planes)
     ]
     start(chip_copies)
+    finish(chip_copies)
+    z_copies[2][1].start()
     finish(along_0)
     start(across_0)
-    finish(chip_copies)
-    onward_1.start()
     total = jnp.zeros_like(state_chip[...])
     power = jnp.ones_like(decay_all)
     for step in range(1, planes):
@@ -529,8 +529,6 @@
             den_s[span, cols] = den
             gated_s[span, cols] = (r_s[span, cols] * mixed).astype(BF)
 
-    finish(z_copies[2])
-    start(along_2)
     put(num_s, num_out)
     put(den_s, den_out)
     put(gated_s, gated_out)
@@ -561,7 +559,10 @@
             norm_b(b)
 
     halo_b_copy.wait()
+    onward_1.start()
     start(onward_2)
+    finish(z_copies[2])
+    start(along_2)
     for m in range(micros):
 
         def mix_b(b, prev, m=m):
@@ -576,7 +577,7 @@
             mg_s[span, :] = (shifted + delta * vec_ref[10:11, :]).astype(BF)
             return normed[block - 1 : block, :]
 
-        lax.fori_loop(0, rows // block, mix_b, halo_b[m : m + 1, :])
+        lax.fori_loop(0, rows // block, mix_b, halo_b[m : m + 1, :], unroll=2)
 
     own, far = (slice(0, tokens), slice(tokens, 2 * tokens))
     mh_copy = remote(
@@ -599,8 +600,6 @@
     )
     ret_copy.start()
     put(gate_s, gate_out)
-    finish(along_2)
-    start(across_2)
     hidden = w1_ref.shape[1]
     w1_own, w2_own = (wk.at[:, 0:hidden], wv.at[0:hidden])
     w1_next, w2_next = (wk.at[:, hidden : 2 * hidden], wv.at[hidden : 2 * hidden])
@@ -619,23 +618,28 @@
     pl.loop(0, half)(step)
     mh_copy.wait()
     ret_copy.wait()
+    finish(along_2)
+    start(across_2)
     put(mh2, mh_all)
     put(gr2, ret_all)
     finish(across_0)
     ff_loads[2].start()
     ff_loads[3].start()
     pl.loop(half, 2 * half)(step)
-    finish(onward_2)
+    feed_grads(mh2, gr2, sq_s, gp_s, parts1.at[0], parts2.at[0])
     onward_1.wait()
-    start(across_1)
-    feed_grads(mh2, gr2, sq_s, gp_s, parts1.at[0], parts2.at[0])
+    across_1[0].start()
     put(parts1.at[0], parts1_out.at[0])
     put(parts2.at[0], parts2_out.at[0])
     ff_loads[2].wait()
     ff_loads[3].wait()
-    pl.loop(0, 2 * half)(
-        feed_rows(w1_next, w2_next, mh2, gr2, sq_s, gp_s, ret_acc, gmh_acc, False)
-    )
+    step = feed_rows(w1_next, w2_next, mh2, gr2, sq_s, gp_s, ret_acc, gmh_acc, False)
+    pl.loop(0, half)(step)
+    onward_2[0].wait()
+    across_1[1].start()
+    pl.loop(half, 2 * half)(step)
+    onward_2[1].wait()
+    across_1[2].start()
     put(ret_acc, ret_acc_out)
     put(gmh_acc, gmh_acc_out)
     feed_grads(mh2, gr2, sq_s, gp_s, parts1.at[1], parts2.at[1])
@@ -792,6 +796,30 @@
     )
 
 
+def fill_square(parts, left, right, planes, split):
+    @pl.loop(0, 4)
+    def _(q):
+        line, side = (lax.div(q, 2), lax.rem(q, 2))
+        made = dot(left[:, tile(q, 256)], right[...], TN).astype(BF)
+        pieces = made.reshape(planes, 2, 256 // (2 * planes), 1024)
+        for core in range(2):
+            if split > 0:
+                parts[core, side, line, :, :, 0:split] = pieces[:, core, :, 0:split]
+            if split < 1024:
+                parts[core, line, side, :, :, split:1024] = pieces[:, core, :, split:1024]
+
+
+def add_square(mine, other, planes):
+    for one in range(2):
+        for two in range(2):
+
+            @pl.loop(0, planes)
+            def _(i):
+                mine[one, two, i] = (
+                    mine[one, two, i].astype(F32) + other[one, two, i].astype(F32)
+                ).astype(BF)
+
+
 def middle_kernel(
     planes,
     micros,
@@ -820,6 +848,8 @@
     den_ref,
     gate_w,
     output_w,
+    gated_ref,
+    mg_ref,
     out_ref,
     gmid_out,
     ggp_out,
@@ -832,6 +862,7 @@
     own2_out,
     rest1_out,
     rest2_out,
+    square_out,
     parts1,
     parts2,
     first1,
@@ -860,12 +891,13 @@
     state_chip,
     state_in,
     carry_s,
-    own1_s,
-    own2_s,
     load_sem,
     out_sem,
     rs_sem,
     s_sem,
+    square_parts,
+    square_across,
+    square_sem,
 ):
     at = Place(planes)
     dp, mp, z, core = (at.dp, at.mp, at.z, at.core)
@@ -896,9 +928,9 @@
         reduces.append(
             (
                 Reduce(at, parts1.at[slot], first1.at[slot], second1.at[slot],
-                       far1 if slot == 1 else None, rs_sem.at[slot, 0], slot, True),
+                       far1.at[slot // 2] if slot % 2 else None, rs_sem.at[slot, 0], slot, True),
                 Reduce(at, parts2.at[slot], first2.at[slot], second2.at[slot],
-                       far2 if slot == 1 else None, rs_sem.at[slot, 1], slot, False),
+                       far2.at[slot // 2] if slot % 2 else None, rs_sem.at[slot, 1], slot, False),
             )
         )
     ret_copy = remote(ret_send, ret_recv, s_sem.at[0, 0], s_sem.at[0, 1], at.other)
@@ -960,7 +992,7 @@
             feed_grads(mh2, gr2, sq_s, gp_s, parts1.at[slot], parts2.at[slot])
             if index == 0:
                 middle(1)
-            begin(slot)
+                begin(slot)
         for copy in late:
             copy.wait()
 
@@ -975,7 +1007,7 @@
     )
     own = slice(0, tokens)
     far = slice(tokens, 2 * tokens)
-    block = 16
+    block = 32
 
     def attention(k_s, v_s, r_s, num_s, den_s, wg, wo, ggp_s, gatt_s, grp_s, gk_s, gv_s):
         need_wg = load(gate_w, wg)
@@ -996,6 +1028,7 @@
                 col_at > row_at,
             ).astype(F32).astype(BF)
         ret_copy.wait()
+        need_gated = load(gated_ref, ret_send)
 
         @pl.loop(0, tokens // block)
         def _(b):
@@ -1018,6 +1051,7 @@
         middle(0)
         gmg = ret_acc.at[far]
         gmh_copy.wait()
+        need_mg = load(mg_ref, gmh_send)
         mix_h, mix_g = (vec_ref[9:10, :], vec_ref[10:11, :])
         gain = vec_ref[7:8, :]
 
@@ -1053,7 +1087,7 @@
                 gatt_s[span, :] = total.astype(BF)
                 return shift[0:1, :]
 
-            lax.fori_loop(0, rows // block, back_b, halo_b[m : m + 1, :])
+            lax.fori_loop(0, rows // block, back_b, halo_b[m : m + 1, :], unroll=2)
 
         put(gmh_acc.at[own], gmid_out)
         put(gatt_s, gatt_out)
@@ -1101,6 +1135,8 @@
         put(grp_s, grp_out)
         core_copy = remote(state_own, state_other, s_sem.at[3, 0], s_sem.at[3, 1], at.other)
         core_copy.start()
+        middle(3)
+        begin(2)
         pair = lax.div(mp, 2) * 2
         decay_all = jnp.exp(-float(rows) * jnp.exp(vec_ref[2:3, :]))
 
@@ -1135,7 +1171,6 @@
             seen(pair + 1, False) == seen(pair, True), state_other[...], 0.0
         )
         carry_s[...] = jnp.where(core == 0, joined, total)
-        middle(3)
         last(0)
 
         @pl.loop(0, 1024 // width)
@@ -1171,20 +1206,43 @@
         for index in range(16):
             sums_flat[index : index + 1, :] = jnp.sum(sums_s[index], axis=0, keepdims=True)
         put(sums_flat, sums_out)
-        for reduce in reduces[1]:
-            reduce.close()
+        last(3)
+        need_gated.wait()
+        need_mg.wait()
+        square_copies = []
+        for index, (left, right) in enumerate(((ret_send, gatt_s), (gmh_send, ggp_s))):
+            fill_square(square_parts.at[index], left, right, planes, 1024 * (1 - index))
+            square_copies.append(
+                remote(
+                    square_parts.at[index, 1 - core],
+                    square_across.at[index],
+                    square_sem.at[index, 0],
+                    square_sem.at[index, 1],
+                    at.other,
+                )
+            )
+            square_copies[index].start()
+        for index in range(2):
+            square_copies[index].wait()
+            add_square(square_parts.at[index, core], square_across.at[index], planes)
+            put(square_parts.at[index, core], square_out.at[index])
         middle(2)
-        last(3)
-        for parts, far_parts, own_s, own_out, rest_out, one, two in (
-            (parts1, far1, own1_s, own1_out, rest1_out, lax.rem(dp, 2), lax.div(dp, 2)),
-            (parts2, far2, own2_s, own2_out, rest2_out, lax.div(dp, 2), lax.rem(dp, 2)),
+        for slot in (1, 3):
+            for reduce in reduces[slot]:
+                reduce.close()
+        for parts, far_parts, own_s, own_out, one, two in (
+            (parts1, far1, mid_s, own1_out, lax.rem(dp, 2), lax.div(dp, 2)),
+            (parts2, far2, gate_s, own2_out, lax.div(dp, 2), lax.rem(dp, 2)),
         ):
-            own_s[...] = parts[0, one, two].astype(F32) + far_parts[...].astype(F32)
-            put(own_s, own_out)
-            put(parts.at[3, one, two], rest_out.at[1])
+            own_s[0:256, 0:hidden] = (
+                parts[0, one, two].astype(F32)
+                + far_parts[0].astype(F32)
+                + far_parts[1].astype(F32)
+            )
+            put(own_s.at[0:256, 0:hidden], own_out)
         last(2)
-        put(parts1.at[2, lax.rem(dp, 2), lax.div(dp, 2)], rest1_out.at[0])
-        put(parts2.at[2, lax.div(dp, 2), lax.rem(dp, 2)], rest2_out.at[0])
+        put(parts1.at[2, lax.rem(dp, 2), lax.div(dp, 2)], rest1_out)
+        put(parts2.at[2, lax.div(dp, 2), lax.rem(dp, 2)], rest2_out)
         for copy in outs:
             copy.wait()
 
@@ -1207,6 +1265,7 @@
 
     few = hold(8, F32)
     quarter = (256, hidden)
+    piece = (planes, 256 // (2 * planes), 1024)
     sems = pltpu.SemaphoreType.DMA
     return pl.pallas_call(
         functools.partial(middle_kernel, planes, micros, rows),
@@ -1214,13 +1273,14 @@
         + [big(BF)] * 5
         + [jax.ShapeDtypeStruct((16, 1024), F32)]
         + [jax.ShapeDtypeStruct(quarter, F32)] * 2
-        + [jax.ShapeDtypeStruct((2,) + quarter, BF)] * 2,
-        in_specs=[VM] * 5 + [ANY] * 19,
-        out_specs=[ANY] * 12,
+        + [jax.ShapeDtypeStruct(quarter, BF)] * 2
+        + [jax.ShapeDtypeStruct((2, 2, 2) + piece, BF)],
+        in_specs=[VM] * 5 + [ANY] * 21,
+        out_specs=[ANY] * 13,
         scratch_shapes=[pltpu.VMEM((planes, 2, 2) + quarter, BF)] * 2
         + [pltpu.VMEM((planes, 2) + quarter, BF)] * 2
         + [pltpu.VMEM((planes,) + quarter, BF)] * 2
-        + [pltpu.VMEM(quarter, BF)] * 2
+        + [pltpu.VMEM((2,) + quarter, BF)] * 2
         + [hold(2 * tokens, F32)] * 2
         + [hold(tokens, BF)] * 4
         + [hold(tokens, F32), hold(tokens, F32), hold(tokens, BF), hold(tokens, F32)]
@@ -1235,12 +1295,13 @@
             few,
             pltpu.VMEM((planes - 1, 8, 1024), F32),
             few,
-            pltpu.VMEM(quarter, F32),
-            pltpu.VMEM(quarter, F32),
-            sems((23,)),
+            sems((25,)),
             sems((14,)),
             sems((planes, 2, 3, 2)),
             sems((3 + planes, 2)),
+            pltpu.VMEM((2, 2, 2, 2) + piece, BF),
+            pltpu.VMEM((2, 2, 2) + piece, BF),
+            sems((2, 2)),
         ],
         compiler_params=pltpu.CompilerParams(
             collective_id=1, has_side_effects=True, vmem_limit_bytes=62 << 20
@@ -1253,44 +1314,26 @@
 
 
 class ReduceSquare:
-    def __init__(self, at, parts, across, first, second, far, sems, x_first):
-        self.at, self.across, self.first, self.second, self.far = (at, across, first, second, far)
-        self.x_first = x_first
+    def __init__(self, at, mine, first, second, far, sems, x_first):
+        self.at, self.mine, self.first, self.second, self.far = (at, mine, first, second, far)
         side = lax.rem(at.dp, 2)
         line = lax.div(at.dp, 2)
         self.one, self.two = (side, line) if x_first else (line, side)
         near, next_to = (at.side_x, at.side_y) if x_first else (at.side_y, at.side_x)
-        self.parts = parts
-        self.mine = parts.at[at.core]
-        self.copy_0 = remote(parts.at[1 - at.core], across, sems.at[0, 0], sems.at[0, 1], at.other)
-        self.copy_1 = remote(self.mine.at[1 - self.one], first, sems.at[1, 0], sems.at[1, 1], near)
+        self.copy_1 = remote(mine.at[1 - self.one], first, sems.at[0, 0], sems.at[0, 1], near)
         self.copy_2 = remote(
-            self.mine.at[self.one, 1 - self.two], second, sems.at[2, 0], sems.at[2, 1], next_to
+            mine.at[self.one, 1 - self.two], second, sems.at[1, 0], sems.at[1, 1], next_to
         )
         self.copies_3 = [
             remote(
-                self.mine.at[self.one, self.two, lax.rem(at.z + step, at.planes)],
+                mine.at[self.one, self.two, lax.rem(at.z + step, at.planes)],
                 far.at[step - 1],
-                sems.at[2 + step, 0],
-                sems.at[2 + step, 1],
+                sems.at[1 + step, 0],
+                sems.at[1 + step, 1],
                 at.plane(step),
             )
             for step in range(1, at.planes)
         ]
-
-    def fill(self, left, right):
-        planes = self.at.planes
-
-        @pl.loop(0, 4)
-        def _(q):
-            line, side = (lax.div(q, 2), lax.rem(q, 2))
-            one, two = (side, line) if self.x_first else (line, side)
-            made = dot(left[:, tile(q, 256)], right[...], TN).astype(BF)
-            split = made.reshape(planes, 2, 256 // (2 * planes), 1024)
-            self.parts[0, one, two] = split[:, 0]
-            self.parts[1, one, two] = split[:, 1]
-
-        self.copy_0.start()
 
     def add(self, one, two, other):
         @pl.loop(0, self.at.planes)
@@ -1300,12 +1343,7 @@
             ).astype(BF)
 
     def begin(self):
-        self.copy_0.wait()
-        for two in range(2):
-            self.add(1 - self.one, two, self.across.at[1 - self.one, two])
         self.copy_1.start()
-        for two in range(2):
-            self.add(self.one, two, self.across.at[self.one, two])
 
     def middle(self):
         self.copy_1.wait()
@@ -1316,6 +1354,8 @@
     def last(self):
         self.copy_2.wait()
         self.add(self.one, self.two, self.second)
+
+    def send(self):
         for copy in self.copies_3:
             copy.start()
 
@@ -1335,10 +1375,7 @@
     vec_ref,
     keep_ref,
     sums_ref,
-    gated_ref,
-    gatt_ref,
-    mg_ref,
-    ggp_ref,
+    square_ref,
     mr_ref,
     grp_ref,
     mv_ref,
@@ -1391,6 +1428,8 @@
     own1_s,
     own2_s,
     ff_sem,
+    ready_s,
+    core_sem,
 ):
     at = Place(planes)
     tokens = micros * rows
@@ -1410,12 +1449,11 @@
         return copy
 
     sides = (
-        (gated_ref, gatt_ref),
-        (mg_ref, ggp_ref),
         (mr_ref, grp_ref),
         (mv_ref, gv_ref),
         (mk_ref, gk_ref),
     )
+    ready_load = load(square_ref, ready_s)
     side_loads = [
         (load(left, left_s.at[index]), load(right, right_s.at[index]))
         for index, (left, right) in enumerate(sides)
@@ -1429,53 +1467,92 @@
         + [at.plane(step) for step in range(1, planes)]
         + [at.ahead(1), at.ahead(-1)]
     )
-    reduces = [
-        ReduceSquare(
-            at, parts.at[index], across.at[index], first.at[index], second.at[index],
-            far.at[index], rs_sem.at[index], index % 2 == 0,
+    core = at.core
+    lefts, rights = (slice(0, 512), slice(512, 1024))
+    reduces = []
+    for index, (cols, x_first) in enumerate(
+        ((None, True), (None, False), (None, True), (None, False), (lefts, True), (rights, False))
+    ):
+        place = min(index, 4)
+        mine = ready_s.at[index] if index < 2 else parts.at[place - 2, core]
+        refs = (mine, first.at[place], second.at[place], far.at[place])
+        if cols is not None:
+            refs = (
+                mine.at[:, :, :, :, cols],
+                first.at[place, :, :, :, cols],
+                second.at[place, :, :, cols],
+                far.at[place, :, :, cols],
+            )
+        reduces.append(ReduceSquare(at, *refs, rs_sem.at[index], x_first))
+    core_copies = [
+        remote(
+            parts.at[index, 1 - core],
+            across.at[index],
+            core_sem.at[index, 0],
+            core_sem.at[index, 1],
+            at.other,
         )
-        for index in range(5)
+        for index in range(3)
     ]
     ff_loads = [load(part1_ref, ff_total.at[0]), load(part2_ref, ff_total.at[1])]
     ff_copies = [
-        remote(rest.at[slot], ff_far.at[slot, index], ff_sem.at[slot, index, 0], ff_sem.at[slot, index, 1], at.plane(planes - 2 + slot))
-        for slot in (1, 0)
+        remote(rest, ff_far.at[index], ff_sem.at[index, 0], ff_sem.at[index, 1], at.plane(2))
         for index, rest in enumerate((rest1_ref, rest2_ref))
     ]
+    ready_load.wait()
+    reduces[0].begin()
+    reduces[1].begin()
+    mixes = (vec_ref[6:7, :], vec_ref[5:6, :], vec_ref[4:5, :])
+    heads = jnp.zeros((16 * micros, 1024), F32)
+    for index in range(3):
+        side_loads[index][1].wait()
+        w_loads[index].wait()
+        picked = jnp.concatenate(
+            [right_s[index, m * rows : m * rows + 16, :] for m in range(micros)], axis=0
+        )
+        heads = heads + dot(picked, w_s[index], NT) * (1.0 - mixes[index])
+    for m in range(micros):
+        pay_a[m : m + 1, :] = heads[16 * m : 16 * m + 1] * wide(
+            keep_ref[m * rows : m * rows + 8, :], 1024
+        )[0:1]
+    pay_a[micros:, :] = jnp.zeros((8 - micros, 1024), F32)
+    halo_copy = remote(pay_a, halo_a, s_sem.at[0, 0], s_sem.at[0, 1], at.ahead(-1))
+    halo_copy.start()
     for copy in ff_copies:
         copy.start()
     sums_s[...] = jnp.zeros_like(sums_s)
-    def fill(index):
-        for copy in side_loads[index]:
-            copy.wait()
-        reduces[index].fill(left_s.at[index], right_s.at[index])
+
+    def fill(index, split):
+        side_loads[index][0].wait()
+        fill_square(parts.at[index], left_s.at[index], right_s.at[index], planes, split)
+        core_copies[index].start()
+
+    def settle(index):
+        core_copies[index].wait()
+        add_square(parts.at[index, core], across.at[index], planes)
 
     def back(index):
-        w_loads[index].wait()
-
         @pl.loop(0, 2)
         def _(i):
             span = tile(i, tokens // 2)
-            g_s[index, span, :] = dot(right_s[2 + index, span, :], w_s[index], NT)
-
-    fill(0)
-    fill(1)
-    reduces[0].begin()
-    fill(2)
-    reduces[1].begin()
-    fill(3)
-    fill(4)
+            g_s[index, span, :] = dot(right_s[index, span, :], w_s[index], NT)
+
+    fill(0, 1024)
+    fill(1, 0)
+    settle(0)
+    fill(2, 512)
+    settle(1)
     back(0)
-    back(1)
     reduces[0].middle()
     reduces[1].middle()
     reduces[2].begin()
     reduces[3].begin()
+    settle(2)
+    back(1)
     back(2)
     for copy in row_loads:
         copy.wait()
-    block = 16
-    mixes = (vec_ref[6:7, :], vec_ref[5:6, :], vec_ref[4:5, :])
+    block = 32
     gain = vec_ref[0:1, :]
 
     def combine(b):
@@ -1484,13 +1561,11 @@
         shift = sum(grad * (1.0 - mix) for grad, mix in zip(grads, mixes))
         return (span, grads, shift * wide(keep_ref[span, :], 1024))
 
-    for m in range(micros):
-        pay_a[m : m + 1, :] = combine(m * (rows // block))[2][0:1, :]
-    pay_a[micros:, :] = jnp.zeros((8 - micros, 1024), F32)
-    halo_copy = remote(pay_a, halo_a, s_sem.at[0, 0], s_sem.at[0, 1], at.ahead(-1))
-    halo_copy.start()
     at_last = lax.broadcasted_iota(jnp.int32, (block, 1024), 0) == block - 1
     halo_copy.wait()
+    for index in range(2):
+        reduces[index].last()
+        reduces[index].send()
     for m in range(micros):
 
         def back_a(i, after, m=m):
@@ -1506,7 +1581,7 @@
             total_s[span, :] = total_s[span, :] + norm_back_rows(grad, unit, inverse, gain)
             return shift[0:1, :]
 
-        lax.fori_loop(0, rows // block, back_a, halo_a[m : m + 1, :])
+        lax.fori_loop(0, rows // block, back_a, halo_a[m : m + 1, :], unroll=2)
     put(total_s, grad_out)
     flat_s[0] = sums_ref[...]
     for index, row in enumerate((4, 5, 6, 0, 1)):
@@ -1519,45 +1594,47 @@
 
     over_core = flat_copy(0, 0, at.other)
     over_core.start()
-    reduces[0].last()
-    reduces[1].last()
-    reduces[4].begin()
     over_core.wait()
     flat_s[1] = flat_s[0] + flat_recv[0]
-    flat_copies = [flat_copy(1, step, at.plane(step)) for step in range(1, planes)]
+    over_x = flat_copy(1, 1, at.side_x)
+    over_x.start()
+    reduces[2].middle()
+    reduces[3].middle()
+    over_x.wait()
+    flat_s[2] = flat_s[1] + flat_recv[1]
+    over_y = flat_copy(2, 2, at.side_y)
+    over_y.start()
+    reduces[4].begin()
+    reduces[5].begin()
+    for index in range(2, 4):
+        reduces[index].last()
+        reduces[index].send()
+    over_y.wait()
+    flat_s[3] = flat_s[2] + flat_recv[2]
+    flat_copies = [flat_copy(3, 2 + step, at.plane(step)) for step in range(1, planes)]
     for copy in flat_copies:
         copy.start()
+    for copy in ff_loads + ff_copies:
+        copy.wait()
+    own1_s[...] = ff_total[0] + ff_far[0].astype(F32)
+    own2_s[...] = (ff_total[1] + ff_far[1].astype(F32)).T
+    put(own1_s, own_hidden)
+    put(own2_s, own_return)
+    reduces[4].middle()
+    reduces[5].middle()
+    for index in range(4, 6):
+        reduces[index].last()
+        reduces[index].send()
+    for index, target in enumerate((own_output, own_gate, own_recept, own_value)):
+        own_s[index] = reduces[index].close()
+        put(own_s.at[index], target)
     for copy in flat_copies:
         copy.wait()
-    flat_s[2] = flat_s[1] + sum(flat_recv[step] for step in range(1, planes))
-    reduces[2].middle()
-    reduces[3].middle()
-    over_x = flat_copy(2, planes, at.side_x)
-    over_x.start()
-    over_x.wait()
-    flat_s[3] = flat_s[2] + flat_recv[planes]
-    over_y = flat_copy(3, planes + 1, at.side_y)
-    over_y.start()
-    reduces[4].middle()
-    reduces[2].last()
-    reduces[3].last()
-    over_y.wait()
-    flat_s[0] = flat_s[3] + flat_recv[planes + 1]
+    flat_s[0] = flat_s[3] + sum(flat_recv[2 + step] for step in range(1, planes))
     put(flat_s.at[0], sums_out)
-    for copy in ff_loads + ff_copies:
-        copy.wait()
-    totals = [
-        ff_total[index] + ff_far[0, index].astype(F32) + ff_far[1, index].astype(F32)
-        for index in range(2)
-    ]
-    own1_s[...] = totals[0]
-    own2_s[...] = totals[1].T
-    put(own1_s, own_hidden)
-    put(own2_s, own_return)
-    reduces[4].last()
-    for index, target in enumerate((own_output, own_gate, own_recept, own_value, own_key)):
-        own_s[index] = reduces[index].close()
-        put(own_s.at[index], target)
+    own_s[4, :, lefts] = reduces[4].close()
+    own_s[4, :, rights] = reduces[5].close()
+    put(own_s.at[4], own_key)
     for copy in outs:
         copy.wait()
 
@@ -1580,19 +1657,19 @@
         ]
         + [jax.ShapeDtypeStruct(piece, F32)] * 5
         + [jax.ShapeDtypeStruct(quarter, F32), jax.ShapeDtypeStruct(quarter[::-1], F32)],
-        in_specs=[VM] * 3 + [ANY] * 20,
+        in_specs=[VM] * 3 + [ANY] * 17,
         out_specs=[ANY] * 9,
         scratch_shapes=[
-            hold(5, BF),
-            hold(5, BF),
+            hold(3, BF),
+            hold(3, BF),
             pltpu.VMEM((3, 1024, 1024), BF),
             pltpu.VMEM((tokens, 1024), BF),
             pltpu.VMEM((tokens, 1024), F32),
             pltpu.VMEM((tokens, 1024), F32),
             hold(3, F32),
             pltpu.VMEM((5, 8, 1024), F32),
-            pltpu.VMEM((5, 2, 2, 2, planes) + piece, BF),
-            pltpu.VMEM((5, 2, 2, planes) + piece, BF),
+            pltpu.VMEM((3, 2, 2, 2, planes) + piece, BF),
+            pltpu.VMEM((3, 2, 2, planes) + piece, BF),
             pltpu.VMEM((5, 2, planes) + piece, BF),
             pltpu.VMEM((5, planes) + piece, BF),
             pltpu.VMEM((5, planes - 1) + piece, BF),
@@ -1603,13 +1680,15 @@
             pltpu.VMEM((2 + planes, 16, 1024), F32),
             sems((18,)),
             sems((9,)),
-            sems((5, 2 + planes, 2)),
+            sems((6, 1 + planes, 2)),
             sems((3 + planes, 2)),
-            pltpu.VMEM((2, 2) + quarter, BF),
+            pltpu.VMEM((2,) + quarter, BF),
             pltpu.VMEM((2,) + quarter, F32),
             pltpu.VMEM(quarter, F32),
             pltpu.VMEM(quarter[::-1], F32),
-            sems((2, 2, 2)),
+            sems((2, 2)),
+            pltpu.VMEM((2, 2, 2, planes) + piece, BF),
+            sems((3, 2)),
         ],
         compiler_params=pltpu.CompilerParams(
             collective_id=2, has_side_effects=True, vmem_limit_bytes=62 << 20
@@ -2041,7 +2120,7 @@
     key_w, value_w, recept_w, output_w, gate_w = matrices
     (
         output, grad_mid, grad_gate, grad_att, grad_recept, grad_key, grad_value, sums,
-        part1, part2, rest1, rest2,
+        part1, part2, rest1, rest2, squares,
     ) = middle_call(
         planes,
         micros,
@@ -2049,7 +2128,7 @@
         (
             table, keep, segs, segcol, segrow, w1_all, w2_all, mh_all, ret_all, ret_acc, gmh_acc,
             parts1, parts2, mid, gate, adjoint, delta_b, keys, values, recept, num, den,
-            gate_w, output_w,
+            gate_w, output_w, gated, mg,
         ),
     )
     (
@@ -2060,7 +2139,7 @@
         micros,
         rows,
         (
-            table, keep, sums, gated, grad_att, mg, grad_gate, mr, grad_recept, mv, grad_value,
+            table, keep, sums, squares, mr, grad_recept, mv, grad_value,
             mk, grad_key, recept_w, value_w, key_w, x, delta_a, grad_mid,
             part1, part2, rest1, rest2,
         ),

time: 252 us -> 225 us (0.89)
  Pallas kernels: 249 us -> 222 us
    pallas_call x1, Pallas kernels: 84.4 us -> 67.2 us  [last_call(): pl.pallas_call(functools.partial(last_kernel, planes, micros, rows), out_...]
    pallas_call x1, Pallas kernels: 80.5 us -> 75.5 us  [forward_call(): pl.pallas_call(functools.partial(forward_kernel, planes, micros, rows), o...]
    pallas_call x1, Pallas kernels: 80.1 us -> 75.3 us  [middle_call(): pl.pallas_call(functools.partial(middle_kernel, planes, micros, rows), ou...]
where the time goes in v5:
time: 225 us
  Pallas kernels  222 us (99%)
    pallas_call x1, Pallas kernels, forward_call(): pl.pallas_call(functools.partial(forward_kernel, planes, micros, rows), o...  75.5 us
    pallas_call x1, Pallas kernels, middle_call(): pl.pallas_call(functools.partial(middle_kernel, planes, micros, rows), ou...  75.3 us
    pallas_call x1, Pallas kernels, last_call(): pl.pallas_call(functools.partial(last_kernel, planes, micros, rows), out_...  67.2 us

profile of v5, /device:TPU:0, one launch (start us, length us, event | category | flops | bytes accessed | tf_op | source)
XLA Modules:
  0.0 224.8 jit_solution(7884274248507547438)
XLA Ops:
  0.7 75.5 %time_mix_forward.1 = (f32[512,1024]{1,0:T(8,128)}, f32[512,1024]{1,0:T(8,128)}, f32[512,1024]{1,0:T(8,128)}, f32[512,1024]{1,0:T(8,128)}, f32[512,1024]{1,0:T(8...) custom-call(bf16[512,1024]{1,0:T(8,128)(2,1)} %bitcast.35, ...), custom_call_target="tpu_custom_call" | custom-call | flops 19327352832 | bytes 41943040 | tf_op jit(solution)/shard_map/time_mix_forward/pallas_call | solution.py:671
  76.1 75.3 %channel_mix_and_adjoint.1 = (f32[512,1024]{1,0:T(8,128)}, f32[512,1024]{1,0:T(8,128)}, bf16[512,1024]{1,0:T(8,128)(2,1)}, bf16[512,1024]{1,0:T(8,128)(2,1)}, bf...) custom-call(f32[16,1024]{1,0:T(8,128)} %get-tuple-element.76.vec_ref, ...), custom_call_target="tpu_custom_call" | custom-call | flops 27917287424 | bytes 62914560 | tf_op jit(solution)/shard_map/channel_mix_and_adjoint/pallas_call | solution.py:1270
  151.4 67.2 %time_mix_weights.1 = (f32[512,1024]{1,0:T(8,128)}, f32[16,1024]{1,0:T(8,128)}, f32[32,1024]{1,0:T(8,128)}, f32[32,1024]{1,0:T(8,128)}, f32[32,1024]{1,0:T(8,128...) custom-call(f32[16,1024]{1,0:T(8,128)} %get-tuple-element.76.vec_ref, ...), custom_call_target="tpu_custom_call" | custom-call | flops 8589934592 | bytes 31457280 | tf_op jit(solution)/shard_map/time_mix_weights/pallas_call | solution.py:1652
  218.6 4.3 %hand_over.1 = (f32[512,1024]{1,0:T(8,128)}, f32[512,1024]{1,0:T(8,128)}, f32[32,1024]{1,0:T(8,128)}, f32[32,1024]{1,0:T(8,128)}, f32[32,1024]{1,0:T(8,128)}, /*...) custom-call(f32[512,1024]{1,0:T(8,128)} %get-tuple-element.99.refs_0_, ...), custom_call_target="tpu_custom_call" | custom-call | tf_op jit(solution)/shard_map/hand_over/pallas_call | solution.py:2049
  222.9 1.7 dynamic-slice_bitcast_fusion

commit v6 on v5

--- a/solution.py
+++ b/solution.py
@@ -736,14 +736,20 @@
 
 
 class Reduce:
-    def __init__(self, at, parts, first, second, far, sems, slot, x_first):
+    def __init__(self, at, parts, first, second, far, sems, slot, x_first, source=None):
         self.at, self.parts, self.slot = (at, parts, slot if far is not None else 0)
         side = lax.rem(at.dp, 2)
         line = lax.div(at.dp, 2)
         self.one, self.two = (side, line) if x_first else (line, side)
         near, next_to = (at.side_x, at.side_y) if x_first else (at.side_y, at.side_x)
         self.first, self.second, self.far = (first, second, far)
-        self.copy_1 = remote(parts.at[1 - self.one], first, sems.at[0, 0], sems.at[0, 1], near)
+        self.copy_1 = remote(
+            (parts if source is None else source).at[1 - self.one],
+            first,
+            sems.at[0, 0],
+            sems.at[0, 1],
+            near,
+        )
         self.copy_2 = remote(
             parts.at[self.one, 1 - self.two], second, sems.at[1, 0], sems.at[1, 1], next_to
         )
@@ -898,6 +904,8 @@
     square_parts,
     square_across,
     square_sem,
+    ahead_s,
+    ahead_sem,
 ):
     at = Place(planes)
     dp, mp, z, core = (at.dp, at.mp, at.z, at.core)
@@ -923,37 +931,75 @@
         + [at.plane(step) for step in range(1, planes)]
         + [at.ahead(1), at.ahead(-1)]
     )
-    reduces = []
-    for slot in range(planes):
-        reduces.append(
+    half_cols = hidden // 2
+    early, late_half = (slice(0, half_cols), slice(half_cols, hidden))
+
+    def group(slot, cols, sem, source):
+        made = []
+        for kind, (parts, first, second, far, parts_ref) in enumerate(
             (
-                Reduce(at, parts1.at[slot], first1.at[slot], second1.at[slot],
-                       far1.at[slot // 2] if slot % 2 else None, rs_sem.at[slot, 0], slot, True),
-                Reduce(at, parts2.at[slot], first2.at[slot], second2.at[slot],
-                       far2.at[slot // 2] if slot % 2 else None, rs_sem.at[slot, 1], slot, False),
+                (parts1, first1, second1, far1, parts1_ref),
+                (parts2, first2, second2, far2, parts2_ref),
             )
+        ):
+            made.append(
+                Reduce(
+                    at,
+                    parts.at[slot, :, :, :, cols],
+                    first.at[slot, :, :, cols],
+                    second.at[slot, :, cols],
+                    far.at[slot // 2, :, cols] if slot % 2 else None,
+                    rs_sem.at[sem, kind],
+                    slot,
+                    kind == 0,
+                    parts_ref.at[slot, :, :, :, cols] if source else None,
+                )
+            )
+        return made
+
+    everything = slice(0, hidden)
+    reduces = {
+        "near": group(1, late_half, 0, True),
+        "own": group(0, late_half, 1, True),
+        "joined": group(0, early, 2, False),
+        3: group(3, everything, 3, False),
+        2: group(2, everything, 4, False),
+    }
+    ahead_copies = [
+        remote(
+            parts_ref.at[1, :, :, :, early],
+            ahead_s.at[kind],
+            ahead_sem.at[kind, 0],
+            ahead_sem.at[kind, 1],
+            at.plane(1),
         )
+        for kind, parts_ref in enumerate((parts1_ref, parts2_ref))
+    ]
     ret_copy = remote(ret_send, ret_recv, s_sem.at[0, 0], s_sem.at[0, 1], at.other)
     gmh_copy = remote(gmh_send, gmh_recv, s_sem.at[1, 0], s_sem.at[1, 1], at.other)
 
+    def begin(name):
+        for reduce in reduces[name]:
+            reduce.start()
+
+    def middle(name):
+        for reduce in reduces[name]:
+            reduce.middle()
+
+    def last(name):
+        for reduce in reduces[name]:
+            reduce.last()
+
+    begin("near")
+    begin("own")
+    for copy in ahead_copies:
+        copy.start()
     part_loads = []
     for slot in (1, 0):
         part_loads.append(
             (load(parts1_ref.at[slot], parts1.at[slot]), load(parts2_ref.at[slot], parts2.at[slot]))
         )
     acc_loads = [load(ret_acc_ref, ret_acc), load(gmh_acc_ref, gmh_acc)]
-
-    def begin(slot):
-        for reduce in reduces[slot]:
-            reduce.start()
-
-    def middle(slot):
-        for reduce in reduces[slot]:
-            reduce.middle()
-
-    def last(slot):
-        for reduce in reduces[slot]:
-            reduce.last()
 
     def feed_forward(w1, w2, mh2, gr2, sq_s, gp_s):
         mh_load = [load(mh_all, mh2), load(ret_all, gr2)]
@@ -963,10 +1009,9 @@
             for index, slot in enumerate(order)
         ]
         late = [load(mid_ref, mid_s), load(gate_ref, gate_s), load(adj_ref, adj_s), load(db_ref, db_s)]
-        for index, slot in enumerate((1, 0)):
-            for copy in part_loads[index]:
+        for copies in part_loads:
+            for copy in copies:
                 copy.wait()
-            begin(slot)
         for copy in mh_load + acc_loads:
             copy.wait()
         half = tokens // 256
@@ -991,7 +1036,8 @@
             pl.loop(0, half)(step)
             feed_grads(mh2, gr2, sq_s, gp_s, parts1.at[slot], parts2.at[slot])
             if index == 0:
-                middle(1)
+                middle("near")
+                middle("own")
                 begin(slot)
         for copy in late:
             copy.wait()
@@ -1048,7 +1094,20 @@
             span = tile(i, tokens // 2)
             ret_acc[tile(2 + i, tokens // 2), :] = dot(ggp_s[span, :], wg[...], NT)
 
-        middle(0)
+        for kind, parts in enumerate((parts1, parts2)):
+            ahead_copies[kind].wait()
+            for one in range(2):
+                for two in range(2):
+
+                    @pl.loop(0, 4)
+                    def _(i, kind=kind, parts=parts, one=one, two=two):
+                        span = tile(i, 64)
+                        parts[0, one, two, span, early] = (
+                            parts[0, one, two, span, early].astype(F32)
+                            + ahead_s[kind, one, two, span, :].astype(F32)
+                        ).astype(BF)
+
+        begin("joined")
         gmg = ret_acc.at[far]
         gmh_copy.wait()
         need_mg = load(mg_ref, gmh_send)
@@ -1069,7 +1128,8 @@
         halo_copy.start()
         at_last = lax.broadcasted_iota(jnp.int32, (block, 1024), 0) == block - 1
         halo_copy.wait()
-        last(1)
+        last("near")
+        last("own")
         for m in range(micros):
 
             def back_b(i, after, m=m):
@@ -1098,6 +1158,8 @@
             span = tile(i, tokens // 2)
             gmh_acc[tile(2 + i, tokens // 2), :] = dot(gatt_s[span, :], wo[...], NT)
 
+        middle(3)
+        begin(2)
         for copy in need:
             copy.wait()
         width = 256
@@ -1135,8 +1197,7 @@
         put(grp_s, grp_out)
         core_copy = remote(state_own, state_other, s_sem.at[3, 0], s_sem.at[3, 1], at.other)
         core_copy.start()
-        middle(3)
-        begin(2)
+        middle("joined")
         pair = lax.div(mp, 2) * 2
         decay_all = jnp.exp(-float(rows) * jnp.exp(vec_ref[2:3, :]))
 
@@ -1171,7 +1232,7 @@
             seen(pair + 1, False) == seen(pair, True), state_other[...], 0.0
         )
         carry_s[...] = jnp.where(core == 0, joined, total)
-        last(0)
+        last(3)
 
         @pl.loop(0, 1024 // width)
         def _(i):
@@ -1206,7 +1267,6 @@
         for index in range(16):
             sums_flat[index : index + 1, :] = jnp.sum(sums_s[index], axis=0, keepdims=True)
         put(sums_flat, sums_out)
-        last(3)
         need_gated.wait()
         need_mg.wait()
         square_copies = []
@@ -1227,18 +1287,17 @@
             add_square(square_parts.at[index, core], square_across.at[index], planes)
             put(square_parts.at[index, core], square_out.at[index])
         middle(2)
-        for slot in (1, 3):
-            for reduce in reduces[slot]:
+        last("joined")
+        for name in ("near", 3):
+            for reduce in reduces[name]:
                 reduce.close()
         for parts, far_parts, own_s, own_out, one, two in (
             (parts1, far1, mid_s, own1_out, lax.rem(dp, 2), lax.div(dp, 2)),
             (parts2, far2, gate_s, own2_out, lax.div(dp, 2), lax.rem(dp, 2)),
         ):
-            own_s[0:256, 0:hidden] = (
-                parts[0, one, two].astype(F32)
-                + far_parts[0].astype(F32)
-                + far_parts[1].astype(F32)
-            )
+            total = parts[0, one, two].astype(F32) + far_parts[1].astype(F32)
+            own_s[0:256, early] = total[:, early]
+            own_s[0:256, late_half] = total[:, late_half] + far_parts[0, :, late_half].astype(F32)
             put(own_s.at[0:256, 0:hidden], own_out)
         last(2)
         put(parts1.at[2, lax.rem(dp, 2), lax.div(dp, 2)], rest1_out)
@@ -1297,14 +1356,16 @@
             few,
             sems((25,)),
             sems((14,)),
-            sems((planes, 2, 3, 2)),
+            sems((planes + 1, 2, 3, 2)),
             sems((3 + planes, 2)),
             pltpu.VMEM((2, 2, 2, 2) + piece, BF),
             pltpu.VMEM((2, 2, 2) + piece, BF),
             sems((2, 2)),
+            pltpu.VMEM((2, 2, 2, 256, hidden // 2), BF),
+            sems((2, 2)),
         ],
         compiler_params=pltpu.CompilerParams(
-            collective_id=1, has_side_effects=True, vmem_limit_bytes=62 << 20
+            collective_id=1, has_side_effects=True, vmem_limit_bytes=63 << 20
         ),
         cost_estimate=pl.CostEstimate(
             flops=52 * tokens * 1024 * 1024, bytes_accessed=60 << 20, transcendentals=6 * tokens * 1024
@@ -1314,13 +1375,19 @@
 
 
 class ReduceSquare:
-    def __init__(self, at, mine, first, second, far, sems, x_first):
+    def __init__(self, at, mine, first, second, far, sems, x_first, source=None):
         self.at, self.mine, self.first, self.second, self.far = (at, mine, first, second, far)
         side = lax.rem(at.dp, 2)
         line = lax.div(at.dp, 2)
         self.one, self.two = (side, line) if x_first else (line, side)
         near, next_to = (at.side_x, at.side_y) if x_first else (at.side_y, at.side_x)
-        self.copy_1 = remote(mine.at[1 - self.one], first, sems.at[0, 0], sems.at[0, 1], near)
+        self.copy_1 = remote(
+            (mine if source is None else source).at[1 - self.one],
+            first,
+            sems.at[0, 0],
+            sems.at[0, 1],
+            near,
+        )
         self.copy_2 = remote(
             mine.at[self.one, 1 - self.two], second, sems.at[1, 0], sems.at[1, 1], next_to
         )
@@ -1483,7 +1550,8 @@
                 second.at[place, :, :, cols],
                 far.at[place, :, :, cols],
             )
-        reduces.append(ReduceSquare(at, *refs, rs_sem.at[index], x_first))
+        source = square_ref.at[index] if index < 2 else None
+        reduces.append(ReduceSquare(at, *refs, rs_sem.at[index], x_first, source))
     core_copies = [
         remote(
             parts.at[index, 1 - core],
@@ -1499,9 +1567,9 @@
         remote(rest, ff_far.at[index], ff_sem.at[index, 0], ff_sem.at[index, 1], at.plane(2))
         for index, rest in enumerate((rest1_ref, rest2_ref))
     ]
-    ready_load.wait()
     reduces[0].begin()
     reduces[1].begin()
+    ready_load.wait()
     mixes = (vec_ref[6:7, :], vec_ref[5:6, :], vec_ref[4:5, :])
     heads = jnp.zeros((16 * micros, 1024), F32)
     for index in range(3):

time: 225 us -> 217 us (0.964)
  Pallas kernels: 222 us -> 215 us
    pallas_call x1, Pallas kernels: 75.3 us -> 68.3 us  [middle_call(): pl.pallas_call(functools.partial(middle_kernel, planes, micros, rows), ou...]
where the time goes in v6:
time: 217 us
  Pallas kernels  215 us (99%)
    pallas_call x1, Pallas kernels, forward_call(): pl.pallas_call(functools.partial(forward_kernel, planes, micros, rows), o...  75.5 us
    pallas_call x1, Pallas kernels, middle_call(): pl.pallas_call(functools.partial(middle_kernel, planes, micros, rows), ou...  68.3 us
    pallas_call x1, Pallas kernels, last_call(): pl.pallas_call(functools.partial(last_kernel, planes, micros, rows), out_...  66.6 us

profile of v6, /device:TPU:0, one launch (start us, length us, event | category | flops | bytes accessed | tf_op | source)
XLA Modules:
  0.0 217.2 jit_solution(12800322986196656899)
XLA Ops:
  0.7 75.5 %time_mix_forward.1 = (f32[512,1024]{1,0:T(8,128)}, f32[512,1024]{1,0:T(8,128)}, f32[512,1024]{1,0:T(8,128)}, f32[512,1024]{1,0:T(8,128)}, f32[512,1024]{1,0:T(8...) custom-call(bf16[512,1024]{1,0:T(8,128)(2,1)} %bitcast.35, ...), custom_call_target="tpu_custom_call" | custom-call | flops 19327352832 | bytes 41943040 | tf_op jit(solution)/shard_map/time_mix_forward/pallas_call | solution.py:671
  76.1 68.3 %channel_mix_and_adjoint.1 = (f32[512,1024]{1,0:T(8,128)}, f32[512,1024]{1,0:T(8,128)}, bf16[512,1024]{1,0:T(8,128)(2,1)}, bf16[512,1024]{1,0:T(8,128)(2,1)}, bf...) custom-call(f32[16,1024]{1,0:T(8,128)} %get-tuple-element.76.vec_ref, ...), custom_call_target="tpu_custom_call" | custom-call | flops 27917287424 | bytes 62914560 | tf_op jit(solution)/shard_map/channel_mix_and_adjoint/pallas_call | solution.py:1329
  144.5 66.6 %time_mix_weights.1 = (f32[512,1024]{1,0:T(8,128)}, f32[16,1024]{1,0:T(8,128)}, f32[32,1024]{1,0:T(8,128)}, f32[32,1024]{1,0:T(8,128)}, f32[32,1024]{1,0:T(8,128...) custom-call(f32[16,1024]{1,0:T(8,128)} %get-tuple-element.76.vec_ref, ...), custom_call_target="tpu_custom_call" | custom-call | flops 8589934592 | bytes 31457280 | tf_op jit(solution)/shard_map/time_mix_weights/pallas_call | solution.py:1720
  211.1 4.3 %hand_over.1 = (f32[512,1024]{1,0:T(8,128)}, f32[512,1024]{1,0:T(8,128)}, f32[32,1024]{1,0:T(8,128)}, f32[32,1024]{1,0:T(8,128)}, f32[32,1024]{1,0:T(8,128)}, /*...) custom-call(f32[512,1024]{1,0:T(8,128)} %get-tuple-element.99.refs_0_, ...), custom_call_target="tpu_custom_call" | custom-call | tf_op jit(solution)/shard_map/hand_over/pallas_call | solution.py:2117
  215.4 1.7 dynamic-slice_bitcast_fusion

commit v7 on v6

--- a/solution.py
+++ b/solution.py
@@ -994,25 +994,23 @@
     begin("own")
     for copy in ahead_copies:
         copy.start()
-    part_loads = []
-    for slot in (1, 0):
-        part_loads.append(
-            (load(parts1_ref.at[slot], parts1.at[slot]), load(parts2_ref.at[slot], parts2.at[slot]))
-        )
-    acc_loads = [load(ret_acc_ref, ret_acc), load(gmh_acc_ref, gmh_acc)]
 
     def feed_forward(w1, w2, mh2, gr2, sq_s, gp_s):
         mh_load = [load(mh_all, mh2), load(ret_all, gr2)]
         order = (planes - 1, planes - 2)
-        slots = [
-            (load(w1_all.at[slot - 1], w1.at[index]), load(w2_all.at[slot - 1], w2.at[index]))
-            for index, slot in enumerate(order)
-        ]
+        slots = []
+        part_loads = []
+        for index, slot in enumerate(order):
+            slots.append(
+                (load(w1_all.at[slot - 1], w1.at[index]), load(w2_all.at[slot - 1], w2.at[index]))
+            )
+            if index == 0:
+                mh_load += [load(ret_acc_ref, ret_acc), load(gmh_acc_ref, gmh_acc)]
+                for part in (1, 0):
+                    part_loads.append(load(parts1_ref.at[part], parts1.at[part]))
+                    part_loads.append(load(parts2_ref.at[part], parts2.at[part]))
         late = [load(mid_ref, mid_s), load(gate_ref, gate_s), load(adj_ref, adj_s), load(db_ref, db_s)]
-        for copies in part_loads:
-            for copy in copies:
-                copy.wait()
-        for copy in mh_load + acc_loads:
+        for copy in mh_load:
             copy.wait()
         half = tokens // 256
         for index, slot in enumerate(order):
@@ -1022,7 +1020,11 @@
                 w1.at[index], w2.at[index], mh2, gr2, sq_s, gp_s, ret_acc, gmh_acc, False
             )
             pl.loop(half, 2 * half)(step)
-            if index == 1:
+            if index == 0:
+                for copy in part_loads:
+                    copy.wait()
+                middle("near")
+            else:
 
                 @pl.loop(0, tokens // 64)
                 def _(i):
@@ -1034,10 +1036,10 @@
                 ret_copy.start()
                 gmh_copy.start()
             pl.loop(0, half)(step)
+            if index == 0:
+                middle("own")
             feed_grads(mh2, gr2, sq_s, gp_s, parts1.at[slot], parts2.at[slot])
             if index == 0:
-                middle("near")
-                middle("own")
                 begin(slot)
         for copy in late:
             copy.wait()
@@ -1130,6 +1132,8 @@
         halo_copy.wait()
         last("near")
         last("own")
+        middle(3)
+        begin(2)
         for m in range(micros):
 
             def back_b(i, after, m=m):
@@ -1158,8 +1162,7 @@
             span = tile(i, tokens // 2)
             gmh_acc[tile(2 + i, tokens // 2), :] = dot(gatt_s[span, :], wo[...], NT)
 
-        middle(3)
-        begin(2)
+        middle("joined")
         for copy in need:
             copy.wait()
         width = 256
@@ -1197,7 +1200,6 @@
         put(grp_s, grp_out)
         core_copy = remote(state_own, state_other, s_sem.at[3, 0], s_sem.at[3, 1], at.other)
         core_copy.start()
-        middle("joined")
         pair = lax.div(mp, 2) * 2
         decay_all = jnp.exp(-float(rows) * jnp.exp(vec_ref[2:3, :]))
 
@@ -1271,7 +1273,7 @@
         need_mg.wait()
         square_copies = []
         for index, (left, right) in enumerate(((ret_send, gatt_s), (gmh_send, ggp_s))):
-            fill_square(square_parts.at[index], left, right, planes, 1024 * (1 - index))
+            fill_square(square_parts.at[index], left, right, planes, 512)
             square_copies.append(
                 remote(
                     square_parts.at[index, 1 - core],
@@ -1282,11 +1284,11 @@
                 )
             )
             square_copies[index].start()
+        middle(2)
         for index in range(2):
             square_copies[index].wait()
             add_square(square_parts.at[index, core], square_across.at[index], planes)
             put(square_parts.at[index, core], square_out.at[index])
-        middle(2)
         last("joined")
         for name in ("near", 3):
             for reduce in reduces[name]:
@@ -1537,21 +1539,42 @@
     core = at.core
     lefts, rights = (slice(0, 512), slice(512, 1024))
     reduces = []
-    for index, (cols, x_first) in enumerate(
-        ((None, True), (None, False), (None, True), (None, False), (lefts, True), (rights, False))
-    ):
-        place = min(index, 4)
-        mine = ready_s.at[index] if index < 2 else parts.at[place - 2, core]
-        refs = (mine, first.at[place], second.at[place], far.at[place])
-        if cols is not None:
-            refs = (
-                mine.at[:, :, :, :, cols],
-                first.at[place, :, :, :, cols],
-                second.at[place, :, :, cols],
-                far.at[place, :, :, cols],
+    for index in range(5):
+        mine = ready_s.at[index] if index < 2 else parts.at[index - 2, core]
+        halves = []
+        for kind, cols in enumerate((lefts, rights)):
+            halves.append(
+                ReduceSquare(
+                    at,
+                    mine.at[:, :, :, :, cols],
+                    first.at[index, :, :, :, cols],
+                    second.at[index, :, :, cols],
+                    far.at[index, :, :, cols],
+                    rs_sem.at[index, kind],
+                    kind == 0,
+                    square_ref.at[index, :, :, :, :, cols] if index < 2 else None,
+                )
             )
-        source = square_ref.at[index] if index < 2 else None
-        reduces.append(ReduceSquare(at, *refs, rs_sem.at[index], x_first, source))
+        reduces.append(halves)
+
+    def begin(index):
+        for half in reduces[index]:
+            half.begin()
+
+    def middle(index):
+        for half in reduces[index]:
+            half.middle()
+
+    def last(index):
+        for half in reduces[index]:
+            half.last()
+            half.send()
+
+    def close(index, target):
+        for half, cols in zip(reduces[index], (lefts, rights)):
+            own_s[index, :, cols] = half.close()
+        put(own_s.at[index], target)
+
     core_copies = [
         remote(
             parts.at[index, 1 - core],
@@ -1567,8 +1590,8 @@
         remote(rest, ff_far.at[index], ff_sem.at[index, 0], ff_sem.at[index, 1], at.plane(2))
         for index, rest in enumerate((rest1_ref, rest2_ref))
     ]
-    reduces[0].begin()
-    reduces[1].begin()
+    begin(0)
+    begin(1)
     ready_load.wait()
     mixes = (vec_ref[6:7, :], vec_ref[5:6, :], vec_ref[4:5, :])
     heads = jnp.zeros((16 * micros, 1024), F32)
@@ -1590,9 +1613,9 @@
         copy.start()
     sums_s[...] = jnp.zeros_like(sums_s)
 
-    def fill(index, split):
+    def fill(index):
         side_loads[index][0].wait()
-        fill_square(parts.at[index], left_s.at[index], right_s.at[index], planes, split)
+        fill_square(parts.at[index], left_s.at[index], right_s.at[index], planes, 512)
         core_copies[index].start()
 
     def settle(index):
@@ -1605,17 +1628,18 @@
             span = tile(i, tokens // 2)
             g_s[index, span, :] = dot(right_s[index, span, :], w_s[index], NT)
 
-    fill(0, 1024)
-    fill(1, 0)
+    fill(0)
+    middle(0)
+    fill(1)
     settle(0)
-    fill(2, 512)
+    begin(2)
+    fill(2)
     settle(1)
+    middle(1)
+    begin(3)
+    settle(2)
     back(0)
-    reduces[0].middle()
-    reduces[1].middle()
-    reduces[2].begin()
-    reduces[3].begin()
-    settle(2)
+    last(0)
     back(1)
     back(2)
     for copy in row_loads:
@@ -1631,9 +1655,6 @@
 
     at_last = lax.broadcasted_iota(jnp.int32, (block, 1024), 0) == block - 1
     halo_copy.wait()
-    for index in range(2):
-        reduces[index].last()
-        reduces[index].send()
     for m in range(micros):
 
         def back_a(i, after, m=m):
@@ -1665,44 +1686,55 @@
     over_core.wait()
     flat_s[1] = flat_s[0] + flat_recv[0]
     over_x = flat_copy(1, 1, at.side_x)
+    middle(2)
     over_x.start()
-    reduces[2].middle()
-    reduces[3].middle()
+    begin(4)
+    last(1)
+    middle(3)
     over_x.wait()
     flat_s[2] = flat_s[1] + flat_recv[1]
     over_y = flat_copy(2, 2, at.side_y)
     over_y.start()
-    reduces[4].begin()
-    reduces[5].begin()
-    for index in range(2, 4):
-        reduces[index].last()
-        reduces[index].send()
+    last(2)
+    middle(4)
     over_y.wait()
     flat_s[3] = flat_s[2] + flat_recv[2]
-    flat_copies = [flat_copy(3, 2 + step, at.plane(step)) for step in range(1, planes)]
+    flat_copies = []
+    for step in range(1, planes):
+        to = lax.rem(at.z + step, planes)
+        lanes = tile(at.dp * (planes // 2) + lax.div(to, 2), 128)
+        slot = 2 + step
+        flat_copies.append(
+            remote(
+                flat_s.at[3, :, lanes],
+                flat_recv.at[slot, :, lanes],
+                s_sem.at[1 + slot, 0],
+                s_sem.at[1 + slot, 1],
+                at.plane(step),
+            )
+        )
     for copy in flat_copies:
         copy.start()
+    last(3)
     for copy in ff_loads + ff_copies:
         copy.wait()
     own1_s[...] = ff_total[0] + ff_far[0].astype(F32)
     own2_s[...] = (ff_total[1] + ff_far[1].astype(F32)).T
     put(own1_s, own_hidden)
     put(own2_s, own_return)
-    reduces[4].middle()
-    reduces[5].middle()
-    for index in range(4, 6):
-        reduces[index].last()
-        reduces[index].send()
-    for index, target in enumerate((own_output, own_gate, own_recept, own_value)):
-        own_s[index] = reduces[index].close()
-        put(own_s.at[index], target)
+    last(4)
+    close(0, own_output)
+    close(1, own_gate)
+    close(2, own_recept)
     for copy in flat_copies:
         copy.wait()
-    flat_s[0] = flat_s[3] + sum(flat_recv[2 + step] for step in range(1, planes))
+    lanes = tile(at.dp * (planes // 2) + lax.div(at.z, 2), 128)
+    flat_s[0, :, lanes] = flat_s[3, :, lanes] + sum(
+        flat_recv[2 + step, :, lanes] for step in range(1, planes)
+    )
     put(flat_s.at[0], sums_out)
-    own_s[4, :, lefts] = reduces[4].close()
-    own_s[4, :, rights] = reduces[5].close()
-    put(own_s.at[4], own_key)
+    close(3, own_value)
+    close(4, own_key)
     for copy in outs:
         copy.wait()
 
@@ -1748,7 +1780,7 @@
             pltpu.VMEM((2 + planes, 16, 1024), F32),
             sems((18,)),
             sems((9,)),
-            sems((6, 1 + planes, 2)),
+            sems((5, 2, 1 + planes, 2)),
             sems((3 + planes, 2)),
             pltpu.VMEM((2,) + quarter, BF),
             pltpu.VMEM((2,) + quarter, F32),

time: 217 us -> 212 us (0.977)
  Pallas kernels: 215 us -> 209 us
    pallas_call x1, Pallas kernels: 66.6 us -> 61.6 us  [last_call(): pl.pallas_call(functools.partial(last_kernel, planes, micros, rows), out_...]
where the time goes in v7:
time: 212 us
  Pallas kernels  209 us (99%)
    pallas_call x1, Pallas kernels, forward_call(): pl.pallas_call(functools.partial(forward_kernel, planes, micros, rows), o...  75.5 us
    pallas_call x1, Pallas kernels, middle_call(): pl.pallas_call(functools.partial(middle_kernel, planes, micros, rows), ou...  67.7 us
    pallas_call x1, Pallas kernels, last_call(): pl.pallas_call(functools.partial(last_kernel, planes, micros, rows), out_...  61.6 us
    pallas_call x1, Pallas kernels, hand_call(): pl.pallas_call(functools.partial(hand_over, count), out_shape=[jax.ShapeD...  4.26 us

profile of v7, /device:TPU:0, one launch (start us, length us, event | category | flops | bytes accessed | tf_op | source)
XLA Modules:
  0.0 211.6 jit_solution(17456638497316805592)
XLA Ops:
  0.7 75.5 %time_mix_forward.1 = (f32[512,1024]{1,0:T(8,128)}, f32[512,1024]{1,0:T(8,128)}, f32[512,1024]{1,0:T(8,128)}, f32[512,1024]{1,0:T(8,128)}, f32[512,1024]{1,0:T(8...) custom-call(bf16[512,1024]{1,0:T(8,128)(2,1)} %bitcast.35, ...), custom_call_target="tpu_custom_call" | custom-call | flops 19327352832 | bytes 41943040 | tf_op jit(solution)/shard_map/time_mix_forward/pallas_call | solution.py:671
  76.1 67.7 %channel_mix_and_adjoint.1 = (f32[512,1024]{1,0:T(8,128)}, f32[512,1024]{1,0:T(8,128)}, bf16[512,1024]{1,0:T(8,128)(2,1)}, bf16[512,1024]{1,0:T(8,128)(2,1)}, bf...) custom-call(f32[16,1024]{1,0:T(8,128)} %get-tuple-element.76.vec_ref, ...), custom_call_target="tpu_custom_call" | custom-call | flops 27917287424 | bytes 62914560 | tf_op jit(solution)/shard_map/channel_mix_and_adjoint/pallas_call | solution.py:1331
  143.8 61.6 %time_mix_weights.1 = (f32[512,1024]{1,0:T(8,128)}, f32[16,1024]{1,0:T(8,128)}, f32[32,1024]{1,0:T(8,128)}, f32[32,1024]{1,0:T(8,128)}, f32[32,1024]{1,0:T(8,128...) custom-call(f32[16,1024]{1,0:T(8,128)} %get-tuple-element.76.vec_ref, ...), custom_call_target="tpu_custom_call" | custom-call | flops 8589934592 | bytes 31457280 | tf_op jit(solution)/shard_map/time_mix_weights/pallas_call | solution.py:1752
  205.4 4.3 %hand_over.1 = (f32[512,1024]{1,0:T(8,128)}, f32[512,1024]{1,0:T(8,128)}, f32[32,1024]{1,0:T(8,128)}, f32[32,1024]{1,0:T(8,128)}, f32[32,1024]{1,0:T(8,128)}, /*...) custom-call(f32[512,1024]{1,0:T(8,128)} %get-tuple-element.99.refs_0_, ...), custom_call_target="tpu_custom_call" | custom-call | tf_op jit(solution)/shard_map/hand_over/pallas_call | solution.py:2149
  209.7 1.7 dynamic-slice_bitcast_fusion

commit v8 on v7

--- a/solution.py
+++ b/solution.py
@@ -347,22 +347,31 @@
     for copy in seg_copies:
         copy.wait()
 
-    def along(step):
-        group = []
-        own1, own2 = (w1_all.at[step, q1], w2_all.at[step, q2])
+    side1 = tile(dp + 1 - 2 * lax.rem(dp, 2), quarter1)
+
+    def hop(array, span, step, index, device):
+        part = array.at[step, span]
+        return remote(part, part, z_sem.at[step, index, 0], z_sem.at[step, index, 1], device)
+
+    def early(step):
         return (
-            remote(own1, own1, z_sem.at[step, 2, 0], z_sem.at[step, 2, 1], at.side_x),
-            remote(own2, own2, z_sem.at[step, 3, 0], z_sem.at[step, 3, 1], at.side_y),
+            hop(w1_all, q1, step, 2, at.side_x),
+            hop(w2_all, q2, step, 3, at.side_y),
+            hop(w2_all, q2, step, 5, at.side_x),
+            hop(w1_all, q1, step, 4, at.side_y),
         )
 
+    def late(step):
+        return (
+            hop(w1_all, side1, step, 7, at.side_y),
+            hop(w2_all, far2, step, 6, at.side_x),
+        )
+
     def across(step):
-        both1 = w1_all.at[step, half1]
-        own2 = w2_all.at[step, q2]
-        next2 = w2_all.at[step, far2]
         return (
-            remote(both1, both1, z_sem.at[step, 4, 0], z_sem.at[step, 4, 1], at.side_y),
-            remote(own2, own2, z_sem.at[step, 5, 0], z_sem.at[step, 5, 1], at.side_x),
-            remote(next2, next2, z_sem.at[step, 6, 0], z_sem.at[step, 6, 1], at.side_x),
+            hop(w1_all, half1, step, 4, at.side_y),
+            hop(w2_all, q2, step, 5, at.side_x),
+            hop(w2_all, far2, step, 6, at.side_x),
         )
 
     def start(group):
@@ -373,8 +382,8 @@
         for copy in group:
             copy.wait()
 
-    along_0, along_2 = (along(0), along(2))
-    across_0, across_1, across_2 = (across(0), across(1), across(2))
+    early_0, early_2 = (early(0), early(2))
+    late_0, across_1, late_2 = (late(0), across(1), late(2))
 
     before = lax.rem(mp + at.count - 1, at.count)
     has_before = mp > 0
@@ -467,7 +476,7 @@
     core_copy = remote(state_own, state_other, s_sem.at[0, 0], s_sem.at[0, 1], at.other)
     core_copy.start()
     finish(z_copies[0])
-    start(along_0)
+    start(early_0)
     z_copies[2][0].start()
 
     loads[2].wait()
@@ -494,10 +503,10 @@
         for step in range(1, planes)
     ]
     start(chip_copies)
+    finish(early_0[0:2])
+    start(late_0)
     finish(chip_copies)
     z_copies[2][1].start()
-    finish(along_0)
-    start(across_0)
     total = jnp.zeros_like(state_chip[...])
     power = jnp.ones_like(decay_all)
     for step in range(1, planes):
@@ -562,7 +571,7 @@
     onward_1.start()
     start(onward_2)
     finish(z_copies[2])
-    start(along_2)
+    start(early_2)
     for m in range(micros):
 
         def mix_b(b, prev, m=m):
@@ -618,11 +627,11 @@
     pl.loop(0, half)(step)
     mh_copy.wait()
     ret_copy.wait()
-    finish(along_2)
-    start(across_2)
+    finish(early_2[0:2])
+    start(late_2)
     put(mh2, mh_all)
     put(gr2, ret_all)
-    finish(across_0)
+    finish(early_0[2:4] + late_0)
     ff_loads[2].start()
     ff_loads[3].start()
     pl.loop(half, 2 * half)(step)
@@ -645,7 +654,7 @@
     feed_grads(mh2, gr2, sq_s, gp_s, parts1.at[1], parts2.at[1])
     put(parts1.at[1], parts1_out.at[1])
     put(parts2.at[1], parts2_out.at[1])
-    finish(across_2)
+    finish(early_2[2:4] + late_2)
     finish(across_1)
     for copy in outs:
         copy.wait()
@@ -712,7 +721,7 @@
             pair((5,)),
             pair((29,)),
             pair((2 * planes + 1, 2)),
-            pair((planes - 1, 7, 2)),
+            pair((planes - 1, 8, 2)),
             pair((planes + 3, 2)),
             pltpu.VMEM((16, 1024), F32),
             pltpu.VMEM((2 * tokens, 1024), BF),
@@ -1522,15 +1531,10 @@
         (mv_ref, gv_ref),
         (mk_ref, gk_ref),
     )
-    ready_load = load(square_ref, ready_s)
-    side_loads = [
-        (load(left, left_s.at[index]), load(right, right_s.at[index]))
-        for index, (left, right) in enumerate(sides)
-    ]
-    w_loads = [
-        load(source, w_s.at[index]) for index, source in enumerate((recept_w, value_w, key_w))
-    ]
-    row_loads = [load(x_ref, x_s), load(da_ref, da_s), load(gmid_ref, total_s)]
+    right_loads, w_loads = ([], [])
+    for index, source in enumerate((recept_w, value_w, key_w)):
+        right_loads.append(load(sides[index][1], right_s.at[index]))
+        w_loads.append(load(source, w_s.at[index]))
     greet(
         [at.other, at.side_x, at.side_y]
         + [at.plane(step) for step in range(1, planes)]
@@ -1592,11 +1596,13 @@
     ]
     begin(0)
     begin(1)
-    ready_load.wait()
+    ready_load = load(square_ref, ready_s)
+    left_loads = [load(left, left_s.at[index]) for index, (left, _) in enumerate(sides)]
+    row_loads = [load(x_ref, x_s), load(da_ref, da_s), load(gmid_ref, total_s)]
     mixes = (vec_ref[6:7, :], vec_ref[5:6, :], vec_ref[4:5, :])
     heads = jnp.zeros((16 * micros, 1024), F32)
     for index in range(3):
-        side_loads[index][1].wait()
+        right_loads[index].wait()
         w_loads[index].wait()
         picked = jnp.concatenate(
             [right_s[index, m * rows : m * rows + 16, :] for m in range(micros)], axis=0
@@ -1614,7 +1620,7 @@
     sums_s[...] = jnp.zeros_like(sums_s)
 
     def fill(index):
-        side_loads[index][0].wait()
+        left_loads[index].wait()
         fill_square(parts.at[index], left_s.at[index], right_s.at[index], planes, 512)
         core_copies[index].start()
 
@@ -1629,6 +1635,7 @@
             g_s[index, span, :] = dot(right_s[index, span, :], w_s[index], NT)
 
     fill(0)
+    ready_load.wait()
     middle(0)
     fill(1)
     settle(0)
@@ -1697,6 +1704,7 @@
     over_y.start()
     last(2)
     middle(4)
+    last(3)
     over_y.wait()
     flat_s[3] = flat_s[2] + flat_recv[2]
     flat_copies = []
@@ -1715,7 +1723,6 @@
         )
     for copy in flat_copies:
         copy.start()
-    last(3)
     for copy in ff_loads + ff_copies:
         copy.wait()
     own1_s[...] = ff_total[0] + ff_far[0].astype(F32)

time: 212 us -> 207 us (0.976)
  Pallas kernels: 209 us -> 204 us
    pallas_call x1, Pallas kernels: 75.5 us -> 70.9 us  [forward_call(): pl.pallas_call(functools.partial(forward_kernel, planes, micros, rows), o...]
where the time goes in v8:
time: 207 us
  Pallas kernels  204 us (99%)
    pallas_call x1, Pallas kernels, forward_call(): pl.pallas_call(functools.partial(forward_kernel, planes, micros, rows), o...  70.9 us
    pallas_call x1, Pallas kernels, middle_call(): pl.pallas_call(functools.partial(middle_kernel, planes, micros, rows), ou...  68.7 us
    pallas_call x1, Pallas kernels, last_call(): pl.pallas_call(functools.partial(last_kernel, planes, micros, rows), out_...  60.6 us
    pallas_call x1, Pallas kernels, hand_call(): pl.pallas_call(functools.partial(hand_over, count), out_shape=[jax.ShapeD...  4.26 us

profile of v8, /device:TPU:0, one launch (start us, length us, event | category | flops | bytes accessed | tf_op | source)
XLA Modules:
  0.0 207.0 jit_solution(17446765383343114032)
XLA Ops:
  0.7 70.9 %time_mix_forward.1 = (f32[512,1024]{1,0:T(8,128)}, f32[512,1024]{1,0:T(8,128)}, f32[512,1024]{1,0:T(8,128)}, f32[512,1024]{1,0:T(8,128)}, f32[512,1024]{1,0:T(8...) custom-call(bf16[512,1024]{1,0:T(8,128)(2,1)} %bitcast.35, ...), custom_call_target="tpu_custom_call" | custom-call | flops 19327352832 | bytes 41943040 | tf_op jit(solution)/shard_map/time_mix_forward/pallas_call | solution.py:680
  71.6 68.7 %channel_mix_and_adjoint.1 = (f32[512,1024]{1,0:T(8,128)}, f32[512,1024]{1,0:T(8,128)}, bf16[512,1024]{1,0:T(8,128)(2,1)}, bf16[512,1024]{1,0:T(8,128)(2,1)}, bf...) custom-call(f32[16,1024]{1,0:T(8,128)} %get-tuple-element.76.vec_ref, ...), custom_call_target="tpu_custom_call" | custom-call | flops 27917287424 | bytes 62914560 | tf_op jit(solution)/shard_map/channel_mix_and_adjoint/pallas_call | solution.py:1340
  140.3 60.6 %time_mix_weights.1 = (f32[512,1024]{1,0:T(8,128)}, f32[16,1024]{1,0:T(8,128)}, f32[32,1024]{1,0:T(8,128)}, f32[32,1024]{1,0:T(8,128)}, f32[32,1024]{1,0:T(8,128...) custom-call(f32[16,1024]{1,0:T(8,128)} %get-tuple-element.76.vec_ref, ...), custom_call_target="tpu_custom_call" | custom-call | flops 8589934592 | bytes 31457280 | tf_op jit(solution)/shard_map/time_mix_weights/pallas_call | solution.py:1759
  200.9 4.3 %hand_over.1 = (f32[512,1024]{1,0:T(8,128)}, f32[512,1024]{1,0:T(8,128)}, f32[32,1024]{1,0:T(8,128)}, f32[32,1024]{1,0:T(8,128)}, f32[32,1024]{1,0:T(8,128)}, /*...) custom-call(f32[512,1024]{1,0:T(8,128)} %get-tuple-element.99.refs_0_, ...), custom_call_target="tpu_custom_call" | custom-call | tf_op jit(solution)/shard_map/hand_over/pallas_call | solution.py:2156
  205.2 1.7 dynamic-slice_bitcast_fusion

commit v9 on v8

--- a/solution.py
+++ b/solution.py
@@ -475,9 +475,9 @@
     put(v_s, v_out)
     core_copy = remote(state_own, state_other, s_sem.at[0, 0], s_sem.at[0, 1], at.other)
     core_copy.start()
+    z_copies[2][0].start()
     finish(z_copies[0])
     start(early_0)
-    z_copies[2][0].start()
 
     loads[2].wait()
 

time: 207 us -> 207 us (level)
  no operation moved by 1% of the time
where the time goes in v9:
time: 207 us; the launch traced here: 206 us
  Pallas kernels  204 us (99%)
    pallas_call x1, Pallas kernels, forward_call(): pl.pallas_call(functools.partial(forward_kernel, planes, micros, rows), o...  72 us
    pallas_call x1, Pallas kernels, middle_call(): pl.pallas_call(functools.partial(middle_kernel, planes, micros, rows), ou...  67.3 us
    pallas_call x1, Pallas kernels, last_call(): pl.pallas_call(functools.partial(last_kernel, planes, micros, rows), out_...  60.4 us
    pallas_call x1, Pallas kernels, hand_call(): pl.pallas_call(functools.partial(hand_over, count), out_shape=[jax.ShapeD...  4.26 us

profile of v9, /device:TPU:0, one launch (start us, length us, event | category | flops | bytes accessed | tf_op | source)
XLA Modules:
  0.0 206.5 jit_solution(10900745365672049482)
XLA Ops:
  0.7 72.0 %time_mix_forward.1 = (f32[512,1024]{1,0:T(8,128)}, f32[512,1024]{1,0:T(8,128)}, f32[512,1024]{1,0:T(8,128)}, f32[512,1024]{1,0:T(8,128)}, f32[512,1024]{1,0:T(8...) custom-call(bf16[512,1024]{1,0:T(8,128)(2,1)} %bitcast.35, ...), custom_call_target="tpu_custom_call" | custom-call | flops 19327352832 | bytes 41943040 | tf_op jit(solution)/shard_map/time_mix_forward/pallas_call | solution.py:680
  72.7 67.3 %channel_mix_and_adjoint.1 = (f32[512,1024]{1,0:T(8,128)}, f32[512,1024]{1,0:T(8,128)}, bf16[512,1024]{1,0:T(8,128)(2,1)}, bf16[512,1024]{1,0:T(8,128)(2,1)}, bf...) custom-call(f32[16,1024]{1,0:T(8,128)} %get-tuple-element.76.vec_ref, ...), custom_call_target="tpu_custom_call" | custom-call | flops 27917287424 | bytes 62914560 | tf_op jit(solution)/shard_map/channel_mix_and_adjoint/pallas_call | solution.py:1340
  140.0 60.4 %time_mix_weights.1 = (f32[512,1024]{1,0:T(8,128)}, f32[16,1024]{1,0:T(8,128)}, f32[32,1024]{1,0:T(8,128)}, f32[32,1024]{1,0:T(8,128)}, f32[32,1024]{1,0:T(8,128...) custom-call(f32[16,1024]{1,0:T(8,128)} %get-tuple-element.76.vec_ref, ...), custom_call_target="tpu_custom_call" | custom-call | flops 8589934592 | bytes 31457280 | tf_op jit(solution)/shard_map/time_mix_weights/pallas_call | solution.py:1759
  200.3 4.3 %hand_over.1 = (f32[512,1024]{1,0:T(8,128)}, f32[512,1024]{1,0:T(8,128)}, f32[32,1024]{1,0:T(8,128)}, f32[32,1024]{1,0:T(8,128)}, f32[32,1024]{1,0:T(8,128)}, /*...) custom-call(f32[512,1024]{1,0:T(8,128)} %get-tuple-element.99.refs_0_, ...), custom_call_target="tpu_custom_call" | custom-call | tf_op jit(solution)/shard_map/hand_over/pallas_call | solution.py:2156
  204.6 1.7 dynamic-slice_bitcast_fusion
